TPU v7x, 32 devices: a whole 2x2x4 slice. The times are simulated.
32 devices in a mesh: grp: 4 (over y, x), row: 8 (over z, core).
Axes of the slice: x: 2, y: 2, z: 4, core: 2. Of those that a mesh axis runs over, the one named last changes fastest.
Arguments:
- snapshots: bfloat16 [8192, 32768], P(None, ('grp', 'row')), may hold values from -8 to 8
- weights: float32 [32768], P(('grp', 'row')), may hold values from 0.25 to 4
- reference_field: float32 [32768], P(('grp', 'row')), may hold values from -6 to 6
- start_basis: float32 [64, 2, 63, 8], replicated, may hold values from -6 to 6
Outputs:
- spod_modes: float32 [64, 16, 32768], P(None, None, ('grp', 'row'))
- energies: float32 [64, 8], replicated
All inputs are finite; a program needn't handle non-finite values.
Results may differ from a plain program's by a relative error of at most 0.012.
The roundings to bfloat16 on the way count: a program that leaves them out, or rounds other values in their place, can miss the bound.
Values may be sent and summed in bfloat16 or wider, within the bound.
No kernel may reach another device: no remote copies, remote signals or barrier semaphores. Data moves between devices by JAX's collectives and lax.ppermute only.
A program may use at most 192 MiB of HBM per device.

v0:
```python
import math

import jax
import jax.numpy as jnp
from jax import lax
from jax.sharding import PartitionSpec as P

NFFT = 256
NBLK = 63
NF = 64
NM = 8
ITERS = 12


highest = lax.Precision.HIGHEST


def dft_table():
    time_steps = jnp.arange(NFFT, dtype=jnp.int32)
    freq_bins = jnp.arange(1, NF + 1, dtype=jnp.int32)
    wrapped = freq_bins[:, None] * time_steps[None, :] % NFFT
    angles = 2.0 * math.pi / NFFT * wrapped.astype(jnp.float32)
    window_taper = 0.5 - 0.5 * jnp.cos(2.0 * math.pi / NFFT * time_steps.astype(jnp.float32))
    scaled_taper = window_taper / jnp.sqrt(jnp.sum(window_taper * window_taper))
    stacked = jnp.stack([jnp.cos(angles), -jnp.sin(angles)]) * scaled_taper[None, None, :]
    return stacked.astype(jnp.bfloat16)


def apply_gram(gram_real, gram_imag, basis_real, basis_imag):
    image_real = jnp.einsum("fbc,fck->fbk", gram_real, basis_real, precision=highest) - jnp.einsum(
        "fbc,fck->fbk", gram_imag, basis_imag, precision=highest
    )
    image_imag = jnp.einsum("fbc,fck->fbk", gram_real, basis_imag, precision=highest) + jnp.einsum(
        "fbc,fck->fbk", gram_imag, basis_real, precision=highest
    )
    return (image_real, image_imag)


def orthonormalize(image_real, image_imag):
    cols_real = []
    cols_imag = []
    for column in range(image_real.shape[2]):
        target_real = image_real[:, :, column]
        target_imag = image_imag[:, :, column]
        for earlier in range(column):
            prior_real = cols_real[earlier]
            prior_imag = cols_imag[earlier]
            inner_real = jnp.sum(
                prior_real * target_real + prior_imag * target_imag, axis=1, keepdims=True
            )
            inner_imag = jnp.sum(
                prior_real * target_imag - prior_imag * target_real, axis=1, keepdims=True
            )
            target_real, target_imag = (
                target_real - (inner_real * prior_real - inner_imag * prior_imag),
                target_imag - (inner_real * prior_imag + inner_imag * prior_real),
            )
        length = jnp.sqrt(
            jnp.sum(target_real * target_real + target_imag * target_imag, axis=1, keepdims=True)
            + 1e-06
        )
        cols_real.append(target_real / length)
        cols_imag.append(target_imag / length)
    return (jnp.stack(cols_real, axis=2), jnp.stack(cols_imag, axis=2))


def subspace_solve(gram_real, gram_imag, start_basis):

    def sweep_once(sweep_index, current):
        image_real, image_imag = apply_gram(gram_real, gram_imag, current[0], current[1])
        return orthonormalize(image_real, image_imag)

    basis_real, basis_imag = lax.fori_loop(
        0, ITERS, sweep_once, (start_basis[:, 0], start_basis[:, 1])
    )
    image_real, image_imag = apply_gram(gram_real, gram_imag, basis_real, basis_imag)
    energy = jnp.sum(basis_real * image_real + basis_imag * image_imag, axis=1)
    return (basis_real, basis_imag, energy)


def coefficient_matrix(basis_real, basis_imag):
    round_real = basis_real.astype(jnp.bfloat16)
    round_imag = basis_imag.astype(jnp.bfloat16)
    upper_half = jnp.concatenate([round_real, round_imag], axis=2)
    lower_half = jnp.concatenate([-round_imag, round_real], axis=2)
    return jnp.stack([upper_half, lower_half], axis=1)


def phase_turn(correlation, energy):
    gain_scale = 1.0 / jnp.sqrt(energy + 1e-06)
    tilt_real = gain_scale * correlation[:, :NM]
    tilt_imag = gain_scale * correlation[:, NM:]
    tilt_size = jnp.sqrt(jnp.maximum(tilt_real * tilt_real + tilt_imag * tilt_imag, 0.25))
    return (gain_scale * tilt_real / tilt_size, -gain_scale * tilt_imag / tilt_size)


def finish(projected, factor_real, factor_imag, root_weight):
    part_real = projected[:, :NM]
    part_imag = projected[:, NM:]
    inverse_root = 1.0 / root_weight
    out_real = (
        part_real * factor_real[:, :, None] - part_imag * factor_imag[:, :, None]
    ) * inverse_root
    out_imag = (
        part_real * factor_imag[:, :, None] + part_imag * factor_real[:, :, None]
    ) * inverse_root
    return jnp.concatenate([out_real, out_imag], axis=1)


def shards(snapshots, weights, reference_field, start_basis):
    dft_rows = dft_table()
    half_len = NFFT // 2
    rows_here = snapshots.shape[1]
    total_rows = rows_here * lax.axis_size(("grp", "row"))
    hop_rows = snapshots.reshape(NBLK + 1, half_len, rows_here)
    root_weight = jnp.sqrt(weights)
    leading = jnp.einsum(
        "pft,htx->fphx",
        dft_rows[:, :, :half_len],
        hop_rows[:NBLK],
        preferred_element_type=jnp.float32,
    )
    trailing = jnp.einsum(
        "pft,htx->fphx", dft_rows[:, :, half_len:], hop_rows[1:], preferred_element_type=jnp.float32
    )
    coeffs = ((leading + trailing) * root_weight).astype(jnp.bfloat16)
    real_part = jnp.einsum("fpbx,fpcx->fbc", coeffs, coeffs, preferred_element_type=jnp.float32)
    cross_part = jnp.einsum(
        "fbx,fcx->fbc", coeffs[:, 0], coeffs[:, 1], preferred_element_type=jnp.float32
    )
    cross_anti = cross_part - jnp.swapaxes(cross_part, 1, 2)
    gram_part = jnp.concatenate([real_part, cross_anti], axis=2)
    probe = (root_weight * reference_field).astype(jnp.bfloat16)
    projection_part = jnp.einsum("fpbx,x->fpb", coeffs, probe, preferred_element_type=jnp.float32)
    freq_share = lax.psum_scatter(gram_part, "row", scatter_dimension=0, tiled=True)
    summed = lax.psum(freq_share, "grp")
    local_count = summed.shape[0]
    local_start = lax.dynamic_slice_in_dim(
        start_basis, lax.axis_index("row") * local_count, local_count, 0
    )
    gram_real = summed[:, :NBLK, :NBLK] / total_rows
    gram_imag = summed[:, :NBLK, NBLK:] / total_rows
    basis_real, basis_imag, energy = subspace_solve(gram_real, gram_imag, local_start)
    local_matrix = coefficient_matrix(basis_real, basis_imag)
    extras = energy[:, None, :]
    coef_matrix = lax.all_gather(local_matrix, "row", axis=0, tiled=True)
    extras = lax.all_gather(extras, "row", axis=0, tiled=True)
    energies = extras[:, 0]
    projected = jnp.einsum(
        "fpbk,fpbx->fkx", coef_matrix, coeffs, preferred_element_type=jnp.float32
    )
    projection = lax.psum(projection_part, ("grp", "row")) / math.sqrt(total_rows)
    correlation = jnp.einsum(
        "fpb,fpbk->fk", projection, coef_matrix.astype(jnp.float32), precision=highest
    )
    factor_real, factor_imag = phase_turn(correlation, energies)
    return (finish(projected, factor_real, factor_imag, root_weight), energies)


def solution(mesh):
    in_specs = (P(None, ("grp", "row")), P(("grp", "row")), P(("grp", "row")), P())
    out_specs = (P(None, None, ("grp", "row")), P())
    return jax.shard_map(shards, mesh=mesh, in_specs=in_specs, out_specs=out_specs, check_vma=False)
```

profile of v0, /device:TPU:0, one launch (start us, length us, event | category | flops | bytes accessed | tf_op | source)
XLA Modules:
  0.0 395.5 jit_solution(15169235983462213389)
XLA Ops:
  7.2 0.6 multiply_reduce_fusion
  9.0 23.1 %fusion.75 = (bf16[8064,1024]{1,0:T(8,128)(2,1)}, bf16[8064,1024]{1,0:T(8,128)(2,1)}) fusion(bf16[8192,1024]{1,0:T(8,128)(2,1)} %param.6), kind=kLoop, calls=%fused_computation.299 | loop fusion | bytes 66060288 | tf_op jit(solution)/shard_map/slice | solution.py:124
  32.1 21.0 %fusion.63 = f32[2,64,63,1024]{3,1,2,0:T(8,128)} fusion(bf16[63,128,1024,1]{2,1,0,3:T(8,128)(2,1)} %bitcast.245, bf16[2,64,256]{2,1,0:T(8,128)(2,1)S(1)} %fusion.56), kind=kOutput, calls=%fused_computation.269 | convolution fusion | flops 2113929216 | bytes 49577984 | tf_op jit(solution)/shard_map/pft,htx->fphx/dot_general | solution.py:117
  53.2 23.1 %fusion.42 = bf16[64,2,63,1024]{3,0,2,1:T(8,128)(2,1)} fusion(f32[1024]{0:T(1024)S(1)} %get-tuple-element.226, f32[2,64,63,1024]{3,1,2,0:T(8,128)} %fusion.63, bf16[63,128,1024,1]{2,1,0,3:T(8,128)(2,1)} %bitcast.244, bf16[2,64,256]{2,1,0:T(8,128)(2,1)S(1)} %fusion.56), kind=kOutput, calls=%fused_computation.233 | convolution fusion | flops 2138701824 | bytes 66097152 | tf_op jit(solution)/shard_map/pft,htx->fphx/dot_general | solution.py:123
  76.3 12.3 %slice_bitcast_fusion.1 = (bf16[64,63,1024]{2,0,1:T(8,128)(2,1)}, bf16[64,63,1024]{2,0,1:T(8,128)(2,1)}) fusion(bf16[64,2,63,1024]{3,0,2,1:T(8,128)(2,1)} %fusion.42), kind=kLoop, calls=%fused_computation.238 | loop fusion | bytes 33030144 | tf_op jit(solution)/shard_map/squeeze | solution.py:129
  88.5 33.2 %fusion.49 = f32[64,63,63]{2,1,0:T(8,128)} fusion(bf16[64,2,63,1024]{3,0,2,1:T(8,128)(2,1)} %fusion.42), kind=kOutput, calls=%fused_computation.245 | convolution fusion | flops 1040449536 | bytes 17531136 | tf_op jit(solution)/shard_map/fpbx,fpcx->fbc/dot_general | solution.py:127
  121.7 14.5 %fusion.43 = f32[64,63,63]{2,1,0:T(8,128)S(1)} fusion(bf16[64,63,1024]{2,0,1:T(8,128)(2,1)} %get-tuple-element.213, bf16[64,63,1024]{2,0,1:T(8,128)(2,1)} %get-tuple-element.212), kind=kOutput, calls=%fused_computation.234 | convolution fusion | flops 520224768 | bytes 17531136 | tf_op jit(solution)/shard_map/fbx,fcx->fbc/dot_general | solution.py:128
  136.2 2.0 copy.242
  138.2 2.0 bitcast_subtract_fusion.14
  140.2 3.5 pad_maximum_fusion.1
  143.8 10.2 %fusion.71 = f32[1,64,2,63]{1,0,3,2:T(1,128)S(1)} fusion(bf16[64,2,63,1024]{3,0,2,1:T(8,128)(2,1)} %fusion.42, bf16[1024,1,1,1]{0,1,2,3:T(2,128)(2,1)S(1)} %reshape.3860), kind=kOutput, calls=%fused_computation.284 | convolution fusion | flops 16515072 | bytes 16549376 | tf_op jit(solution)/shard_map/fpbx,x->fpb/dot_general | solution.py:134
  154.0 28.4 %reduce-scatter.2.cloned.1.call-done = f32[8,63,126]{2,1,0:T(8,128)} async-done(((f32[64,63,126]{2,1,0:T(8,128)}), f32[8,63,126]{2,1,0:T(8,128)}) %reduce-scatter.2.cloned.1.call-update) | async-done | bytes 254032 | tf_op jit(solution)/shard_map/reduce_scatter | solution.py:135
  183.0 38.2 %psum.15 = f32[64,2,63]{2,1,0:T(2,128)S(1)} all-reduce(f32[64,2,63]{2,1,0:T(2,128)S(1)} %bitcast.248), channel_id=1, replica_groups=mesh['grp'=4,'row'=8] {'grp','row'}, use_global_device_ids=true, to_apply=%region_70.71 | all-reduce | flops 8064 | bytes 64512 | tf_op jit(solution)/shard_map/psum | solution.py:152
  221.3 5.9 %all-reduce.2.cloned.1.call-done = f32[8,63,126]{2,1,0:T(8,128)} async-done(((f32[8,63,126]{2,1,0:T(8,128)}), f32[8,63,126]{2,1,0:T(8,128)}) %all-reduce.2.cloned.1.call-update) | async-done | bytes 254032 | tf_op jit(solution)/shard_map/psum | solution.py:136
  227.2 1.2 slice_multiply_fusion
  228.4 92.7 %while.12 = (s32[]{:T(128)}, f32[8,63,8]{1,0,2:T(8,128)S(1)}, f32[8,63,8]{1,0,2:T(8,128)S(1)}, f32[8,63,63]{2,1,0:T(8,128)S(1)}, f32[8,63,63]{2,1,0:T(8,128)S(1)}, /*index=5*/s32[]{:T(128)}) while((s32[]{:T(128)}, f32[8,63,8]{1,0,2:T(8,128)S(1)}, f32[8,63,8]{1,0,2:T(8,128)S(1)}, f32[8,63,63]{2,1,0:T(8,128)S(1)}, ...), condition=%wide.region_68.69_spmd, body=%wide.region_3.68_spmd.sunk | while | flops 12931688 | bytes 1827781 | solution.py:73
  228.9 0.5 fusion.111
  229.5 0.5 fusion.112
  230.0 0.5 fusion.113
  236.2 0.5 fusion.110
  236.7 0.5 fusion.111
  237.2 0.5 fusion.112
  237.7 0.5 fusion.113
  243.9 0.5 fusion.110
  244.4 0.5 fusion.111
  244.9 0.5 fusion.112
  245.5 0.5 fusion.113
  252.1 0.5 fusion.111
  252.7 0.5 fusion.112
  253.2 0.5 fusion.113
  259.9 0.5 fusion.111
  260.4 0.5 fusion.112
  260.9 0.5 fusion.113
  267.6 0.5 fusion.111
  268.1 0.5 fusion.112
  268.6 0.5 fusion.113
  275.3 0.5 fusion.111
  275.8 0.5 fusion.112
  276.4 0.5 fusion.113
  283.0 0.5 fusion.111
  283.6 0.5 fusion.112
  284.1 0.5 fusion.113
  290.8 0.5 fusion.111
  291.3 0.5 fusion.112
  291.8 0.5 fusion.113
  298.5 0.5 fusion.111
  299.0 0.5 fusion.112
  299.6 0.5 fusion.113
  306.2 0.5 fusion.111
  306.8 0.5 fusion.112
  307.3 0.5 fusion.113
  314.0 0.5 fusion.111
  314.5 0.5 fusion.112
  315.0 0.5 fusion.113
  321.2 0.5 fusion.69
  321.7 0.5 fusion.65
  322.3 0.6 fusion.52
  322.9 0.7 fusion.55
  323.5 14.1 %all-gather = f32[64,8]{1,0:T(8,128)S(1)} all-gather(f32[8,8]{1,0:T(8,128)S(1)} %fusion.55), channel_id=2, replica_groups=mesh['grp'=4,'row'=8] {'row'}, dimensions={0}, use_global_device_ids=true | all-gather | bytes 2304 | tf_op jit(solution)/shard_map/all_gather | solution.py:147
  337.7 14.7 %all_gather.6 = bf16[64,2,63,16]{2,3,1,0:T(8,128)(2,1)S(1)} all-gather(bf16[8,2,63,16]{2,3,1,0:T(8,128)(2,1)S(1)} %pad_maximum_fusion.2), channel_id=1, replica_groups=mesh['grp'=4,'row'=8] {'row'}, dimensions={0}, use_global_device_ids=true | all-gather | bytes 290304 | tf_op jit(solution)/shard_map/all_gather | solution.py:146
  352.4 29.5 %fusion.46 = f32[64,16,1024]{2,1,0:T(8,128)} fusion(bf16[64,2,63,16]{2,3,1,0:T(8,128)(2,1)S(1)} %all_gather.6, bf16[64,2,63,1024]{3,0,2,1:T(8,128)(2,1)} %fusion.42), kind=kOutput, calls=%fused_computation.240 | convolution fusion | flops 264241152 | bytes 20967424 | tf_op jit(solution)/shard_map/fpbk,fpbx->fkx/dot_general | solution.py:149
  382.0 0.5 fusion.76
  382.8 2.9 subtract_multiply_fusion
  385.7 2.6 pad_maximum_fusion
  (524 shorter events, 72.4 us)
Async XLA Ops:
  7.2 175.2 %reduce-scatter.2.cloned.1.call-start = ((), (), s32[]{:S(2)}) async-start(), calls=%async_computation.1 | async-start | bytes 2359296 | tf_op jit(solution)/shard_map/reduce_scatter | solution.py:135
  32.1 21.1 %copy-start.3 = (f32[1024]{0:T(1024)S(1)}, f32[1024]{0:T(1024)}, u32[]{:S(2)}) copy-start(f32[1024]{0:T(1024)} %param.8) | copy-start | bytes 12292
  32.1 21.1 %copy-start.4 = (f32[1024]{0:T(1024)S(1)}, f32[1024]{0:T(1024)}, u32[]{:S(2)}) copy-start(f32[1024]{0:T(1024)} %param.7) | copy-start | bytes 12292
  143.7 83.5 %all-reduce.2.cloned.1.call-start = ((), (), s32[]{:S(2)}) async-start(), calls=%async_computation.2 | async-start | bytes 524288 | tf_op jit(solution)/shard_map/psum | solution.py:136
  143.8 38.6 %copy-start.1 = (f32[64,2,63,8]{0,3,2,1:T(8,128)S(1)}, f32[64,2,63,8]{0,3,2,1:T(8,128)}, u32[]{:S(2)}) copy-start(f32[64,2,63,8]{0,3,2,1:T(8,128)} %param.9) | copy-start | bytes 774148
  228.4 92.8 %copy-start = (f32[8,63,126]{2,1,0:T(8,128)S(1)}, f32[8,63,126]{2,1,0:T(8,128)}, u32[]{:S(2)}) copy-start(f32[8,63,126]{2,1,0:T(8,128)} %all-reduce.2.cloned.1.call-done) | copy-start | bytes 762052
  337.7 44.9 %copy-start.2 = (f32[64,8]{0,1:T(8,128)}, f32[64,8]{0,1:T(8,128)S(1)}, u32[]{:S(2)}) copy-start(f32[64,8]{0,1:T(8,128)S(1)} %copy.253) | copy-start | bytes 6148
Sparse Core Ops, SparseCore 0:
  143.9 38.4 reduce-scatter.1
  185.3 41.9 all-reduce.1
where the time goes:
time: 401 us; the launch traced here: 396 us
  matrix products  160 us (40%)
  other arithmetic  79 us (20%)
  blocking collectives  67 us (17%)
  local copies, waits for them, and re-layouts  38.4 us (10%)
  waiting for transfers between devices  34.3 us (9%)
  between operations  15.4 us (4%)
    psum x1, blocking collectives, shards(): lax.psum(projection_part, ('grp', 'row')) / math.sqrt(total_rows)  38.2 us
    dot_general x1, matrix products, shards(): jnp.einsum('fpbx,fpcx->fbc', coeffs, coeffs, preferred_element_type=jnp.f...  33.2 us
    dot_general x1, matrix products, shards(): jnp.einsum('fpbk,fpbx->fkx', coef_matrix, coeffs, preferred_element_type=...  29.5 us
    reduce_scatter x1, waiting for transfers between devices, shards(): lax.psum_scatter(gram_part, 'row', scatter_dimension=0, tiled=True)  28.4 us
    reduce_sum x96, other arithmetic, orthonormalize(): jnp.sum(prior_real * target_real + prior_imag * target_imag, axis=1, keep...  27.2 us
    slice x1, local copies, waits for them, and re-layouts, shards(): hop_rows[1:]  23.1 us
    dot_general x1, matrix products, shards(): jnp.einsum('pft,htx->fphx', dft_rows[:, :, half_len:], hop_rows[1:], pref...  23.1 us
    dot_general x1, matrix products, shards(): jnp.einsum('pft,htx->fphx', dft_rows[:, :, :half_len], hop_rows[:NBLK], p...  21 us
  transfers between devices with their start and end apart: 2, of which 2 were waited for; matrix products, arithmetic and copies ran while one was open for 3% of the time, Pallas kernels for 0%

commit v1 on v0

v1 whole, which is shorter than its diff:
```python
import functools
import math

import jax
import jax.numpy as jnp
import numpy as np
from jax import lax
from jax.experimental import pallas as pl
from jax.experimental.pallas import tpu as pltpu
from jax.sharding import PartitionSpec as P

NFFT = 256
HALF = NFFT // 2
NBLK = 63
NB = 64
NF = 64
NM = 8
ITERS = 12
EPS = 1e-06
LANES = 128
VMEM_LIMIT = 56 * 1024 * 1024

highest = lax.Precision.HIGHEST


def dft_table():
    time_steps = np.arange(NFFT, dtype=np.int32)
    freq_bins = np.arange(1, NF + 1, dtype=np.int32)
    wrapped = freq_bins[:, None] * time_steps[None, :] % NFFT
    angles = np.float32(2.0 * math.pi / NFFT) * wrapped.astype(np.float32)
    taper = np.float32(0.5) - np.float32(0.5) * np.cos(
        np.float32(2.0 * math.pi / NFFT) * time_steps.astype(np.float32)
    )
    taper = taper / np.sqrt(np.sum(taper * taper))
    stacked = np.concatenate([np.cos(angles), -np.sin(angles)]) * taper[None, :]
    return jnp.asarray(stacked, dtype=jnp.float32).astype(jnp.bfloat16)


class Plan:
    def __init__(self, grp, row):
        self.grp, self.row, self.deep = grp, row, row // 2
        self.split_grp = NF % (grp * row) == 0
        self.g_slots = grp if self.split_grp else 1
        self.owners = row * self.g_slots
        self.per = NF // self.owners

    def first_freq(self, core_slot, grp_slot, z_slot):
        row_index = lax.axis_index("row")
        core = (row_index & 1) ^ core_slot
        deep = (row_index >> 1) ^ z_slot
        owner = deep * 2 + core
        if self.split_grp:
            owner = (lax.axis_index("grp") ^ grp_slot) * self.row + owner
        return owner * self.per


def lane_index(shape):
    return lax.broadcasted_iota(jnp.int32, shape, 1)


def row_index_of(shape):
    return lax.broadcasted_iota(jnp.int32, shape, 0)


def transform_kernel(plan, snap_ref, root_ref, probe_ref, table_ref, coef_ref, keep_ref, send_ref, flip, gram):
    step = pl.program_id(0)
    tile = snap_ref.shape[1]
    pieces = tile // LANES
    table = table_ref[...]
    root = root_ref[...]

    def one_block(b, carry):
        rows = snap_ref[pl.ds(pl.multiple_of(b * HALF, HALF), NFFT), :]
        out = jnp.dot(table, rows, preferred_element_type=jnp.float32) * root
        for part in range(2):
            for piece in range(pieces):
                flip[piece, pl.ds(part * NB + b, NF, stride=2 * NB), :] = out[
                    part * NF : (part + 1) * NF, piece * LANES : (piece + 1) * LANES
                ]
        return carry

    lax.fori_loop(0, NBLK, one_block, 0, unroll=3)
    for piece in range(pieces):
        probe = probe_ref[:, piece * LANES : (piece + 1) * LANES]
        flip[piece, pl.ds(NB - 1, NF, stride=2 * NB), :] = jnp.broadcast_to(probe, (NF, LANES))
        flip[piece, pl.ds(2 * NB - 1, NF, stride=2 * NB), :] = jnp.zeros((NF, LANES), jnp.float32)

    @pl.when(step == 0)
    def _():
        gram[...] = jnp.zeros_like(gram)

    def one_freq(f, carry):
        base = pl.multiple_of(f * 2 * NB, 2 * NB)
        wide = jnp.concatenate([flip[piece, pl.ds(base, 2 * NB), :] for piece in range(pieces)], axis=1)
        coefs = wide.astype(jnp.bfloat16)
        coef_ref[f] = coefs
        gram[f] += lax.dot_general(
            coefs, coefs, (((1,), (1,)), ((), ())), preferred_element_type=jnp.float32
        )
        return carry

    lax.fori_loop(0, NF, one_freq, 0, unroll=4)

    @pl.when(step == pl.num_programs(0) - 1)
    def _():
        upper = row_index_of((NB, LANES)) < lane_index((NB, LANES))
        left = lane_index((NB // 2, LANES)) < NB

        def pack(f):
            top = gram[f, :NB, :]
            low = gram[f, NB:, :]
            real = top + pltpu.roll(low, NB, 1)
            imag = pltpu.roll(top, NB, 1) - low
            packed = jnp.where(upper, imag, real)
            return jnp.where(left, packed[: NB // 2], pltpu.roll(packed[NB // 2 :], NB, 1))

        for core_slot, out_ref in ((0, keep_ref), (1, send_ref)):

            def one_slot(slot, carry):
                first = plan.first_freq(core_slot, slot // plan.deep, slot % plan.deep)
                for j in range(plan.per):
                    out_ref[slot * plan.per + j] = pack(first + j)
                return carry

            lax.fori_loop(0, plan.g_slots * plan.deep, one_slot, 0)


def transform(plan, snapshots, root_weight, probe):
    rows_here = snapshots.shape[1]
    tile = min(256, rows_here)
    half_freqs = NF // 2
    packed = jax.ShapeDtypeStruct((half_freqs, NB // 2, LANES), jnp.float32)
    packed_spec = pl.BlockSpec((half_freqs, NB // 2, LANES), lambda i: (0, 0, 0))
    return pl.pallas_call(
        functools.partial(transform_kernel, plan),
        grid=(rows_here // tile,),
        in_specs=[
            pl.BlockSpec((snapshots.shape[0], tile), lambda i: (0, i)),
            pl.BlockSpec((1, tile), lambda i: (0, i)),
            pl.BlockSpec((1, tile), lambda i: (0, i)),
            pl.BlockSpec((2 * NF, NFFT), lambda i: (0, 0)),
        ],
        out_specs=[
            pl.BlockSpec((NF, 2 * NB, tile), lambda i: (0, 0, i)),
            packed_spec,
            packed_spec,
        ],
        out_shape=[
            jax.ShapeDtypeStruct((NF, 2 * NB, rows_here), jnp.bfloat16),
            packed,
            packed,
        ],
        scratch_shapes=[
            pltpu.VMEM((tile // LANES, NF * 2 * NB, LANES), jnp.float32),
            pltpu.VMEM((NF, 2 * NB, LANES), jnp.float32),
        ],
        compiler_params=pltpu.CompilerParams(vmem_limit_bytes=VMEM_LIMIT),
        name="transform",
    )(snapshots, root_weight[None], probe[None], dft_table())


def solve_kernel(plan, total_rows, packed_ref, start_ref, out_ref):
    lane = lane_index((NB, LANES))
    row = row_index_of((NB, LANES))
    col = lane & (NB - 1)
    left = lane < NB
    inside = (row < NBLK) & (col < NBLK)
    lane8 = lane_index((NM, LANES))
    row8 = row_index_of((NM, LANES))
    left8 = lane8 < NB

    systems, probes, basis = [], [], []
    for i in range(plan.per):
        folded = packed_ref[i]
        turned = pltpu.roll(folded, NB, 1)
        wide = jnp.concatenate([folded, turned], axis=0)
        twice = jnp.where(left, wide, pltpu.roll(wide, NB, 1))
        flipped = jnp.transpose(jnp.concatenate([twice, twice], axis=0))[:NB]
        real = jnp.where(inside, jnp.where(row >= col, twice, flipped), 0.0) / total_rows
        imag = jnp.where(row < col, twice, jnp.where(row > col, -flipped, 0.0))
        imag = jnp.where(inside, imag, 0.0) / total_rows
        systems.append(
            jnp.concatenate([jnp.where(left, real, -imag), jnp.where(left, imag, real)], axis=0)
        )
        along = twice[NB - 1 :]
        across = flipped[NB - 1 :]
        left1 = lane_index((1, LANES)) < NB
        probes.append((jnp.where(left1, along, across), jnp.where(left1, -across, along)))
        basis.append(start_ref[i])

    def image_of(i, v):
        return jnp.dot(v, systems[i], precision=highest, preferred_element_type=jnp.float32)

    def lane_sum(x):
        return jnp.sum(x, axis=1, keepdims=True)

    def orthonormalize(y):
        swapped = pltpu.roll(y, NB, 1)
        turned = jnp.where(left8, -swapped, swapped)
        v = jnp.zeros_like(y)
        for j in range(NM):
            pivot = jnp.broadcast_to(y[j : j + 1], y.shape)
            pivot_turned = jnp.broadcast_to(turned[j : j + 1], y.shape)
            size = lane_sum(pivot * pivot) + EPS
            v = jnp.where(row8 == j, pivot * lax.rsqrt(size), v)
            if j < NM - 1:
                inner_real = lane_sum(pivot * y)
                inner_imag = lane_sum(pivot_turned * y)
                inverse = 1.0 / size
                later = row8 > j
                a = jnp.where(later, inner_real * inverse, 0.0)
                c = jnp.where(later, inner_imag * inverse, 0.0)
                y, turned = (
                    y - (a * pivot + c * pivot_turned),
                    turned - (a * pivot_turned - c * pivot),
                )
        return v

    def sweep(index, current):
        images = [image_of(i, v) for i, v in enumerate(current)]
        return tuple(orthonormalize(y) for y in images)

    basis = lax.fori_loop(0, ITERS, sweep, tuple(basis))
    extras = jnp.zeros((NM, LANES), jnp.float32)
    scale = 1.0 / math.sqrt(total_rows)
    for i, v in enumerate(basis):
        energy = lane_sum(v * image_of(i, v))
        coef = v.astype(jnp.bfloat16).astype(jnp.float32)
        out_ref[i * NM : (i + 1) * NM] = coef
        gain = 1.0 / jnp.sqrt(energy + EPS)
        tilt_real = gain * (lane_sum(coef * probes[i][0]) * scale)
        tilt_imag = gain * (lane_sum(coef * probes[i][1]) * scale)
        size = jnp.sqrt(jnp.maximum(tilt_real * tilt_real + tilt_imag * tilt_imag, 0.25))
        extras = jnp.where(lane8 == 3 * i, gain * tilt_real / size, extras)
        extras = jnp.where(lane8 == 3 * i + 1, -gain * tilt_imag / size, extras)
        extras = jnp.where(lane8 == 3 * i + 2, energy, extras)
    out_ref[plan.per * NM :] = extras


def solve(plan, total_rows, packed, start):
    return pl.pallas_call(
        functools.partial(solve_kernel, plan, total_rows),
        out_shape=jax.ShapeDtypeStruct(((plan.per + 1) * NM, LANES), jnp.float32),
        compiler_params=pltpu.CompilerParams(vmem_limit_bytes=VMEM_LIMIT),
        name="solve",
    )(packed, start)


def modes_kernel(plan, coef_ref, pay_ref, root_ref, out_ref, energy_ref):
    inverse_root = 1.0 / root_ref[...]
    left = lane_index((NM, LANES)) < NB
    lane8 = lane_index((NM, LANES))
    slots = plan.owners

    def one_slot(slot, energies):
        core_slot = slot // (plan.g_slots * plan.deep)
        rest = slot % (plan.g_slots * plan.deep)
        first = plan.first_freq(core_slot, rest // plan.deep, rest % plan.deep)
        for j in range(plan.per):
            f = first + j
            c = pay_ref[slot, j * NM : (j + 1) * NM, :]
            matrix = jnp.concatenate([jnp.where(left, c, -c), pltpu.roll(c, NB, 1)], axis=0)
            extras = pay_ref[slot, plan.per * NM :, :]
            factor_real = extras[:, 3 * j : 3 * j + 1]
            factor_imag = extras[:, 3 * j + 1 : 3 * j + 2]
            projected = jnp.dot(
                matrix.astype(jnp.bfloat16), coef_ref[f], preferred_element_type=jnp.float32
            )
            real = projected[:NM]
            imag = projected[NM:]
            out_ref[f, :NM, :] = (real * factor_real - imag * factor_imag) * inverse_root
            out_ref[f, NM:, :] = (real * factor_imag + imag * factor_real) * inverse_root
            energies = jnp.where(lane8 == f, extras[:, 3 * j + 2 : 3 * j + 3], energies)
        return energies

    energies = lax.fori_loop(0, slots, one_slot, jnp.zeros((NM, LANES), jnp.float32), unroll=2)
    square = jnp.concatenate([energies] + [jnp.zeros_like(energies)] * (LANES // NM - 1), axis=0)
    energy_ref[...] = jnp.transpose(square)[:NF, :NM]


def modes(plan, coeffs, payload, root_weight):
    rows_here = coeffs.shape[2]
    tile = min(256, rows_here)
    return pl.pallas_call(
        functools.partial(modes_kernel, plan),
        grid=(rows_here // tile,),
        in_specs=[
            pl.BlockSpec((NF, 2 * NB, tile), lambda i: (0, 0, i)),
            pl.BlockSpec(payload.shape, lambda i: (0, 0, 0)),
            pl.BlockSpec((1, tile), lambda i: (0, i)),
        ],
        out_specs=[
            pl.BlockSpec((NF, 2 * NM, tile), lambda i: (0, 0, i)),
            pl.BlockSpec((NF, NM), lambda i: (0, 0)),
        ],
        out_shape=[
            jax.ShapeDtypeStruct((NF, 2 * NM, rows_here), jnp.float32),
            jax.ShapeDtypeStruct((NF, NM), jnp.float32),
        ],
        compiler_params=pltpu.CompilerParams(vmem_limit_bytes=VMEM_LIMIT),
        name="modes",
    )(coeffs, payload, root_weight[None])


def swap(x, axis, size, offset):
    return lax.ppermute(x, axis, [(i, i ^ offset) for i in range(size)])


def shards(plan, snapshots, weights, reference_field, start_basis):
    total_rows = snapshots.shape[1] * plan.grp * plan.row
    root_weight = jnp.sqrt(weights)
    probe = (root_weight * reference_field).astype(jnp.bfloat16).astype(jnp.float32)
    start = lax.dynamic_slice_in_dim(start_basis, plan.first_freq(0, 0, 0), plan.per, 0)
    start = jnp.pad(start, ((0, 0), (0, 0), (0, NB - NBLK), (0, 0)))
    start = jnp.transpose(start, (0, 3, 1, 2)).reshape(plan.per, NM, 2 * NB)

    coeffs, keep, send = transform(plan, snapshots, root_weight, probe)

    held = keep + swap(send, "row", plan.row, 1)
    if plan.split_grp:
        held = held.reshape((plan.grp, plan.deep * plan.per) + held.shape[1:])
        arrived = [swap(held[d], "grp", plan.grp, d) for d in range(1, plan.grp)]
        held = functools.reduce(jnp.add, arrived, held[0])
    held = held.reshape((plan.deep, plan.per) + held.shape[1:])
    arrived = [swap(held[d], "row", plan.row, 2 * d) for d in range(1, plan.deep)]
    held = functools.reduce(jnp.add, arrived, held[0])
    if not plan.split_grp:
        held = lax.psum(held, "grp")

    payload = solve(plan, total_rows, held, start)

    payload = jnp.stack(
        [payload] + [swap(payload, "row", plan.row, 2 * d) for d in range(1, plan.deep)]
    )
    if plan.split_grp:
        payload = jnp.concatenate(
            [payload] + [swap(payload, "grp", plan.grp, d) for d in range(1, plan.grp)]
        )
    payload = jnp.concatenate([payload, swap(payload, "row", plan.row, 1)])
    return tuple(modes(plan, coeffs, payload, root_weight))


def solution(mesh):
    plan = Plan(mesh.shape["grp"], mesh.shape["row"])
    in_specs = (P(None, ("grp", "row")), P(("grp", "row")), P(("grp", "row")), P())
    out_specs = (P(None, None, ("grp", "row")), P())
    return jax.shard_map(
        functools.partial(shards, plan),
        mesh=mesh,
        in_specs=in_specs,
        out_specs=out_specs,
        check_vma=False,
    )
```

time: 401 us -> 148 us (0.37); the launches traced: 396 us -> 148 us
  matrix products: 160 us -> 0 us
  Pallas kernels: 0 us -> 103 us
  other arithmetic: 79 us -> 3.85 us
  blocking collectives: 67 us -> 0 us
  local copies, waits for them, and re-layouts: 38.4 us -> 4.04 us
  starting transfers between devices: 0.08 us -> 17.1 us
  waiting for transfers between devices: 34.3 us -> 19.6 us
  between operations: 15.4 us -> 0.75 us
    dot_general x59 -> x0, matrix products: 160 us -> none  [the longest x1 33.2 us: shards(): jnp.einsum('fpbx,fpcx->fbc', coeffs, coeffs, preferred_element_type=jnp.f...]
    pallas_call x0 -> x3, Pallas kernels: none -> 103 us  [the longest x1 72.1 us: transform(): pl.pallas_call(functools.partial(transform_kernel, plan), grid=(rows_here...]
    reduce_sum x193 -> x0, other arithmetic: 45.2 us -> none  [the longest x96 27.2 us: orthonormalize(): jnp.sum(prior_real * target_real + prior_imag * target_imag, axis=1, keep...]
    psum x1 -> x0, blocking collectives: 38.2 us -> none  [shards(): lax.psum(projection_part, ('grp', 'row')) / math.sqrt(total_rows)]
    all_gather x2 -> x0, blocking collectives: 28.7 us -> none  [the longest x1 14.7 us: shards(): coef_matrix = lax.all_gather(local_matrix, 'row', axis=0, tiled=True)]
    reduce_scatter x1 -> x0, waiting for transfers between devices: 28.4 us -> none  [shards(): lax.psum_scatter(gram_part, 'row', scatter_dimension=0, tiled=True)]
    slice x2, local copies, waits for them, and re-layouts: 23.3 us -> 0.04 us  [the longest x1 0.03 us: shards(): arrived = [swap(held[d], 'grp', plan.grp, d) for d in range(1, plan.grp)]]
    ppermute x0 -> x14, waiting for transfers between devices: none -> 19.6 us  [swap(): return lax.ppermute(x, axis, [(i, i ^ offset) for i in range(size)])]
  transfers between devices with their start and end apart: 2 -> 14, of which waited for: 2 -> 11; matrix products, arithmetic and copies ran while one was open for 3% -> 1% of each run, Pallas kernels for 0% -> 0%
where the time goes in v1:
time: 148 us
  Pallas kernels  103 us (70%)
  waiting for transfers between devices  19.6 us (13%)
  starting transfers between devices  17.1 us (12%)
  local copies, waits for them, and re-layouts  4.04 us (3%)
  other arithmetic  3.85 us (3%)
    pallas_call x1, Pallas kernels, transform(): pl.pallas_call(functools.partial(transform_kernel, plan), grid=(rows_here...  72.1 us
    ppermute x14, waiting for transfers between devices, swap(): return lax.ppermute(x, axis, [(i, i ^ offset) for i in range(size)])  19.6 us
    ppermute x14, starting transfers between devices, swap(): return lax.ppermute(x, axis, [(i, i ^ offset) for i in range(size)])  17.1 us
    pallas_call x1, Pallas kernels, modes(): pl.pallas_call(functools.partial(modes_kernel, plan), grid=(rows_here //...  16.8 us
    pallas_call x1, Pallas kernels, solve(): pl.pallas_call(functools.partial(solve_kernel, plan, total_rows), out_sha...  13.8 us
  transfers between devices with their start and end apart: 14, of which 11 were waited for; matrix products, arithmetic and copies ran while one was open for 1% of the time, Pallas kernels for 0%

profile of v1, /device:TPU:0, one launch (start us, length us, event | category | flops | bytes accessed | tf_op | source)
XLA Modules:
  0.0 148.0 jit_solution(1949419932141781064)
XLA Ops:
  0.6 0.0 copy-start
  0.6 1.4 fusion.4
  2.0 72.1 %transform.1 = (bf16[64,128,1024]{2,1,0:T(8,128)(2,1)}, f32[32,32,128]{2,1,0:T(8,128)}, f32[32,32,128]{2,1,0:T(8,128)}) custom-call(bf16[8192,1024]{1,0:T(8,128)(2,1)} %snap_ref.1, f32[1,1024]{1,0:T(1,128)} %bitcast.22, f32[1,1024]{1,0:T(1,128)} %bitcast.24, bf16[128,256]{1,0:T(8,128)(2,1)} %constant.25.table_ref), custom_call_target="tpu_custom_call" | custom-call | tf_op jit(solution)/shard_map/transform/pallas_call | solution.py:134
  74.1 0.5 collective-permute-start
  74.5 1.7 %collective-permute-done = f32[32,32,128]{2,1,0:T(8,128)S(1)} collective-permute-done((f32[32,32,128]{2,1,0:T(8,128)}, f32[32,32,128]{2,1,0:T(8,128)S(1)}, u32[]{:S(2)}, u32[]{:S(2)}) %collective-permute-start) | collective-permute-done | bytes 524320 | tf_op jit(solution)/shard_map/ppermute | solution.py:306
  76.3 1.1 add.32
  77.4 2.9 %collective-permute-start.1 = (f32[8,32,128]{2,1,0:T(8,128)S(1)}, f32[8,32,128]{2,1,0:T(8,128)S(1)}, u32[]{:S(2)}, u32[]{:S(2)}) collective-permute-start(f32[8,32,128]{2,1,0:T(8,128)S(1)} %get-tuple-element.10), channel_id=1, source_target_pairs={{0,8},{8,0},{16,24},{24,16},{1,9},{9,1},{17,25},{25,17},{2,10},{10... | collective-permute-start | bytes 393224 | tf_op jit(solution)/shard_map/ppermute | solution.py:306
  80.4 1.5 %collective-permute-start.3 = (f32[8,32,128]{2,1,0:T(8,128)S(1)}, f32[8,32,128]{2,1,0:T(8,128)S(1)}, u32[]{:S(2)}, u32[]{:S(2)}) collective-permute-start(f32[8,32,128]{2,1,0:T(8,128)S(1)} %get-tuple-element.11), channel_id=1, source_target_pairs={{0,24},{8,16},{16,8},{24,0},{1,25},{9,17},{17,9},{25,1},{2,26},{10... | collective-permute-start | bytes 393224 | tf_op jit(solution)/shard_map/ppermute | solution.py:306
  81.8 0.1 collective-permute-start.2
  81.9 2.6 %collective-permute-done.1 = f32[8,32,128]{2,1,0:T(8,128)S(1)} collective-permute-done((f32[8,32,128]{2,1,0:T(8,128)S(1)}, f32[8,32,128]{2,1,0:T(8,128)S(1)}, u32[]{:S(2)}, u32[]{:S(2)}) %collective-permute-start.1) | collective-permute-done | bytes 131104 | tf_op jit(solution)/shard_map/ppermute | solution.py:306
  84.5 3.8 %collective-permute-done.3 = f32[8,32,128]{2,1,0:T(8,128)S(1)} collective-permute-done((f32[8,32,128]{2,1,0:T(8,128)S(1)}, f32[8,32,128]{2,1,0:T(8,128)S(1)}, u32[]{:S(2)}, u32[]{:S(2)}) %collective-permute-start.3) | collective-permute-done | bytes 131104 | tf_op jit(solution)/shard_map/ppermute | solution.py:306
  88.3 1.4 collective-permute-done.2
  89.7 1.6 %collective-permute-start.4 = (f32[2,32,128]{2,1,0:T(8,128)S(1)}, f32[2,32,128]{2,1,0:T(8,128)S(1)}, u32[]{:S(2)}, u32[]{:S(2)}) collective-permute-start(f32[2,32,128]{2,1,0:T(8,128)S(1)} %get-tuple-element.13), channel_id=1, source_target_pairs={{0,2},{1,3},{2,0},{3,1},{4,6},{5,7},{6,4},{7,5},{8,10},{9,11},{10,... | collective-permute-start | bytes 98312 | tf_op jit(solution)/shard_map/ppermute | solution.py:306
  91.3 2.5 %collective-permute-start.6 = (f32[2,32,128]{2,1,0:T(8,128)S(1)}, f32[2,32,128]{2,1,0:T(8,128)S(1)}, u32[]{:S(2)}, u32[]{:S(2)}) collective-permute-start(f32[2,32,128]{2,1,0:T(8,128)S(1)} %get-tuple-element.14), channel_id=1, source_target_pairs={{0,6},{1,7},{2,4},{3,5},{4,2},{5,3},{6,0},{7,1},{8,14},{9,15},{10,... | collective-permute-start | bytes 98312 | tf_op jit(solution)/shard_map/ppermute | solution.py:306
  93.8 0.1 collective-permute-start.5
  93.9 0.0 copy-done
  93.9 0.2 constant_dynamic-slice_fusion
  94.2 0.8 copy.9.start_ref
  95.0 0.0 collective-permute-done.4
  95.0 2.1 %collective-permute-done.6 = f32[2,32,128]{2,1,0:T(8,128)S(1)} collective-permute-done((f32[2,32,128]{2,1,0:T(8,128)S(1)}, f32[2,32,128]{2,1,0:T(8,128)S(1)}, u32[]{:S(2)}, u32[]{:S(2)}) %collective-permute-start.6) | collective-permute-done | bytes 32800 | tf_op jit(solution)/shard_map/ppermute | solution.py:306
  97.0 1.9 %collective-permute-done.5 = f32[2,32,128]{2,1,0:T(8,128)S(1)} collective-permute-done((f32[2,32,128]{2,1,0:T(8,128)S(1)}, f32[2,32,128]{2,1,0:T(8,128)S(1)}, u32[]{:S(2)}, u32[]{:S(2)}) %collective-permute-start.5) | collective-permute-done | bytes 32800 | tf_op jit(solution)/shard_map/ppermute | solution.py:306
  99.0 0.6 fusion.3.packed_ref
  99.6 13.8 %solve.1 = f32[24,128]{1,0:T(8,128)} custom-call(f32[2,32,128]{2,1,0:T(8,128)} %fusion.3.packed_ref, f32[2,8,128]{2,1,0:T(8,128)} %copy.9.start_ref), custom_call_target="tpu_custom_call" | custom-call | tf_op jit(solution)/shard_map/solve/pallas_call | solution.py:241
  113.4 1.2 collective-permute-start.9
  114.7 0.6 collective-permute-start.8
  115.3 2.5 %collective-permute-start.7 = (f32[24,128]{1,0:T(8,128)}, f32[24,128]{1,0:T(8,128)S(1)}, u32[]{:S(2)}, u32[]{:S(2)}) collective-permute-start(f32[24,128]{1,0:T(8,128)} %solve.1), channel_id=1, source_target_pairs={{0,2},{1,3},{2,0},{3,1},{4,6},{5,7},{6,4},{7,5},{8,10},{9,11},{10,... | collective-permute-start | bytes 36872 | tf_op jit(solution)/shard_map/ppermute | solution.py:306
  117.8 0.7 constant_dynamic-update-slice_fusion.6
  118.5 0.6 collective-permute-done.9
  119.1 0.4 collective-permute-done.8
  119.5 0.2 collective-permute-done.7
  119.7 0.7 pad_maximum_fusion
  120.4 1.4 collective-permute-start.12
  121.9 1.5 %collective-permute-start.11 = (f32[4,24,128]{2,1,0:T(8,128)S(1)}, f32[4,24,128]{2,1,0:T(8,128)S(1)}, u32[]{:S(2)}, u32[]{:S(2)}) collective-permute-start(f32[4,24,128]{2,1,0:T(8,128)S(1)} %pad_maximum_fusion), channel_id=1, source_target_pairs={{0,16},{8,24},{16,0},{24,8},{1,17},{9,25},{17,1},{25,9},{2,18},{10... | collective-permute-start | bytes 147464 | tf_op jit(solution)/shard_map/ppermute | solution.py:306
  123.4 0.5 collective-permute-start.10
  123.9 3.5 %collective-permute-done.10 = f32[4,24,128]{2,1,0:T(8,128)S(1)} collective-permute-done((f32[4,24,128]{2,1,0:T(8,128)S(1)}, f32[4,24,128]{2,1,0:T(8,128)S(1)}, u32[]{:S(2)}, u32[]{:S(2)}) %collective-permute-start.10) | collective-permute-done | bytes 49184 | tf_op jit(solution)/shard_map/ppermute | solution.py:306
  127.5 0.0 collective-permute-done.11
  127.5 0.0 collective-permute-done.12
  127.5 0.1 collective-permute-start.13
  127.6 1.4 collective-permute-done.13
  129.1 0.0 copy-start.1
  129.1 0.7 copy-done.1
  129.8 16.8 %modes.1 = (f32[64,16,1024]{2,1,0:T(8,128)}, f32[64,8]{1,0:T(8,128)}) custom-call(bf16[64,128,1024]{2,1,0:T(8,128)(2,1)} %get-tuple-element.5.coef_ref, f32[32,24,128]{2,1,0:T(8,128)} %copy-done.1, f32[1,1024]{1,0:T(1,128)} %bitcast.23), custom_call_target="tpu_custom_call" | custom-call | tf_op jit(solution)/shard_map/modes/pallas_call | solution.py:284
  146.6 1.4 copy.8
  (11 shorter events, 0.2 us)
Async XLA Ops:
  0.6 93.3 %copy-start = (f32[64,2,63,8]{0,3,2,1:T(8,128)S(1)}, f32[64,2,63,8]{0,3,2,1:T(8,128)}, u32[]{:S(2)}) copy-start(f32[64,2,63,8]{0,3,2,1:T(8,128)} %param.8) | copy-start | bytes 774148
  74.1 2.2 %collective-permute-start = (f32[32,32,128]{2,1,0:T(8,128)}, f32[32,32,128]{2,1,0:T(8,128)S(1)}, u32[]{:S(2)}, u32[]{:S(2)}) collective-permute-start(f32[32,32,128]{2,1,0:T(8,128)} %get-tuple-element.7), channel_id=1, source_target_pairs={{0,1},{1,0},{2,3},{3,2},{4,5},{5,4},{6,7},{7,6},{8,9},{9,8},{10,11... | collective-permute-start | bytes 1572872 | tf_op jit(solution)/shard_map/ppermute | solution.py:306
  77.4 7.0 %collective-permute-start.1 = (f32[8,32,128]{2,1,0:T(8,128)S(1)}, f32[8,32,128]{2,1,0:T(8,128)S(1)}, u32[]{:S(2)}, u32[]{:S(2)}) collective-permute-start(f32[8,32,128]{2,1,0:T(8,128)S(1)} %get-tuple-element.10), channel_id=1, source_target_pairs={{0,8},{8,0},{16,24},{24,16},{1,9},{9,1},{17,25},{25,17},{2,10},{10... | collective-permute-start | bytes 393224 | tf_op jit(solution)/shard_map/ppermute | solution.py:306
  80.4 7.9 %collective-permute-start.3 = (f32[8,32,128]{2,1,0:T(8,128)S(1)}, f32[8,32,128]{2,1,0:T(8,128)S(1)}, u32[]{:S(2)}, u32[]{:S(2)}) collective-permute-start(f32[8,32,128]{2,1,0:T(8,128)S(1)} %get-tuple-element.11), channel_id=1, source_target_pairs={{0,24},{8,16},{16,8},{24,0},{1,25},{9,17},{17,9},{25,1},{2,26},{10... | collective-permute-start | bytes 393224 | tf_op jit(solution)/shard_map/ppermute | solution.py:306
  81.8 7.8 %collective-permute-start.2 = (f32[8,32,128]{2,1,0:T(8,128)S(1)}, f32[8,32,128]{2,1,0:T(8,128)S(1)}, u32[]{:S(2)}, u32[]{:S(2)}) collective-permute-start(f32[8,32,128]{2,1,0:T(8,128)S(1)} %get-tuple-element.12), channel_id=1, source_target_pairs={{0,16},{8,24},{16,0},{24,8},{1,17},{9,25},{17,1},{25,9},{2,18},{10... | collective-permute-start | bytes 393224 | tf_op jit(solution)/shard_map/ppermute | solution.py:306
  89.7 5.3 %collective-permute-start.4 = (f32[2,32,128]{2,1,0:T(8,128)S(1)}, f32[2,32,128]{2,1,0:T(8,128)S(1)}, u32[]{:S(2)}, u32[]{:S(2)}) collective-permute-start(f32[2,32,128]{2,1,0:T(8,128)S(1)} %get-tuple-element.13), channel_id=1, source_target_pairs={{0,2},{1,3},{2,0},{3,1},{4,6},{5,7},{6,4},{7,5},{8,10},{9,11},{10,... | collective-permute-start | bytes 98312 | tf_op jit(solution)/shard_map/ppermute | solution.py:306
  91.3 5.7 %collective-permute-start.6 = (f32[2,32,128]{2,1,0:T(8,128)S(1)}, f32[2,32,128]{2,1,0:T(8,128)S(1)}, u32[]{:S(2)}, u32[]{:S(2)}) collective-permute-start(f32[2,32,128]{2,1,0:T(8,128)S(1)} %get-tuple-element.14), channel_id=1, source_target_pairs={{0,6},{1,7},{2,4},{3,5},{4,2},{5,3},{6,0},{7,1},{8,14},{9,15},{10,... | collective-permute-start | bytes 98312 | tf_op jit(solution)/shard_map/ppermute | solution.py:306
  93.8 5.2 %collective-permute-start.5 = (f32[2,32,128]{2,1,0:T(8,128)S(1)}, f32[2,32,128]{2,1,0:T(8,128)S(1)}, u32[]{:S(2)}, u32[]{:S(2)}) collective-permute-start(f32[2,32,128]{2,1,0:T(8,128)S(1)} %get-tuple-element.15), channel_id=1, source_target_pairs={{0,4},{1,5},{2,6},{3,7},{4,0},{5,1},{6,2},{7,3},{8,12},{9,13},{10,... | collective-permute-start | bytes 98312 | tf_op jit(solution)/shard_map/ppermute | solution.py:306
  113.4 5.7 %collective-permute-start.9 = (f32[24,128]{1,0:T(8,128)}, f32[24,128]{1,0:T(8,128)S(1)}, u32[]{:S(2)}, u32[]{:S(2)}) collective-permute-start(f32[24,128]{1,0:T(8,128)} %solve.1), channel_id=1, source_target_pairs={{0,6},{1,7},{2,4},{3,5},{4,2},{5,3},{6,0},{7,1},{8,14},{9,15},{10,... | collective-permute-start | bytes 36872 | tf_op jit(solution)/shard_map/ppermute | solution.py:306
  114.7 4.8 %collective-permute-start.8 = (f32[24,128]{1,0:T(8,128)}, f32[24,128]{1,0:T(8,128)S(1)}, u32[]{:S(2)}, u32[]{:S(2)}) collective-permute-start(f32[24,128]{1,0:T(8,128)} %solve.1), channel_id=1, source_target_pairs={{0,4},{1,5},{2,6},{3,7},{4,0},{5,1},{6,2},{7,3},{8,12},{9,13},{10,... | collective-permute-start | bytes 36872 | tf_op jit(solution)/shard_map/ppermute | solution.py:306
  115.3 4.4 %collective-permute-start.7 = (f32[24,128]{1,0:T(8,128)}, f32[24,128]{1,0:T(8,128)S(1)}, u32[]{:S(2)}, u32[]{:S(2)}) collective-permute-start(f32[24,128]{1,0:T(8,128)} %solve.1), channel_id=1, source_target_pairs={{0,2},{1,3},{2,0},{3,1},{4,6},{5,7},{6,4},{7,5},{8,10},{9,11},{10,... | collective-permute-start | bytes 36872 | tf_op jit(solution)/shard_map/ppermute | solution.py:306
  120.4 7.1 %collective-permute-start.12 = (f32[4,24,128]{2,1,0:T(8,128)S(1)}, f32[4,24,128]{2,1,0:T(8,128)S(1)}, u32[]{:S(2)}, u32[]{:S(2)}) collective-permute-start(f32[4,24,128]{2,1,0:T(8,128)S(1)} %pad_maximum_fusion), channel_id=1, source_target_pairs={{0,24},{8,16},{16,8},{24,0},{1,25},{9,17},{17,9},{25,1},{2,26},{10... | collective-permute-start | bytes 147464 | tf_op jit(solution)/shard_map/ppermute | solution.py:306
  121.9 5.6 %collective-permute-start.11 = (f32[4,24,128]{2,1,0:T(8,128)S(1)}, f32[4,24,128]{2,1,0:T(8,128)S(1)}, u32[]{:S(2)}, u32[]{:S(2)}) collective-permute-start(f32[4,24,128]{2,1,0:T(8,128)S(1)} %pad_maximum_fusion), channel_id=1, source_target_pairs={{0,16},{8,24},{16,0},{24,8},{1,17},{9,25},{17,1},{25,9},{2,18},{10... | collective-permute-start | bytes 147464 | tf_op jit(solution)/shard_map/ppermute | solution.py:306
  123.4 4.1 %collective-permute-start.10 = (f32[4,24,128]{2,1,0:T(8,128)S(1)}, f32[4,24,128]{2,1,0:T(8,128)S(1)}, u32[]{:S(2)}, u32[]{:S(2)}) collective-permute-start(f32[4,24,128]{2,1,0:T(8,128)S(1)} %pad_maximum_fusion), channel_id=1, source_target_pairs={{0,8},{8,0},{16,24},{24,16},{1,9},{9,1},{17,25},{25,17},{2,10},{10... | collective-permute-start | bytes 147464 | tf_op jit(solution)/shard_map/ppermute | solution.py:306
  127.5 1.5 %collective-permute-start.13 = (f32[16,24,128]{2,1,0:T(8,128)S(1)}, f32[16,24,128]{2,1,0:T(8,128)S(1)}, u32[]{:S(2)}, u32[]{:S(2)}) collective-permute-start(f32[16,24,128]{2,1,0:T(8,128)S(1)} %get-tuple-element.16), channel_id=1, source_target_pairs={{0,1},{1,0},{2,3},{3,2},{4,5},{5,4},{6,7},{7,6},{8,9},{9,8},{10,11... | collective-permute-start | bytes 589832 | tf_op jit(solution)/shard_map/ppermute | solution.py:306
  129.1 0.7 copy-start.1

commit v2 on v1

--- a/solution.py
+++ b/solution.py
@@ -18,9 +18,8 @@
 ITERS = 12
 EPS = 1e-06
 LANES = 128
+PITCH = 2 * NB + 1
 VMEM_LIMIT = 56 * 1024 * 1024
-
-highest = lax.Precision.HIGHEST
 
 
 def dft_table():
@@ -74,24 +73,25 @@
         out = jnp.dot(table, rows, preferred_element_type=jnp.float32) * root
         for part in range(2):
             for piece in range(pieces):
-                flip[piece, pl.ds(part * NB + b, NF, stride=2 * NB), :] = out[
+                flip[piece, pl.ds(part * NB + b, NF, stride=PITCH), :] = out[
                     part * NF : (part + 1) * NF, piece * LANES : (piece + 1) * LANES
                 ]
         return carry
 
-    lax.fori_loop(0, NBLK, one_block, 0, unroll=3)
+    lax.fori_loop(0, NBLK, one_block, 0, unroll=21)
     for piece in range(pieces):
         probe = probe_ref[:, piece * LANES : (piece + 1) * LANES]
-        flip[piece, pl.ds(NB - 1, NF, stride=2 * NB), :] = jnp.broadcast_to(probe, (NF, LANES))
-        flip[piece, pl.ds(2 * NB - 1, NF, stride=2 * NB), :] = jnp.zeros((NF, LANES), jnp.float32)
+        flip[piece, pl.ds(NB - 1, NF, stride=PITCH), :] = jnp.broadcast_to(probe, (NF, LANES))
+        flip[piece, pl.ds(2 * NB - 1, NF, stride=PITCH), :] = jnp.zeros((NF, LANES), jnp.float32)
 
     @pl.when(step == 0)
     def _():
         gram[...] = jnp.zeros_like(gram)
 
     def one_freq(f, carry):
-        base = pl.multiple_of(f * 2 * NB, 2 * NB)
-        wide = jnp.concatenate([flip[piece, pl.ds(base, 2 * NB), :] for piece in range(pieces)], axis=1)
+        wide = jnp.concatenate(
+            [flip[piece, pl.ds(f * PITCH, 2 * NB), :] for piece in range(pieces)], axis=1
+        )
         coefs = wide.astype(jnp.bfloat16)
         coef_ref[f] = coefs
         gram[f] += lax.dot_general(
@@ -99,7 +99,7 @@
         )
         return carry
 
-    lax.fori_loop(0, NF, one_freq, 0, unroll=4)
+    lax.fori_loop(0, NF, one_freq, 0, unroll=16)
 
     @pl.when(step == pl.num_programs(0) - 1)
     def _():
@@ -122,7 +122,7 @@
                     out_ref[slot * plan.per + j] = pack(first + j)
                 return carry
 
-            lax.fori_loop(0, plan.g_slots * plan.deep, one_slot, 0)
+            lax.fori_loop(0, plan.g_slots * plan.deep, one_slot, 0, unroll=4)
 
 
 def transform(plan, snapshots, root_weight, probe):
@@ -151,12 +151,20 @@
             packed,
         ],
         scratch_shapes=[
-            pltpu.VMEM((tile // LANES, NF * 2 * NB, LANES), jnp.float32),
+            pltpu.VMEM((tile // LANES, NF * PITCH, LANES), jnp.float32),
             pltpu.VMEM((NF, 2 * NB, LANES), jnp.float32),
         ],
         compiler_params=pltpu.CompilerParams(vmem_limit_bytes=VMEM_LIMIT),
         name="transform",
     )(snapshots, root_weight[None], probe[None], dft_table())
+
+
+def split_three(x):
+    high = x.astype(jnp.bfloat16)
+    rest = x - high.astype(jnp.float32)
+    middle = rest.astype(jnp.bfloat16)
+    low = (rest - middle.astype(jnp.float32)).astype(jnp.bfloat16)
+    return high, middle, low
 
 
 def solve_kernel(plan, total_rows, packed_ref, start_ref, out_ref):
@@ -179,8 +187,16 @@
         real = jnp.where(inside, jnp.where(row >= col, twice, flipped), 0.0) / total_rows
         imag = jnp.where(row < col, twice, jnp.where(row > col, -flipped, 0.0))
         imag = jnp.where(inside, imag, 0.0) / total_rows
+        system = jnp.concatenate([jnp.where(left, real, -imag), jnp.where(left, imag, real)], axis=0)
+        high, middle, low = split_three(system)
         systems.append(
-            jnp.concatenate([jnp.where(left, real, -imag), jnp.where(left, imag, real)], axis=0)
+            jnp.concatenate(
+                [
+                    jnp.concatenate([high, low], axis=1),
+                    jnp.concatenate([middle, jnp.zeros_like(low)], axis=1),
+                ],
+                axis=0,
+            )
         )
         along = twice[NB - 1 :]
         across = flipped[NB - 1 :]
@@ -189,7 +205,20 @@
         basis.append(start_ref[i])
 
     def image_of(i, v):
-        return jnp.dot(v, systems[i], precision=highest, preferred_element_type=jnp.float32)
+        high, middle, low = split_three(v)
+        zeros = jnp.zeros_like(high)
+        parts = jnp.concatenate(
+            [
+                jnp.concatenate([high, high], axis=1),
+                jnp.concatenate([middle, middle], axis=1),
+                jnp.concatenate([low, zeros], axis=1),
+                jnp.concatenate([zeros, zeros], axis=1),
+            ],
+            axis=0,
+        )
+        out = jnp.dot(parts, systems[i], preferred_element_type=jnp.float32)
+        small = out[:NM, LANES:] + out[2 * NM : 3 * NM, :LANES]
+        return out[:NM, :LANES] + (out[NM : 2 * NM, :LANES] + small)
 
     def lane_sum(x):
         return jnp.sum(x, axis=1, keepdims=True)
@@ -246,16 +275,13 @@
     )(packed, start)
 
 
-def modes_kernel(plan, coef_ref, pay_ref, root_ref, out_ref, energy_ref):
+def modes_kernel(plan, coef_ref, near_ref, far_ref, root_ref, out_ref, energy_ref):
     inverse_root = 1.0 / root_ref[...]
     left = lane_index((NM, LANES)) < NB
     lane8 = lane_index((NM, LANES))
-    slots = plan.owners
-
-    def one_slot(slot, energies):
-        core_slot = slot // (plan.g_slots * plan.deep)
-        rest = slot % (plan.g_slots * plan.deep)
-        first = plan.first_freq(core_slot, rest // plan.deep, rest % plan.deep)
+
+    def one_slot(core_slot, pay_ref, slot, energies):
+        first = plan.first_freq(core_slot, slot // plan.deep, slot % plan.deep)
         for j in range(plan.per):
             f = first + j
             c = pay_ref[slot, j * NM : (j + 1) * NM, :]
@@ -273,12 +299,20 @@
             energies = jnp.where(lane8 == f, extras[:, 3 * j + 2 : 3 * j + 3], energies)
         return energies
 
-    energies = lax.fori_loop(0, slots, one_slot, jnp.zeros((NM, LANES), jnp.float32), unroll=2)
+    energies = jnp.zeros((NM, LANES), jnp.float32)
+    for core_slot, pay_ref in ((0, near_ref), (1, far_ref)):
+        energies = lax.fori_loop(
+            0,
+            plan.g_slots * plan.deep,
+            functools.partial(one_slot, core_slot, pay_ref),
+            energies,
+            unroll=8,
+        )
     square = jnp.concatenate([energies] + [jnp.zeros_like(energies)] * (LANES // NM - 1), axis=0)
     energy_ref[...] = jnp.transpose(square)[:NF, :NM]
 
 
-def modes(plan, coeffs, payload, root_weight):
+def modes(plan, coeffs, near, far, root_weight):
     rows_here = coeffs.shape[2]
     tile = min(256, rows_here)
     return pl.pallas_call(
@@ -286,7 +320,8 @@
         grid=(rows_here // tile,),
         in_specs=[
             pl.BlockSpec((NF, 2 * NB, tile), lambda i: (0, 0, i)),
-            pl.BlockSpec(payload.shape, lambda i: (0, 0, 0)),
+            pl.BlockSpec(near.shape, lambda i: (0, 0, 0)),
+            pl.BlockSpec(far.shape, lambda i: (0, 0, 0)),
             pl.BlockSpec((1, tile), lambda i: (0, i)),
         ],
         out_specs=[
@@ -299,7 +334,7 @@
         ],
         compiler_params=pltpu.CompilerParams(vmem_limit_bytes=VMEM_LIMIT),
         name="modes",
-    )(coeffs, payload, root_weight[None])
+    )(coeffs, near, far, root_weight[None])
 
 
 def swap(x, axis, size, offset):
@@ -336,8 +371,7 @@
         payload = jnp.concatenate(
             [payload] + [swap(payload, "grp", plan.grp, d) for d in range(1, plan.grp)]
         )
-    payload = jnp.concatenate([payload, swap(payload, "row", plan.row, 1)])
-    return tuple(modes(plan, coeffs, payload, root_weight))
+    return tuple(modes(plan, coeffs, payload, swap(payload, "row", plan.row, 1), root_weight))
 
 
 def solution(mesh):

time: 148 us -> 90.6 us (0.61)
  Pallas kernels: 103 us -> 44.9 us
    pallas_call x1, Pallas kernels: 72.1 us -> 21.9 us  [transform(): pl.pallas_call(functools.partial(transform_kernel, plan), grid=(rows_here...]
    pallas_call x1, Pallas kernels: 16.8 us -> 10.1 us  [modes(): pl.pallas_call(functools.partial(modes_kernel, plan), grid=(rows_here //...]
  transfers between devices with their start and end apart: 14 -> 14, of which waited for: 11 -> 11; matrix products, arithmetic and copies ran while one was open for 1% -> 2% of each run, Pallas kernels for 0% -> 0%
where the time goes in v2:
time: 90.6 us; the launch traced here: 90.2 us
  Pallas kernels  44.9 us (50%)
  waiting for transfers between devices  19.6 us (22%)
  starting transfers between devices  17.1 us (19%)
  local copies, waits for them, and re-layouts  3.95 us (4%)
  other arithmetic  3.85 us (4%)
    pallas_call x1, Pallas kernels, transform(): pl.pallas_call(functools.partial(transform_kernel, plan), grid=(rows_here...  21.9 us
    ppermute x14, waiting for transfers between devices, swap(): return lax.ppermute(x, axis, [(i, i ^ offset) for i in range(size)])  19.6 us
    ppermute x14, starting transfers between devices, swap(): return lax.ppermute(x, axis, [(i, i ^ offset) for i in range(size)])  17.1 us
    pallas_call x1, Pallas kernels, solve(): pl.pallas_call(functools.partial(solve_kernel, plan, total_rows), out_sha...  13 us
    pallas_call x1, Pallas kernels, modes(): pl.pallas_call(functools.partial(modes_kernel, plan), grid=(rows_here //...  10.1 us
  transfers between devices with their start and end apart: 14, of which 11 were waited for; matrix products, arithmetic and copies ran while one was open for 2% of the time, Pallas kernels for 0%

profile of v2, /device:TPU:0, one launch (start us, length us, event | category | flops | bytes accessed | tf_op | source)
XLA Modules:
  0.0 90.2 jit_solution(15759382031919735363)
XLA Ops:
  0.6 0.0 copy-start
  0.6 1.4 %fusion.4 = (f32[1024]{0:T(1024)}, f32[1024]{0:T(1024)}) fusion(f32[1024]{0:T(1024)} %param.7, f32[1024]{0:T(1024)} %param.6), kind=kLoop, calls=%fused_computation.15 | loop fusion | flops 3072 | bytes 16384 | tf_op jit(solution)/shard_map/broadcast_in_dim | solution.py:159
  2.0 21.9 %transform.1 = (bf16[64,128,1024]{2,1,0:T(8,128)(2,1)}, f32[32,32,128]{2,1,0:T(8,128)}, f32[32,32,128]{2,1,0:T(8,128)}) custom-call(bf16[8192,1024]{1,0:T(8,128)(2,1)} %snap_ref.1, f32[1,1024]{1,0:T(1,128)} %bitcast.18, f32[1,1024]{1,0:T(1,128)} %bitcast.20, bf16[128,256]{1,0:T(8,128)(2,1)} %constant.25.table_ref), custom_call_target="tpu_custom_call" | custom-call | tf_op jit(solution)/shard_map/transform/pallas_call | solution.py:134
  23.9 0.5 collective-permute-start
  24.4 1.7 %collective-permute-done = f32[32,32,128]{2,1,0:T(8,128)S(1)} collective-permute-done((f32[32,32,128]{2,1,0:T(8,128)}, f32[32,32,128]{2,1,0:T(8,128)S(1)}, u32[]{:S(2)}, u32[]{:S(2)}) %collective-permute-start) | collective-permute-done | bytes 524320 | tf_op jit(solution)/shard_map/ppermute | solution.py:341
  26.1 1.1 %add.32 = f32[32,32,128]{2,1,0:T(8,128)S(1)} add(f32[32,32,128]{2,1,0:T(8,128)} %get-tuple-element.6, f32[32,32,128]{2,1,0:T(8,128)S(1)} %collective-permute-done) | non-fusion elementwise | flops 131072 | bytes 1572864 | tf_op jit(solution)/shard_map/add | solution.py:354
  27.3 2.9 %collective-permute-start.1 = (f32[8,32,128]{2,1,0:T(8,128)S(1)}, f32[8,32,128]{2,1,0:T(8,128)S(1)}, u32[]{:S(2)}, u32[]{:S(2)}) collective-permute-start(f32[8,32,128]{2,1,0:T(8,128)S(1)} %get-tuple-element.10), channel_id=1, source_target_pairs={{0,8},{8,0},{16,24},{24,16},{1,9},{9,1},{17,25},{25,17},{2,10},{10... | collective-permute-start | bytes 393224 | tf_op jit(solution)/shard_map/ppermute | solution.py:341
  30.2 1.5 %collective-permute-start.3 = (f32[8,32,128]{2,1,0:T(8,128)S(1)}, f32[8,32,128]{2,1,0:T(8,128)S(1)}, u32[]{:S(2)}, u32[]{:S(2)}) collective-permute-start(f32[8,32,128]{2,1,0:T(8,128)S(1)} %get-tuple-element.11), channel_id=1, source_target_pairs={{0,24},{8,16},{16,8},{24,0},{1,25},{9,17},{17,9},{25,1},{2,26},{10... | collective-permute-start | bytes 393224 | tf_op jit(solution)/shard_map/ppermute | solution.py:341
  31.7 0.1 collective-permute-start.2
  31.7 2.6 %collective-permute-done.1 = f32[8,32,128]{2,1,0:T(8,128)S(1)} collective-permute-done((f32[8,32,128]{2,1,0:T(8,128)S(1)}, f32[8,32,128]{2,1,0:T(8,128)S(1)}, u32[]{:S(2)}, u32[]{:S(2)}) %collective-permute-start.1) | collective-permute-done | bytes 131104 | tf_op jit(solution)/shard_map/ppermute | solution.py:341
  34.3 3.8 %collective-permute-done.3 = f32[8,32,128]{2,1,0:T(8,128)S(1)} collective-permute-done((f32[8,32,128]{2,1,0:T(8,128)S(1)}, f32[8,32,128]{2,1,0:T(8,128)S(1)}, u32[]{:S(2)}, u32[]{:S(2)}) %collective-permute-start.3) | collective-permute-done | bytes 131104 | tf_op jit(solution)/shard_map/ppermute | solution.py:341
  38.1 1.4 %collective-permute-done.2 = f32[8,32,128]{2,1,0:T(8,128)S(1)} collective-permute-done((f32[8,32,128]{2,1,0:T(8,128)S(1)}, f32[8,32,128]{2,1,0:T(8,128)S(1)}, u32[]{:S(2)}, u32[]{:S(2)}) %collective-permute-start.2) | collective-permute-done | bytes 131104 | tf_op jit(solution)/shard_map/ppermute | solution.py:341
  39.5 1.7 %collective-permute-start.4 = (f32[2,32,128]{2,1,0:T(8,128)S(1)}, f32[2,32,128]{2,1,0:T(8,128)S(1)}, u32[]{:S(2)}, u32[]{:S(2)}) collective-permute-start(f32[2,32,128]{2,1,0:T(8,128)S(1)} %get-tuple-element.13), channel_id=1, source_target_pairs={{0,2},{1,3},{2,0},{3,1},{4,6},{5,7},{6,4},{7,5},{8,10},{9,11},{10,... | collective-permute-start | bytes 98312 | tf_op jit(solution)/shard_map/ppermute | solution.py:341
  41.2 2.5 %collective-permute-start.6 = (f32[2,32,128]{2,1,0:T(8,128)S(1)}, f32[2,32,128]{2,1,0:T(8,128)S(1)}, u32[]{:S(2)}, u32[]{:S(2)}) collective-permute-start(f32[2,32,128]{2,1,0:T(8,128)S(1)} %get-tuple-element.14), channel_id=1, source_target_pairs={{0,6},{1,7},{2,4},{3,5},{4,2},{5,3},{6,0},{7,1},{8,14},{9,15},{10,... | collective-permute-start | bytes 98312 | tf_op jit(solution)/shard_map/ppermute | solution.py:341
  43.6 0.1 collective-permute-start.5
  43.8 0.0 copy-done
  43.8 0.2 constant_dynamic-slice_fusion
  44.0 0.8 copy.9.start_ref
  44.8 0.0 collective-permute-done.4
  44.8 2.1 %collective-permute-done.6 = f32[2,32,128]{2,1,0:T(8,128)S(1)} collective-permute-done((f32[2,32,128]{2,1,0:T(8,128)S(1)}, f32[2,32,128]{2,1,0:T(8,128)S(1)}, u32[]{:S(2)}, u32[]{:S(2)}) %collective-permute-start.6) | collective-permute-done | bytes 32800 | tf_op jit(solution)/shard_map/ppermute | solution.py:341
  46.9 1.9 %collective-permute-done.5 = f32[2,32,128]{2,1,0:T(8,128)S(1)} collective-permute-done((f32[2,32,128]{2,1,0:T(8,128)S(1)}, f32[2,32,128]{2,1,0:T(8,128)S(1)}, u32[]{:S(2)}, u32[]{:S(2)}) %collective-permute-start.5) | collective-permute-done | bytes 32800 | tf_op jit(solution)/shard_map/ppermute | solution.py:341
  48.8 0.6 fusion.3.packed_ref
  49.4 13.0 %solve.1 = f32[24,128]{1,0:T(8,128)} custom-call(f32[2,32,128]{2,1,0:T(8,128)} %fusion.3.packed_ref, f32[2,8,128]{2,1,0:T(8,128)} %copy.9.start_ref), custom_call_target="tpu_custom_call" | custom-call | tf_op jit(solution)/shard_map/solve/pallas_call | solution.py:270
  62.4 1.2 %collective-permute-start.9 = (f32[24,128]{1,0:T(8,128)}, f32[24,128]{1,0:T(8,128)S(1)}, u32[]{:S(2)}, u32[]{:S(2)}) collective-permute-start(f32[24,128]{1,0:T(8,128)} %solve.1), channel_id=1, source_target_pairs={{0,6},{1,7},{2,4},{3,5},{4,2},{5,3},{6,0},{7,1},{8,14},{9,15},{10,... | collective-permute-start | bytes 36872 | tf_op jit(solution)/shard_map/ppermute | solution.py:341
  63.6 0.6 collective-permute-start.8
  64.3 2.5 %collective-permute-start.7 = (f32[24,128]{1,0:T(8,128)}, f32[24,128]{1,0:T(8,128)S(1)}, u32[]{:S(2)}, u32[]{:S(2)}) collective-permute-start(f32[24,128]{1,0:T(8,128)} %solve.1), channel_id=1, source_target_pairs={{0,2},{1,3},{2,0},{3,1},{4,6},{5,7},{6,4},{7,5},{8,10},{9,11},{10,... | collective-permute-start | bytes 36872 | tf_op jit(solution)/shard_map/ppermute | solution.py:341
  66.8 0.7 constant_dynamic-update-slice_fusion.6
  67.5 0.6 collective-permute-done.9
  68.1 0.4 collective-permute-done.8
  68.5 0.2 collective-permute-done.7
  68.7 0.7 pad_maximum_fusion
  69.4 1.4 %collective-permute-start.12 = (f32[4,24,128]{2,1,0:T(8,128)S(1)}, f32[4,24,128]{2,1,0:T(8,128)S(1)}, u32[]{:S(2)}, u32[]{:S(2)}) collective-permute-start(f32[4,24,128]{2,1,0:T(8,128)S(1)} %pad_maximum_fusion), channel_id=1, source_target_pairs={{0,24},{8,16},{16,8},{24,0},{1,25},{9,17},{17,9},{25,1},{2,26},{10... | collective-permute-start | bytes 147464 | tf_op jit(solution)/shard_map/ppermute | solution.py:341
  70.8 1.5 %collective-permute-start.11 = (f32[4,24,128]{2,1,0:T(8,128)S(1)}, f32[4,24,128]{2,1,0:T(8,128)S(1)}, u32[]{:S(2)}, u32[]{:S(2)}) collective-permute-start(f32[4,24,128]{2,1,0:T(8,128)S(1)} %pad_maximum_fusion), channel_id=1, source_target_pairs={{0,16},{8,24},{16,0},{24,8},{1,17},{9,25},{17,1},{25,9},{2,18},{10... | collective-permute-start | bytes 147464 | tf_op jit(solution)/shard_map/ppermute | solution.py:341
  72.4 0.5 collective-permute-start.10
  72.9 3.5 %collective-permute-done.10 = f32[4,24,128]{2,1,0:T(8,128)S(1)} collective-permute-done((f32[4,24,128]{2,1,0:T(8,128)S(1)}, f32[4,24,128]{2,1,0:T(8,128)S(1)}, u32[]{:S(2)}, u32[]{:S(2)}) %collective-permute-start.10) | collective-permute-done | bytes 49184 | tf_op jit(solution)/shard_map/ppermute | solution.py:341
  76.4 0.0 collective-permute-done.11
  76.5 0.0 collective-permute-done.12
  76.5 0.0 copy-start.1
  76.5 0.1 collective-permute-start.13
  76.6 1.4 %collective-permute-done.13.far_ref = f32[16,24,128]{2,1,0:T(8,128)S(1)} collective-permute-done((f32[16,24,128]{2,1,0:T(8,128)S(1)}, f32[16,24,128]{2,1,0:T(8,128)S(1)}, u32[]{:S(2)}, u32[]{:S(2)}) %collective-permute-start.13) | collective-permute-done | bytes 196640 | tf_op jit(solution)/shard_map/ppermute | solution.py:341
  78.0 0.0 copy-start.2
  78.0 0.0 copy-done.1
  78.0 0.7 copy-done.2
  78.7 10.1 %modes.1 = (f32[64,16,1024]{2,1,0:T(8,128)}, f32[64,8]{1,0:T(8,128)}) custom-call(bf16[64,128,1024]{2,1,0:T(8,128)(2,1)} %get-tuple-element.5.coef_ref, f32[16,24,128]{2,1,0:T(8,128)} %copy-done.1, f32[16,24,128]{2,1,0:T(8,128)} %copy-done.2, f32[1,1024]{1,0:T(1,128)} %bitcast.19), custom_call_target="tpu_custom_call" | custom-call | tf_op jit(solution)/shard_map/modes/pallas_call | solution.py:318
  88.8 1.4 %copy.8 = f32[64,8]{0,1:T(8,128)} copy(f32[64,8]{1,0:T(8,128)} %get-tuple-element.9) | data formatting | bytes 4096 | tf_op jit(solution)/shard_map/modes/pallas_call | solution.py:318
  (10 shorter events, 0.1 us)
Async XLA Ops:
  0.6 43.1 %copy-start = (f32[64,2,63,8]{0,3,2,1:T(8,128)S(1)}, f32[64,2,63,8]{0,3,2,1:T(8,128)}, u32[]{:S(2)}) copy-start(f32[64,2,63,8]{0,3,2,1:T(8,128)} %param.8) | copy-start | bytes 774148
  23.9 2.2 %collective-permute-start = (f32[32,32,128]{2,1,0:T(8,128)}, f32[32,32,128]{2,1,0:T(8,128)S(1)}, u32[]{:S(2)}, u32[]{:S(2)}) collective-permute-start(f32[32,32,128]{2,1,0:T(8,128)} %get-tuple-element.7), channel_id=1, source_target_pairs={{0,1},{1,0},{2,3},{3,2},{4,5},{5,4},{6,7},{7,6},{8,9},{9,8},{10,11... | collective-permute-start | bytes 1572872 | tf_op jit(solution)/shard_map/ppermute | solution.py:341
  27.3 7.1 %collective-permute-start.1 = (f32[8,32,128]{2,1,0:T(8,128)S(1)}, f32[8,32,128]{2,1,0:T(8,128)S(1)}, u32[]{:S(2)}, u32[]{:S(2)}) collective-permute-start(f32[8,32,128]{2,1,0:T(8,128)S(1)} %get-tuple-element.10), channel_id=1, source_target_pairs={{0,8},{8,0},{16,24},{24,16},{1,9},{9,1},{17,25},{25,17},{2,10},{10... | collective-permute-start | bytes 393224 | tf_op jit(solution)/shard_map/ppermute | solution.py:341
  30.2 7.9 %collective-permute-start.3 = (f32[8,32,128]{2,1,0:T(8,128)S(1)}, f32[8,32,128]{2,1,0:T(8,128)S(1)}, u32[]{:S(2)}, u32[]{:S(2)}) collective-permute-start(f32[8,32,128]{2,1,0:T(8,128)S(1)} %get-tuple-element.11), channel_id=1, source_target_pairs={{0,24},{8,16},{16,8},{24,0},{1,25},{9,17},{17,9},{25,1},{2,26},{10... | collective-permute-start | bytes 393224 | tf_op jit(solution)/shard_map/ppermute | solution.py:341
  31.7 7.8 %collective-permute-start.2 = (f32[8,32,128]{2,1,0:T(8,128)S(1)}, f32[8,32,128]{2,1,0:T(8,128)S(1)}, u32[]{:S(2)}, u32[]{:S(2)}) collective-permute-start(f32[8,32,128]{2,1,0:T(8,128)S(1)} %get-tuple-element.12), channel_id=1, source_target_pairs={{0,16},{8,24},{16,0},{24,8},{1,17},{9,25},{17,1},{25,9},{2,18},{10... | collective-permute-start | bytes 393224 | tf_op jit(solution)/shard_map/ppermute | solution.py:341
  39.5 5.3 %collective-permute-start.4 = (f32[2,32,128]{2,1,0:T(8,128)S(1)}, f32[2,32,128]{2,1,0:T(8,128)S(1)}, u32[]{:S(2)}, u32[]{:S(2)}) collective-permute-start(f32[2,32,128]{2,1,0:T(8,128)S(1)} %get-tuple-element.13), channel_id=1, source_target_pairs={{0,2},{1,3},{2,0},{3,1},{4,6},{5,7},{6,4},{7,5},{8,10},{9,11},{10,... | collective-permute-start | bytes 98312 | tf_op jit(solution)/shard_map/ppermute | solution.py:341
  41.2 5.7 %collective-permute-start.6 = (f32[2,32,128]{2,1,0:T(8,128)S(1)}, f32[2,32,128]{2,1,0:T(8,128)S(1)}, u32[]{:S(2)}, u32[]{:S(2)}) collective-permute-start(f32[2,32,128]{2,1,0:T(8,128)S(1)} %get-tuple-element.14), channel_id=1, source_target_pairs={{0,6},{1,7},{2,4},{3,5},{4,2},{5,3},{6,0},{7,1},{8,14},{9,15},{10,... | collective-permute-start | bytes 98312 | tf_op jit(solution)/shard_map/ppermute | solution.py:341
  43.6 5.2 %collective-permute-start.5 = (f32[2,32,128]{2,1,0:T(8,128)S(1)}, f32[2,32,128]{2,1,0:T(8,128)S(1)}, u32[]{:S(2)}, u32[]{:S(2)}) collective-permute-start(f32[2,32,128]{2,1,0:T(8,128)S(1)} %get-tuple-element.15), channel_id=1, source_target_pairs={{0,4},{1,5},{2,6},{3,7},{4,0},{5,1},{6,2},{7,3},{8,12},{9,13},{10,... | collective-permute-start | bytes 98312 | tf_op jit(solution)/shard_map/ppermute | solution.py:341
  62.4 5.7 %collective-permute-start.9 = (f32[24,128]{1,0:T(8,128)}, f32[24,128]{1,0:T(8,128)S(1)}, u32[]{:S(2)}, u32[]{:S(2)}) collective-permute-start(f32[24,128]{1,0:T(8,128)} %solve.1), channel_id=1, source_target_pairs={{0,6},{1,7},{2,4},{3,5},{4,2},{5,3},{6,0},{7,1},{8,14},{9,15},{10,... | collective-permute-start | bytes 36872 | tf_op jit(solution)/shard_map/ppermute | solution.py:341
  63.6 4.8 %collective-permute-start.8 = (f32[24,128]{1,0:T(8,128)}, f32[24,128]{1,0:T(8,128)S(1)}, u32[]{:S(2)}, u32[]{:S(2)}) collective-permute-start(f32[24,128]{1,0:T(8,128)} %solve.1), channel_id=1, source_target_pairs={{0,4},{1,5},{2,6},{3,7},{4,0},{5,1},{6,2},{7,3},{8,12},{9,13},{10,... | collective-permute-start | bytes 36872 | tf_op jit(solution)/shard_map/ppermute | solution.py:341
  64.3 4.4 %collective-permute-start.7 = (f32[24,128]{1,0:T(8,128)}, f32[24,128]{1,0:T(8,128)S(1)}, u32[]{:S(2)}, u32[]{:S(2)}) collective-permute-start(f32[24,128]{1,0:T(8,128)} %solve.1), channel_id=1, source_target_pairs={{0,2},{1,3},{2,0},{3,1},{4,6},{5,7},{6,4},{7,5},{8,10},{9,11},{10,... | collective-permute-start | bytes 36872 | tf_op jit(solution)/shard_map/ppermute | solution.py:341
  69.4 7.1 %collective-permute-start.12 = (f32[4,24,128]{2,1,0:T(8,128)S(1)}, f32[4,24,128]{2,1,0:T(8,128)S(1)}, u32[]{:S(2)}, u32[]{:S(2)}) collective-permute-start(f32[4,24,128]{2,1,0:T(8,128)S(1)} %pad_maximum_fusion), channel_id=1, source_target_pairs={{0,24},{8,16},{16,8},{24,0},{1,25},{9,17},{17,9},{25,1},{2,26},{10... | collective-permute-start | bytes 147464 | tf_op jit(solution)/shard_map/ppermute | solution.py:341
  70.8 5.6 %collective-permute-start.11 = (f32[4,24,128]{2,1,0:T(8,128)S(1)}, f32[4,24,128]{2,1,0:T(8,128)S(1)}, u32[]{:S(2)}, u32[]{:S(2)}) collective-permute-start(f32[4,24,128]{2,1,0:T(8,128)S(1)} %pad_maximum_fusion), channel_id=1, source_target_pairs={{0,16},{8,24},{16,0},{24,8},{1,17},{9,25},{17,1},{25,9},{2,18},{10... | collective-permute-start | bytes 147464 | tf_op jit(solution)/shard_map/ppermute | solution.py:341
  72.4 4.1 %collective-permute-start.10 = (f32[4,24,128]{2,1,0:T(8,128)S(1)}, f32[4,24,128]{2,1,0:T(8,128)S(1)}, u32[]{:S(2)}, u32[]{:S(2)}) collective-permute-start(f32[4,24,128]{2,1,0:T(8,128)S(1)} %pad_maximum_fusion), channel_id=1, source_target_pairs={{0,8},{8,0},{16,24},{24,16},{1,9},{9,1},{17,25},{25,17},{2,10},{10... | collective-permute-start | bytes 147464 | tf_op jit(solution)/shard_map/ppermute | solution.py:341
  76.5 1.5 %copy-start.1 = (f32[16,24,128]{2,1,0:T(8,128)}, f32[16,24,128]{2,1,0:T(8,128)S(1)}, u32[]{:S(2)}) copy-start(f32[16,24,128]{2,1,0:T(8,128)S(1)} %constant_dynamic-update-slice_fusion.near_ref) | copy-start | bytes 589828
  76.5 1.5 %collective-permute-start.13 = (f32[16,24,128]{2,1,0:T(8,128)S(1)}, f32[16,24,128]{2,1,0:T(8,128)S(1)}, u32[]{:S(2)}, u32[]{:S(2)}) collective-permute-start(f32[16,24,128]{2,1,0:T(8,128)S(1)} %constant_dynamic-update-slice_fusion.near_ref), channel_id=1, source_target_pairs={{0,1},{1,0},{2,3},{3,2},{4,5},{5,4},{6,7},{7,6},{8,9},{9,8},{10,11... | collective-permute-start | bytes 589832 | tf_op jit(solution)/shard_map/ppermute | solution.py:341
  78.0 0.7 copy-start.2

commit v3 on v2

--- a/solution.py
+++ b/solution.py
@@ -19,7 +19,8 @@
 EPS = 1e-06
 LANES = 128
 PITCH = 2 * NB + 1
-VMEM_LIMIT = 56 * 1024 * 1024
+MIB = 1024 * 1024
+TRANSFORM_MIB, SOLVE_MIB, MODES_MIB = 28, 8, 8
 
 
 def dft_table():
@@ -61,12 +62,14 @@
     return lax.broadcasted_iota(jnp.int32, shape, 0)
 
 
-def transform_kernel(plan, snap_ref, root_ref, probe_ref, table_ref, coef_ref, keep_ref, send_ref, flip, gram):
+def transform_kernel(plan, snap_ref, weight_ref, field_ref, table_ref, coef_ref, keep_ref, send_ref, flip, gram):
     step = pl.program_id(0)
     tile = snap_ref.shape[1]
     pieces = tile // LANES
     table = table_ref[...]
-    root = root_ref[...]
+    root = jnp.sqrt(weight_ref[...])
+    probe_row = (root * field_ref[...]).astype(jnp.bfloat16).astype(jnp.float32)
+    here = pl.ds(pl.multiple_of(step * tile, tile), tile)
 
     def one_block(b, carry):
         rows = snap_ref[pl.ds(pl.multiple_of(b * HALF, HALF), NFFT), :]
@@ -80,7 +83,7 @@
 
     lax.fori_loop(0, NBLK, one_block, 0, unroll=21)
     for piece in range(pieces):
-        probe = probe_ref[:, piece * LANES : (piece + 1) * LANES]
+        probe = probe_row[:, piece * LANES : (piece + 1) * LANES]
         flip[piece, pl.ds(NB - 1, NF, stride=PITCH), :] = jnp.broadcast_to(probe, (NF, LANES))
         flip[piece, pl.ds(2 * NB - 1, NF, stride=PITCH), :] = jnp.zeros((NF, LANES), jnp.float32)
 
@@ -93,7 +96,7 @@
             [flip[piece, pl.ds(f * PITCH, 2 * NB), :] for piece in range(pieces)], axis=1
         )
         coefs = wide.astype(jnp.bfloat16)
-        coef_ref[f] = coefs
+        coef_ref[f, :, here] = coefs
         gram[f] += lax.dot_general(
             coefs, coefs, (((1,), (1,)), ((), ())), preferred_element_type=jnp.float32
         )
@@ -125,7 +128,7 @@
             lax.fori_loop(0, plan.g_slots * plan.deep, one_slot, 0, unroll=4)
 
 
-def transform(plan, snapshots, root_weight, probe):
+def transform(plan, snapshots, weights, reference_field):
     rows_here = snapshots.shape[1]
     tile = min(256, rows_here)
     half_freqs = NF // 2
@@ -141,7 +144,7 @@
             pl.BlockSpec((2 * NF, NFFT), lambda i: (0, 0)),
         ],
         out_specs=[
-            pl.BlockSpec((NF, 2 * NB, tile), lambda i: (0, 0, i)),
+            pl.BlockSpec(memory_space=pltpu.VMEM),
             packed_spec,
             packed_spec,
         ],
@@ -154,9 +157,9 @@
             pltpu.VMEM((tile // LANES, NF * PITCH, LANES), jnp.float32),
             pltpu.VMEM((NF, 2 * NB, LANES), jnp.float32),
         ],
-        compiler_params=pltpu.CompilerParams(vmem_limit_bytes=VMEM_LIMIT),
+        compiler_params=pltpu.CompilerParams(vmem_limit_bytes=TRANSFORM_MIB * MIB),
         name="transform",
-    )(snapshots, root_weight[None], probe[None], dft_table())
+    )(snapshots, weights[None], reference_field[None], dft_table())
 
 
 def split_three(x):
@@ -269,14 +272,18 @@
 def solve(plan, total_rows, packed, start):
     return pl.pallas_call(
         functools.partial(solve_kernel, plan, total_rows),
+        in_specs=[pl.BlockSpec(memory_space=pltpu.VMEM)] * 2,
+        out_specs=pl.BlockSpec(memory_space=pltpu.VMEM),
         out_shape=jax.ShapeDtypeStruct(((plan.per + 1) * NM, LANES), jnp.float32),
-        compiler_params=pltpu.CompilerParams(vmem_limit_bytes=VMEM_LIMIT),
+        compiler_params=pltpu.CompilerParams(vmem_limit_bytes=SOLVE_MIB * MIB),
         name="solve",
     )(packed, start)
 
 
-def modes_kernel(plan, coef_ref, near_ref, far_ref, root_ref, out_ref, energy_ref):
-    inverse_root = 1.0 / root_ref[...]
+def modes_kernel(plan, coef_ref, near_ref, far_ref, weight_ref, out_ref, energy_ref):
+    tile = out_ref.shape[2]
+    here = pl.ds(pl.multiple_of(pl.program_id(0) * tile, tile), tile)
+    inverse_root = 1.0 / jnp.sqrt(weight_ref[...])
     left = lane_index((NM, LANES)) < NB
     lane8 = lane_index((NM, LANES))
 
@@ -290,7 +297,7 @@
             factor_real = extras[:, 3 * j : 3 * j + 1]
             factor_imag = extras[:, 3 * j + 1 : 3 * j + 2]
             projected = jnp.dot(
-                matrix.astype(jnp.bfloat16), coef_ref[f], preferred_element_type=jnp.float32
+                matrix.astype(jnp.bfloat16), coef_ref[f, :, here], preferred_element_type=jnp.float32
             )
             real = projected[:NM]
             imag = projected[NM:]
@@ -308,33 +315,32 @@
             energies,
             unroll=8,
         )
-    square = jnp.concatenate([energies] + [jnp.zeros_like(energies)] * (LANES // NM - 1), axis=0)
-    energy_ref[...] = jnp.transpose(square)[:NF, :NM]
-
-
-def modes(plan, coeffs, near, far, root_weight):
+    energy_ref[...] = energies[:, :NF]
+
+
+def modes(plan, coeffs, near, far, weights):
     rows_here = coeffs.shape[2]
     tile = min(256, rows_here)
     return pl.pallas_call(
         functools.partial(modes_kernel, plan),
         grid=(rows_here // tile,),
         in_specs=[
-            pl.BlockSpec((NF, 2 * NB, tile), lambda i: (0, 0, i)),
-            pl.BlockSpec(near.shape, lambda i: (0, 0, 0)),
-            pl.BlockSpec(far.shape, lambda i: (0, 0, 0)),
+            pl.BlockSpec(memory_space=pltpu.VMEM),
+            pl.BlockSpec(memory_space=pltpu.VMEM),
+            pl.BlockSpec(memory_space=pltpu.VMEM),
             pl.BlockSpec((1, tile), lambda i: (0, i)),
         ],
         out_specs=[
             pl.BlockSpec((NF, 2 * NM, tile), lambda i: (0, 0, i)),
-            pl.BlockSpec((NF, NM), lambda i: (0, 0)),
+            pl.BlockSpec((NM, NF), lambda i: (0, 0)),
         ],
         out_shape=[
             jax.ShapeDtypeStruct((NF, 2 * NM, rows_here), jnp.float32),
-            jax.ShapeDtypeStruct((NF, NM), jnp.float32),
-        ],
-        compiler_params=pltpu.CompilerParams(vmem_limit_bytes=VMEM_LIMIT),
+            jax.ShapeDtypeStruct((NM, NF), jnp.float32),
+        ],
+        compiler_params=pltpu.CompilerParams(vmem_limit_bytes=MODES_MIB * MIB),
         name="modes",
-    )(coeffs, near, far, root_weight[None])
+    )(coeffs, near, far, weights[None])
 
 
 def swap(x, axis, size, offset):
@@ -343,13 +349,11 @@
 
 def shards(plan, snapshots, weights, reference_field, start_basis):
     total_rows = snapshots.shape[1] * plan.grp * plan.row
-    root_weight = jnp.sqrt(weights)
-    probe = (root_weight * reference_field).astype(jnp.bfloat16).astype(jnp.float32)
     start = lax.dynamic_slice_in_dim(start_basis, plan.first_freq(0, 0, 0), plan.per, 0)
     start = jnp.pad(start, ((0, 0), (0, 0), (0, NB - NBLK), (0, 0)))
     start = jnp.transpose(start, (0, 3, 1, 2)).reshape(plan.per, NM, 2 * NB)
 
-    coeffs, keep, send = transform(plan, snapshots, root_weight, probe)
+    coeffs, keep, send = transform(plan, snapshots, weights, reference_field)
 
     held = keep + swap(send, "row", plan.row, 1)
     if plan.split_grp:
@@ -371,7 +375,9 @@
         payload = jnp.concatenate(
             [payload] + [swap(payload, "grp", plan.grp, d) for d in range(1, plan.grp)]
         )
-    return tuple(modes(plan, coeffs, payload, swap(payload, "row", plan.row, 1), root_weight))
+    far = swap(payload, "row", plan.row, 1)
+    spod_modes, energies = modes(plan, coeffs, payload, far, weights)
+    return spod_modes, jnp.transpose(energies)
 
 
 def solution(mesh):

time: 90.6 us -> 90.4 us (level)
  local copies, waits for them, and re-layouts: 3.95 us -> 14.3 us
  Pallas kernels: 44.9 us -> 37.3 us
  other arithmetic: 3.85 us -> 0.13 us
  waiting for transfers between devices: 19.6 us -> 20.6 us
    unnamed x12 -> x20, local copies, waits for them, and re-layouts: 1.44 us -> 13.8 us
    pallas_call x1, Pallas kernels: 10.1 us -> 6.1 us  [modes(): pl.pallas_call(functools.partial(modes_kernel, plan), grid=(rows_here //...]
    pallas_call x1, Pallas kernels: 21.9 us -> 19.6 us  [transform(): pl.pallas_call(functools.partial(transform_kernel, plan), grid=(rows_here...]
    pallas_call x1 -> x0, local copies, waits for them, and re-layouts: 1.42 us -> none  [modes(): pl.pallas_call(functools.partial(modes_kernel, plan), grid=(rows_here //...]
    pallas_call x1, Pallas kernels: 13 us -> 11.6 us  [solve(): pl.pallas_call(functools.partial(solve_kernel, plan, total_rows), in_spec...]
    broadcast_in_dim x1 -> x0, other arithmetic: 1.37 us -> none  [transform(): probe[None]]
    add x1, other arithmetic: 1.11 us -> 0.08 us  [shards(): held = keep + swap(send, 'row', plan.row, 1)]
    ppermute x14, waiting for transfers between devices: 19.6 us -> 20.6 us  [swap(): return lax.ppermute(x, axis, [(i, i ^ offset) for i in range(size)])]
  transfers between devices with their start and end apart: 14 -> 14, of which waited for: 11 -> 11; matrix products, arithmetic and copies ran while one was open for 2% -> 1% of each run, Pallas kernels for 0% -> 0%
where the time goes in v3:
time: 90.4 us; the launch traced here: 90.1 us
  Pallas kernels  37.3 us (41%)
  waiting for transfers between devices  20.6 us (23%)
  starting transfers between devices  17.1 us (19%)
  local copies, waits for them, and re-layouts  14.3 us (16%)
    ppermute x14, waiting for transfers between devices, swap(): return lax.ppermute(x, axis, [(i, i ^ offset) for i in range(size)])  20.6 us
    pallas_call x1, Pallas kernels, transform(): pl.pallas_call(functools.partial(transform_kernel, plan), grid=(rows_here...  19.6 us
    ppermute x14, starting transfers between devices, swap(): return lax.ppermute(x, axis, [(i, i ^ offset) for i in range(size)])  17.1 us
    unnamed x20, local copies, waits for them, and re-layouts  13.8 us
    pallas_call x1, Pallas kernels, solve(): pl.pallas_call(functools.partial(solve_kernel, plan, total_rows), in_spec...  11.6 us
    pallas_call x1, Pallas kernels, modes(): pl.pallas_call(functools.partial(modes_kernel, plan), grid=(rows_here //...  6.1 us
  transfers between devices with their start and end apart: 14, of which 11 were waited for; matrix products, arithmetic and copies ran while one was open for 1% of the time, Pallas kernels for 0%

profile of v3, /device:TPU:0, one launch (start us, length us, event | category | flops | bytes accessed | tf_op | source)
XLA Modules:
  0.0 90.1 jit_solution(16704960659770889937)
XLA Ops:
  0.6 0.0 copy-start
  0.6 0.0 copy-start.3
  0.7 0.9 copy-done.3
  1.5 0.0 copy-start.4
  1.5 0.7 copy-done.4
  2.2 0.0 copy-start.6
  2.2 0.7 copy-done.6
  2.9 0.0 copy-start.5
  2.9 19.6 %transform.1 = (bf16[64,128,1024]{2,1,0:T(8,128)(2,1)S(1)}, f32[32,32,128]{2,1,0:T(8,128)S(1)}, f32[32,32,128]{2,1,0:T(8,128)S(1)}) custom-call(bf16[8192,1024]{1,0:T(8,128)(2,1)} %snap_ref.1, f32[1,1024]{1,0:T(1,128)S(1)} %bitcast.15, f32[1,1024]{1,0:T(1,128)S(1)} %bitcast.17, bf16[128,256]{1,0:T(8,128)(2,1)S(1)} %copy-done.3), custom_call_target="tpu_custom_call" | custom-call | tf_op jit(solution)/shard_map/transform/pallas_call | solution.py:137
  22.5 0.0 copy-start.1
  22.6 5.7 %copy-done.1 = bf16[64,128,1024]{2,1,0:T(8,128)(2,1)} copy-done((bf16[64,128,1024]{2,1,0:T(8,128)(2,1)}, bf16[64,128,1024]{2,1,0:T(8,128)(2,1)S(1)}, u32[]{:S(2)}) %copy-start.1) | copy-done | bytes 16777240
  28.3 0.5 collective-permute-start
  28.7 1.5 %collective-permute-done = f32[32,32,128]{2,1,0:T(8,128)S(1)} collective-permute-done((f32[32,32,128]{2,1,0:T(8,128)S(1)}, f32[32,32,128]{2,1,0:T(8,128)S(1)}, u32[]{:S(2)}, u32[]{:S(2)}) %collective-permute-start) | collective-permute-done | bytes 524320 | tf_op jit(solution)/shard_map/ppermute | solution.py:347
  30.3 0.1 add.32
  30.4 2.9 %collective-permute-start.1 = (f32[8,32,128]{2,1,0:T(8,128)S(1)}, f32[8,32,128]{2,1,0:T(8,128)S(1)}, u32[]{:S(2)}, u32[]{:S(2)}) collective-permute-start(f32[8,32,128]{2,1,0:T(8,128)S(1)} %get-tuple-element.12), channel_id=1, source_target_pairs={{0,8},{8,0},{16,24},{24,16},{1,9},{9,1},{17,25},{25,17},{2,10},{10... | collective-permute-start | bytes 393224 | tf_op jit(solution)/shard_map/ppermute | solution.py:347
  33.3 1.5 %collective-permute-start.3 = (f32[8,32,128]{2,1,0:T(8,128)S(1)}, f32[8,32,128]{2,1,0:T(8,128)S(1)}, u32[]{:S(2)}, u32[]{:S(2)}) collective-permute-start(f32[8,32,128]{2,1,0:T(8,128)S(1)} %get-tuple-element.13), channel_id=1, source_target_pairs={{0,24},{8,16},{16,8},{24,0},{1,25},{9,17},{17,9},{25,1},{2,26},{10... | collective-permute-start | bytes 393224 | tf_op jit(solution)/shard_map/ppermute | solution.py:347
  34.8 0.0 collective-permute-start.2
  34.8 2.6 %collective-permute-done.1 = f32[8,32,128]{2,1,0:T(8,128)S(1)} collective-permute-done((f32[8,32,128]{2,1,0:T(8,128)S(1)}, f32[8,32,128]{2,1,0:T(8,128)S(1)}, u32[]{:S(2)}, u32[]{:S(2)}) %collective-permute-start.1) | collective-permute-done | bytes 131104 | tf_op jit(solution)/shard_map/ppermute | solution.py:347
  37.4 3.8 %collective-permute-done.3 = f32[8,32,128]{2,1,0:T(8,128)S(1)} collective-permute-done((f32[8,32,128]{2,1,0:T(8,128)S(1)}, f32[8,32,128]{2,1,0:T(8,128)S(1)}, u32[]{:S(2)}, u32[]{:S(2)}) %collective-permute-start.3) | collective-permute-done | bytes 131104 | tf_op jit(solution)/shard_map/ppermute | solution.py:347
  41.2 1.4 %collective-permute-done.2 = f32[8,32,128]{2,1,0:T(8,128)S(1)} collective-permute-done((f32[8,32,128]{2,1,0:T(8,128)S(1)}, f32[8,32,128]{2,1,0:T(8,128)S(1)}, u32[]{:S(2)}, u32[]{:S(2)}) %collective-permute-start.2) | collective-permute-done | bytes 131104 | tf_op jit(solution)/shard_map/ppermute | solution.py:347
  42.6 1.6 %collective-permute-start.4 = (f32[2,32,128]{2,1,0:T(8,128)S(1)}, f32[2,32,128]{2,1,0:T(8,128)S(1)}, u32[]{:S(2)}, u32[]{:S(2)}) collective-permute-start(f32[2,32,128]{2,1,0:T(8,128)S(1)} %get-tuple-element.15), channel_id=1, source_target_pairs={{0,2},{1,3},{2,0},{3,1},{4,6},{5,7},{6,4},{7,5},{8,10},{9,11},{10,... | collective-permute-start | bytes 98312 | tf_op jit(solution)/shard_map/ppermute | solution.py:347
  44.3 2.4 %collective-permute-start.6 = (f32[2,32,128]{2,1,0:T(8,128)S(1)}, f32[2,32,128]{2,1,0:T(8,128)S(1)}, u32[]{:S(2)}, u32[]{:S(2)}) collective-permute-start(f32[2,32,128]{2,1,0:T(8,128)S(1)} %get-tuple-element.16), channel_id=1, source_target_pairs={{0,6},{1,7},{2,4},{3,5},{4,2},{5,3},{6,0},{7,1},{8,14},{9,15},{10,... | collective-permute-start | bytes 98312 | tf_op jit(solution)/shard_map/ppermute | solution.py:347
  46.7 0.1 collective-permute-start.5
  46.8 0.0 copy-done
  46.9 0.2 constant_dynamic-slice_fusion
  47.1 0.2 copy.8.start_ref
  47.3 0.0 collective-permute-done.4
  47.3 2.7 %collective-permute-done.6 = f32[2,32,128]{2,1,0:T(8,128)S(1)} collective-permute-done((f32[2,32,128]{2,1,0:T(8,128)S(1)}, f32[2,32,128]{2,1,0:T(8,128)S(1)}, u32[]{:S(2)}, u32[]{:S(2)}) %collective-permute-start.6) | collective-permute-done | bytes 32800 | tf_op jit(solution)/shard_map/ppermute | solution.py:347
  50.0 1.9 %collective-permute-done.5 = f32[2,32,128]{2,1,0:T(8,128)S(1)} collective-permute-done((f32[2,32,128]{2,1,0:T(8,128)S(1)}, f32[2,32,128]{2,1,0:T(8,128)S(1)}, u32[]{:S(2)}, u32[]{:S(2)}) %collective-permute-start.5) | collective-permute-done | bytes 32800 | tf_op jit(solution)/shard_map/ppermute | solution.py:347
  51.9 11.6 %solve.1 = f32[24,128]{1,0:T(8,128)S(1)} custom-call(f32[2,32,128]{2,1,0:T(8,128)S(1)} %fusion.3.packed_ref, f32[2,8,128]{2,1,0:T(8,128)S(1)} %copy.8.start_ref), custom_call_target="tpu_custom_call" | custom-call | tf_op jit(solution)/shard_map/solve/pallas_call | solution.py:273
  63.5 1.3 %collective-permute-start.9 = (f32[24,128]{1,0:T(8,128)S(1)}, f32[24,128]{1,0:T(8,128)S(1)}, u32[]{:S(2)}, u32[]{:S(2)}) collective-permute-start(f32[24,128]{1,0:T(8,128)S(1)} %solve.1), channel_id=1, source_target_pairs={{0,6},{1,7},{2,4},{3,5},{4,2},{5,3},{6,0},{7,1},{8,14},{9,15},{10,... | collective-permute-start | bytes 36872 | tf_op jit(solution)/shard_map/ppermute | solution.py:347
  64.8 0.7 collective-permute-start.8
  65.5 2.5 %collective-permute-start.7 = (f32[24,128]{1,0:T(8,128)S(1)}, f32[24,128]{1,0:T(8,128)S(1)}, u32[]{:S(2)}, u32[]{:S(2)}) collective-permute-start(f32[24,128]{1,0:T(8,128)S(1)} %solve.1), channel_id=1, source_target_pairs={{0,2},{1,3},{2,0},{3,1},{4,6},{5,7},{6,4},{7,5},{8,10},{9,11},{10,... | collective-permute-start | bytes 36872 | tf_op jit(solution)/shard_map/ppermute | solution.py:347
  68.0 1.1 %collective-permute-done.9 = f32[24,128]{1,0:T(8,128)S(1)} collective-permute-done((f32[24,128]{1,0:T(8,128)S(1)}, f32[24,128]{1,0:T(8,128)S(1)}, u32[]{:S(2)}, u32[]{:S(2)}) %collective-permute-start.9) | collective-permute-done | bytes 12320 | tf_op jit(solution)/shard_map/ppermute | solution.py:347
  69.1 0.4 collective-permute-done.8
  69.4 0.2 collective-permute-done.7
  69.6 1.5 %collective-permute-start.12 = (f32[4,24,128]{2,1,0:T(8,128)S(1)}, f32[4,24,128]{2,1,0:T(8,128)S(1)}, u32[]{:S(2)}, u32[]{:S(2)}) collective-permute-start(f32[4,24,128]{2,1,0:T(8,128)S(1)} %pad_maximum_fusion), channel_id=1, source_target_pairs={{0,24},{8,16},{16,8},{24,0},{1,25},{9,17},{17,9},{25,1},{2,26},{10... | collective-permute-start | bytes 147464 | tf_op jit(solution)/shard_map/ppermute | solution.py:347
  71.1 1.5 %collective-permute-start.11 = (f32[4,24,128]{2,1,0:T(8,128)S(1)}, f32[4,24,128]{2,1,0:T(8,128)S(1)}, u32[]{:S(2)}, u32[]{:S(2)}) collective-permute-start(f32[4,24,128]{2,1,0:T(8,128)S(1)} %pad_maximum_fusion), channel_id=1, source_target_pairs={{0,16},{8,24},{16,0},{24,8},{1,17},{9,25},{17,1},{25,9},{2,18},{10... | collective-permute-start | bytes 147464 | tf_op jit(solution)/shard_map/ppermute | solution.py:347
  72.6 0.5 collective-permute-start.10
  73.1 3.6 %collective-permute-done.10 = f32[4,24,128]{2,1,0:T(8,128)S(1)} collective-permute-done((f32[4,24,128]{2,1,0:T(8,128)S(1)}, f32[4,24,128]{2,1,0:T(8,128)S(1)}, u32[]{:S(2)}, u32[]{:S(2)}) %collective-permute-start.10) | collective-permute-done | bytes 49184 | tf_op jit(solution)/shard_map/ppermute | solution.py:347
  76.7 0.0 collective-permute-done.11
  76.7 0.0 collective-permute-done.12
  76.8 0.1 collective-permute-start.13
  76.8 1.4 %collective-permute-done.13.far_ref = f32[16,24,128]{2,1,0:T(8,128)S(1)} collective-permute-done((f32[16,24,128]{2,1,0:T(8,128)S(1)}, f32[16,24,128]{2,1,0:T(8,128)S(1)}, u32[]{:S(2)}, u32[]{:S(2)}) %collective-permute-start.13) | collective-permute-done | bytes 196640 | tf_op jit(solution)/shard_map/ppermute | solution.py:347
  78.3 0.0 copy-done.5
  78.3 0.0 copy-start.2
  78.3 5.8 %copy-done.2 = bf16[64,128,1024]{2,1,0:T(8,128)(2,1)S(1)} copy-done((bf16[64,128,1024]{2,1,0:T(8,128)(2,1)S(1)}, bf16[64,128,1024]{2,1,0:T(8,128)(2,1)}, u32[]{:S(2)}) %copy-start.2) | copy-done | bytes 16777240
  84.0 6.1 %modes.1 = (f32[64,16,1024]{2,1,0:T(8,128)}, f32[8,64]{1,0:T(8,128)}) custom-call(bf16[64,128,1024]{2,1,0:T(8,128)(2,1)S(1)} %copy-done.2, f32[16,24,128]{2,1,0:T(8,128)S(1)} %constant_dynamic-update-slice_fusion.near_ref, f32[16,24,128]{2,1,0:T(8,128)S(1)} %collective-permute-done.13.far_ref, f32[1,1024]{1,0:T(1,128)S(1)} %bitcast.16), custom_call_target="tpu_custom_call" | custom-call | tf_op jit(solution)/shard_map/modes/pallas_call | solution.py:324
  (13 shorter events, 0.2 us)
Async XLA Ops:
  0.6 46.2 %copy-start = (f32[64,2,63,8]{0,3,2,1:T(8,128)S(1)}, f32[64,2,63,8]{0,3,2,1:T(8,128)}, u32[]{:S(2)}) copy-start(f32[64,2,63,8]{0,3,2,1:T(8,128)} %param.8) | copy-start | bytes 774148
  0.6 0.9 copy-start.3
  1.5 0.7 copy-start.4
  2.2 0.7 copy-start.6
  2.9 75.4 %copy-start.5 = (f32[1024]{0:T(1024)S(1)}, f32[1024]{0:T(1024)}, u32[]{:S(2)}) copy-start(f32[1024]{0:T(1024)} %param.6) | copy-start | bytes 12292
  22.5 5.7 %copy-start.1 = (bf16[64,128,1024]{2,1,0:T(8,128)(2,1)}, bf16[64,128,1024]{2,1,0:T(8,128)(2,1)S(1)}, u32[]{:S(2)}) copy-start(bf16[64,128,1024]{2,1,0:T(8,128)(2,1)S(1)} %get-tuple-element.7.coef_ref) | copy-start | bytes 50331652
  28.3 2.0 %collective-permute-start = (f32[32,32,128]{2,1,0:T(8,128)S(1)}, f32[32,32,128]{2,1,0:T(8,128)S(1)}, u32[]{:S(2)}, u32[]{:S(2)}) collective-permute-start(f32[32,32,128]{2,1,0:T(8,128)S(1)} %get-tuple-element.9), channel_id=1, source_target_pairs={{0,1},{1,0},{2,3},{3,2},{4,5},{5,4},{6,7},{7,6},{8,9},{9,8},{10,11... | collective-permute-start | bytes 1572872 | tf_op jit(solution)/shard_map/ppermute | solution.py:347
  30.4 7.0 %collective-permute-start.1 = (f32[8,32,128]{2,1,0:T(8,128)S(1)}, f32[8,32,128]{2,1,0:T(8,128)S(1)}, u32[]{:S(2)}, u32[]{:S(2)}) collective-permute-start(f32[8,32,128]{2,1,0:T(8,128)S(1)} %get-tuple-element.12), channel_id=1, source_target_pairs={{0,8},{8,0},{16,24},{24,16},{1,9},{9,1},{17,25},{25,17},{2,10},{10... | collective-permute-start | bytes 393224 | tf_op jit(solution)/shard_map/ppermute | solution.py:347
  33.3 8.0 %collective-permute-start.3 = (f32[8,32,128]{2,1,0:T(8,128)S(1)}, f32[8,32,128]{2,1,0:T(8,128)S(1)}, u32[]{:S(2)}, u32[]{:S(2)}) collective-permute-start(f32[8,32,128]{2,1,0:T(8,128)S(1)} %get-tuple-element.13), channel_id=1, source_target_pairs={{0,24},{8,16},{16,8},{24,0},{1,25},{9,17},{17,9},{25,1},{2,26},{10... | collective-permute-start | bytes 393224 | tf_op jit(solution)/shard_map/ppermute | solution.py:347
  34.8 7.8 %collective-permute-start.2 = (f32[8,32,128]{2,1,0:T(8,128)S(1)}, f32[8,32,128]{2,1,0:T(8,128)S(1)}, u32[]{:S(2)}, u32[]{:S(2)}) collective-permute-start(f32[8,32,128]{2,1,0:T(8,128)S(1)} %get-tuple-element.14), channel_id=1, source_target_pairs={{0,16},{8,24},{16,0},{24,8},{1,17},{9,25},{17,1},{25,9},{2,18},{10... | collective-permute-start | bytes 393224 | tf_op jit(solution)/shard_map/ppermute | solution.py:347
  42.6 4.7 %collective-permute-start.4 = (f32[2,32,128]{2,1,0:T(8,128)S(1)}, f32[2,32,128]{2,1,0:T(8,128)S(1)}, u32[]{:S(2)}, u32[]{:S(2)}) collective-permute-start(f32[2,32,128]{2,1,0:T(8,128)S(1)} %get-tuple-element.15), channel_id=1, source_target_pairs={{0,2},{1,3},{2,0},{3,1},{4,6},{5,7},{6,4},{7,5},{8,10},{9,11},{10,... | collective-permute-start | bytes 98312 | tf_op jit(solution)/shard_map/ppermute | solution.py:347
  44.3 5.7 %collective-permute-start.6 = (f32[2,32,128]{2,1,0:T(8,128)S(1)}, f32[2,32,128]{2,1,0:T(8,128)S(1)}, u32[]{:S(2)}, u32[]{:S(2)}) collective-permute-start(f32[2,32,128]{2,1,0:T(8,128)S(1)} %get-tuple-element.16), channel_id=1, source_target_pairs={{0,6},{1,7},{2,4},{3,5},{4,2},{5,3},{6,0},{7,1},{8,14},{9,15},{10,... | collective-permute-start | bytes 98312 | tf_op jit(solution)/shard_map/ppermute | solution.py:347
  46.7 5.2 %collective-permute-start.5 = (f32[2,32,128]{2,1,0:T(8,128)S(1)}, f32[2,32,128]{2,1,0:T(8,128)S(1)}, u32[]{:S(2)}, u32[]{:S(2)}) collective-permute-start(f32[2,32,128]{2,1,0:T(8,128)S(1)} %get-tuple-element.17), channel_id=1, source_target_pairs={{0,4},{1,5},{2,6},{3,7},{4,0},{5,1},{6,2},{7,3},{8,12},{9,13},{10,... | collective-permute-start | bytes 98312 | tf_op jit(solution)/shard_map/ppermute | solution.py:347
  63.5 5.6 %collective-permute-start.9 = (f32[24,128]{1,0:T(8,128)S(1)}, f32[24,128]{1,0:T(8,128)S(1)}, u32[]{:S(2)}, u32[]{:S(2)}) collective-permute-start(f32[24,128]{1,0:T(8,128)S(1)} %solve.1), channel_id=1, source_target_pairs={{0,6},{1,7},{2,4},{3,5},{4,2},{5,3},{6,0},{7,1},{8,14},{9,15},{10,... | collective-permute-start | bytes 36872 | tf_op jit(solution)/shard_map/ppermute | solution.py:347
  64.8 4.6 %collective-permute-start.8 = (f32[24,128]{1,0:T(8,128)S(1)}, f32[24,128]{1,0:T(8,128)S(1)}, u32[]{:S(2)}, u32[]{:S(2)}) collective-permute-start(f32[24,128]{1,0:T(8,128)S(1)} %solve.1), channel_id=1, source_target_pairs={{0,4},{1,5},{2,6},{3,7},{4,0},{5,1},{6,2},{7,3},{8,12},{9,13},{10,... | collective-permute-start | bytes 36872 | tf_op jit(solution)/shard_map/ppermute | solution.py:347
  65.5 4.2 %collective-permute-start.7 = (f32[24,128]{1,0:T(8,128)S(1)}, f32[24,128]{1,0:T(8,128)S(1)}, u32[]{:S(2)}, u32[]{:S(2)}) collective-permute-start(f32[24,128]{1,0:T(8,128)S(1)} %solve.1), channel_id=1, source_target_pairs={{0,2},{1,3},{2,0},{3,1},{4,6},{5,7},{6,4},{7,5},{8,10},{9,11},{10,... | collective-permute-start | bytes 36872 | tf_op jit(solution)/shard_map/ppermute | solution.py:347
  69.6 7.1 %collective-permute-start.12 = (f32[4,24,128]{2,1,0:T(8,128)S(1)}, f32[4,24,128]{2,1,0:T(8,128)S(1)}, u32[]{:S(2)}, u32[]{:S(2)}) collective-permute-start(f32[4,24,128]{2,1,0:T(8,128)S(1)} %pad_maximum_fusion), channel_id=1, source_target_pairs={{0,24},{8,16},{16,8},{24,0},{1,25},{9,17},{17,9},{25,1},{2,26},{10... | collective-permute-start | bytes 147464 | tf_op jit(solution)/shard_map/ppermute | solution.py:347
  71.1 5.6 %collective-permute-start.11 = (f32[4,24,128]{2,1,0:T(8,128)S(1)}, f32[4,24,128]{2,1,0:T(8,128)S(1)}, u32[]{:S(2)}, u32[]{:S(2)}) collective-permute-start(f32[4,24,128]{2,1,0:T(8,128)S(1)} %pad_maximum_fusion), channel_id=1, source_target_pairs={{0,16},{8,24},{16,0},{24,8},{1,17},{9,25},{17,1},{25,9},{2,18},{10... | collective-permute-start | bytes 147464 | tf_op jit(solution)/shard_map/ppermute | solution.py:347
  72.6 4.1 %collective-permute-start.10 = (f32[4,24,128]{2,1,0:T(8,128)S(1)}, f32[4,24,128]{2,1,0:T(8,128)S(1)}, u32[]{:S(2)}, u32[]{:S(2)}) collective-permute-start(f32[4,24,128]{2,1,0:T(8,128)S(1)} %pad_maximum_fusion), channel_id=1, source_target_pairs={{0,8},{8,0},{16,24},{24,16},{1,9},{9,1},{17,25},{25,17},{2,10},{10... | collective-permute-start | bytes 147464 | tf_op jit(solution)/shard_map/ppermute | solution.py:347
  76.8 1.5 %collective-permute-start.13 = (f32[16,24,128]{2,1,0:T(8,128)S(1)}, f32[16,24,128]{2,1,0:T(8,128)S(1)}, u32[]{:S(2)}, u32[]{:S(2)}) collective-permute-start(f32[16,24,128]{2,1,0:T(8,128)S(1)} %constant_dynamic-update-slice_fusion.near_ref), channel_id=1, source_target_pairs={{0,1},{1,0},{2,3},{3,2},{4,5},{5,4},{6,7},{7,6},{8,9},{9,8},{10,11... | collective-permute-start | bytes 589832 | tf_op jit(solution)/shard_map/ppermute | solution.py:347
  78.3 5.8 %copy-start.2 = (bf16[64,128,1024]{2,1,0:T(8,128)(2,1)S(1)}, bf16[64,128,1024]{2,1,0:T(8,128)(2,1)}, u32[]{:S(2)}) copy-start(bf16[64,128,1024]{2,1,0:T(8,128)(2,1)} %copy-done.1) | copy-start | bytes 50331652

commit v4 on v3

--- a/solution.py
+++ b/solution.py
@@ -81,7 +81,7 @@
                 ]
         return carry
 
-    lax.fori_loop(0, NBLK, one_block, 0, unroll=21)
+    lax.fori_loop(0, NBLK, one_block, 0, unroll=63)
     for piece in range(pieces):
         probe = probe_row[:, piece * LANES : (piece + 1) * LANES]
         flip[piece, pl.ds(NB - 1, NF, stride=PITCH), :] = jnp.broadcast_to(probe, (NF, LANES))
@@ -102,20 +102,23 @@
         )
         return carry
 
-    lax.fori_loop(0, NF, one_freq, 0, unroll=16)
+    lax.fori_loop(0, NF, one_freq, 0, unroll=64)
 
     @pl.when(step == pl.num_programs(0) - 1)
     def _():
-        upper = row_index_of((NB, LANES)) < lane_index((NB, LANES))
-        left = lane_index((NB // 2, LANES)) < NB
+        row = row_index_of((NB, LANES))
+        lane = lane_index((NB, LANES))
+        left = lane < NB
+        upper = row < (lane & (NB - 1))
+        left_half = left[: NB // 2]
 
         def pack(f):
             top = gram[f, :NB, :]
             low = gram[f, NB:, :]
-            real = top + pltpu.roll(low, NB, 1)
-            imag = pltpu.roll(top, NB, 1) - low
-            packed = jnp.where(upper, imag, real)
-            return jnp.where(left, packed[: NB // 2], pltpu.roll(packed[NB // 2 :], NB, 1))
+            parts = jnp.where(left, jnp.where(upper, -low, top), jnp.where(upper, top, low))
+            first, second = parts[: NB // 2], parts[NB // 2 :]
+            other = pltpu.roll(jnp.where(left_half, second, first), NB, 1)
+            return jnp.where(left_half, first, second) + other
 
         for core_slot, out_ref in ((0, keep_ref), (1, send_ref)):
 
@@ -125,7 +128,7 @@
                     out_ref[slot * plan.per + j] = pack(first + j)
                 return carry
 
-            lax.fori_loop(0, plan.g_slots * plan.deep, one_slot, 0, unroll=4)
+            lax.fori_loop(0, plan.g_slots * plan.deep, one_slot, 0, unroll=8)
 
 
 def transform(plan, snapshots, weights, reference_field):
@@ -352,6 +355,7 @@
     start = lax.dynamic_slice_in_dim(start_basis, plan.first_freq(0, 0, 0), plan.per, 0)
     start = jnp.pad(start, ((0, 0), (0, 0), (0, NB - NBLK), (0, 0)))
     start = jnp.transpose(start, (0, 3, 1, 2)).reshape(plan.per, NM, 2 * NB)
+    snapshots, start = lax.optimization_barrier((snapshots, start))
 
     coeffs, keep, send = transform(plan, snapshots, weights, reference_field)
 

time: 90.4 us -> 74.6 us (0.83)
  local copies, waits for them, and re-layouts: 14.3 us -> 3.77 us
  Pallas kernels: 37.3 us -> 31.5 us
    unnamed x20 -> x14, local copies, waits for them, and re-layouts: 13.8 us -> 3.28 us
    pallas_call x1, Pallas kernels: 19.6 us -> 13.8 us  [transform(): pl.pallas_call(functools.partial(transform_kernel, plan), grid=(rows_here...]
  transfers between devices with their start and end apart: 14 -> 14, of which waited for: 11 -> 11; matrix products, arithmetic and copies ran while one was open for 1% -> 0% of each run, Pallas kernels for 0% -> 0%
where the time goes in v4:
time: 74.6 us; the launch traced here: 74.4 us
  Pallas kernels  31.5 us (42%)
  waiting for transfers between devices  21 us (28%)
  starting transfers between devices  17.2 us (23%)
  local copies, waits for them, and re-layouts  3.77 us (5%)
  between operations  0.75 us (1%)
    ppermute x14, waiting for transfers between devices, swap(): return lax.ppermute(x, axis, [(i, i ^ offset) for i in range(size)])  21 us
    ppermute x14, starting transfers between devices, swap(): return lax.ppermute(x, axis, [(i, i ^ offset) for i in range(size)])  17.2 us
    pallas_call x1, Pallas kernels, transform(): pl.pallas_call(functools.partial(transform_kernel, plan), grid=(rows_here...  13.8 us
    pallas_call x1, Pallas kernels, solve(): pl.pallas_call(functools.partial(solve_kernel, plan, total_rows), in_spec...  11.6 us
    pallas_call x1, Pallas kernels, modes(): pl.pallas_call(functools.partial(modes_kernel, plan), grid=(rows_here //...  6.1 us
    unnamed x14, local copies, waits for them, and re-layouts  3.28 us
  transfers between devices with their start and end apart: 14, of which 11 were waited for; matrix products, arithmetic and copies ran while one was open for 0% of the time, Pallas kernels for 0%

profile of v4, /device:TPU:0, one launch (start us, length us, event | category | flops | bytes accessed | tf_op | source)
XLA Modules:
  0.0 74.4 jit_solution(8541257326873553857)
XLA Ops:
  0.6 0.0 copy-start
  0.7 1.0 %copy-done = f32[64,2,63,8]{0,3,2,1:T(8,128)S(1)} copy-done((f32[64,2,63,8]{0,3,2,1:T(8,128)S(1)}, f32[64,2,63,8]{0,3,2,1:T(8,128)}, u32[]{:S(2)}) %copy-start) | copy-done | bytes 258072
  1.7 0.2 constant_dynamic-slice_fusion
  1.9 0.2 copy.8.start_ref
  2.1 0.0 copy-start.1
  2.1 0.9 %copy-done.1 = bf16[128,256]{1,0:T(8,128)(2,1)S(1)} copy-done((bf16[128,256]{1,0:T(8,128)(2,1)S(1)}, bf16[128,256]{1,0:T(8,128)(2,1)}, u32[]{:S(2)}) %copy-start.1) | copy-done | bytes 65560
  3.0 0.0 copy-start.2
  3.0 0.7 copy-done.2
  3.7 0.0 copy-start.3
  3.7 0.7 copy-done.3
  4.4 13.8 %transform.1 = (bf16[64,128,1024]{2,1,0:T(8,128)(2,1)S(1)}, f32[32,32,128]{2,1,0:T(8,128)S(1)}, f32[32,32,128]{2,1,0:T(8,128)S(1)}) custom-call(bf16[8192,1024]{1,0:T(8,128)(2,1)} %snap_ref, f32[1,1024]{1,0:T(1,128)S(1)} %bitcast.15, f32[1,1024]{1,0:T(1,128)S(1)} %bitcast.17, bf16[128,256]{1,0:T(8,128)(2,1)S(1)} %copy-done.1), custom_call_target="tpu_custom_call" | custom-call | tf_op jit(solution)/shard_map/transform/pallas_call | solution.py:140
  18.2 0.5 collective-permute-start
  18.7 1.5 %collective-permute-done = f32[32,32,128]{2,1,0:T(8,128)S(1)} collective-permute-done((f32[32,32,128]{2,1,0:T(8,128)S(1)}, f32[32,32,128]{2,1,0:T(8,128)S(1)}, u32[]{:S(2)}, u32[]{:S(2)}) %collective-permute-start) | collective-permute-done | bytes 524320 | tf_op jit(solution)/shard_map/ppermute | solution.py:350
  20.2 0.1 add.35
  20.4 2.9 %collective-permute-start.1 = (f32[8,32,128]{2,1,0:T(8,128)S(1)}, f32[8,32,128]{2,1,0:T(8,128)S(1)}, u32[]{:S(2)}, u32[]{:S(2)}) collective-permute-start(f32[8,32,128]{2,1,0:T(8,128)S(1)} %get-tuple-element.16), channel_id=1, source_target_pairs={{0,8},{8,0},{16,24},{24,16},{1,9},{9,1},{17,25},{25,17},{2,10},{10... | collective-permute-start | bytes 393224 | tf_op jit(solution)/shard_map/ppermute | solution.py:350
  23.3 1.5 %collective-permute-start.3 = (f32[8,32,128]{2,1,0:T(8,128)S(1)}, f32[8,32,128]{2,1,0:T(8,128)S(1)}, u32[]{:S(2)}, u32[]{:S(2)}) collective-permute-start(f32[8,32,128]{2,1,0:T(8,128)S(1)} %get-tuple-element.17), channel_id=1, source_target_pairs={{0,24},{8,16},{16,8},{24,0},{1,25},{9,17},{17,9},{25,1},{2,26},{10... | collective-permute-start | bytes 393224 | tf_op jit(solution)/shard_map/ppermute | solution.py:350
  24.8 0.1 collective-permute-start.2
  24.8 2.6 %collective-permute-done.1 = f32[8,32,128]{2,1,0:T(8,128)S(1)} collective-permute-done((f32[8,32,128]{2,1,0:T(8,128)S(1)}, f32[8,32,128]{2,1,0:T(8,128)S(1)}, u32[]{:S(2)}, u32[]{:S(2)}) %collective-permute-start.1) | collective-permute-done | bytes 131104 | tf_op jit(solution)/shard_map/ppermute | solution.py:350
  27.4 3.8 %collective-permute-done.3 = f32[8,32,128]{2,1,0:T(8,128)S(1)} collective-permute-done((f32[8,32,128]{2,1,0:T(8,128)S(1)}, f32[8,32,128]{2,1,0:T(8,128)S(1)}, u32[]{:S(2)}, u32[]{:S(2)}) %collective-permute-start.3) | collective-permute-done | bytes 131104 | tf_op jit(solution)/shard_map/ppermute | solution.py:350
  31.2 1.4 %collective-permute-done.2 = f32[8,32,128]{2,1,0:T(8,128)S(1)} collective-permute-done((f32[8,32,128]{2,1,0:T(8,128)S(1)}, f32[8,32,128]{2,1,0:T(8,128)S(1)}, u32[]{:S(2)}, u32[]{:S(2)}) %collective-permute-start.2) | collective-permute-done | bytes 131104 | tf_op jit(solution)/shard_map/ppermute | solution.py:350
  32.6 1.6 %collective-permute-start.4 = (f32[2,32,128]{2,1,0:T(8,128)S(1)}, f32[2,32,128]{2,1,0:T(8,128)S(1)}, u32[]{:S(2)}, u32[]{:S(2)}) collective-permute-start(f32[2,32,128]{2,1,0:T(8,128)S(1)} %get-tuple-element.19), channel_id=1, source_target_pairs={{0,2},{1,3},{2,0},{3,1},{4,6},{5,7},{6,4},{7,5},{8,10},{9,11},{10,... | collective-permute-start | bytes 98312 | tf_op jit(solution)/shard_map/ppermute | solution.py:350
  34.2 2.5 %collective-permute-start.6 = (f32[2,32,128]{2,1,0:T(8,128)S(1)}, f32[2,32,128]{2,1,0:T(8,128)S(1)}, u32[]{:S(2)}, u32[]{:S(2)}) collective-permute-start(f32[2,32,128]{2,1,0:T(8,128)S(1)} %get-tuple-element.20), channel_id=1, source_target_pairs={{0,6},{1,7},{2,4},{3,5},{4,2},{5,3},{6,0},{7,1},{8,14},{9,15},{10,... | collective-permute-start | bytes 98312 | tf_op jit(solution)/shard_map/ppermute | solution.py:350
  36.7 0.1 collective-permute-start.5
  36.8 0.0 collective-permute-done.4
  36.8 3.1 %collective-permute-done.6 = f32[2,32,128]{2,1,0:T(8,128)S(1)} collective-permute-done((f32[2,32,128]{2,1,0:T(8,128)S(1)}, f32[2,32,128]{2,1,0:T(8,128)S(1)}, u32[]{:S(2)}, u32[]{:S(2)}) %collective-permute-start.6) | collective-permute-done | bytes 32800 | tf_op jit(solution)/shard_map/ppermute | solution.py:350
  40.0 1.9 %collective-permute-done.5 = f32[2,32,128]{2,1,0:T(8,128)S(1)} collective-permute-done((f32[2,32,128]{2,1,0:T(8,128)S(1)}, f32[2,32,128]{2,1,0:T(8,128)S(1)}, u32[]{:S(2)}, u32[]{:S(2)}) %collective-permute-start.5) | collective-permute-done | bytes 32800 | tf_op jit(solution)/shard_map/ppermute | solution.py:350
  41.9 11.6 %solve.1 = f32[24,128]{1,0:T(8,128)S(1)} custom-call(f32[2,32,128]{2,1,0:T(8,128)S(1)} %fusion.3.packed_ref, f32[2,8,128]{2,1,0:T(8,128)S(1)} %copy.8.start_ref), custom_call_target="tpu_custom_call" | custom-call | tf_op jit(solution)/shard_map/solve/pallas_call | solution.py:276
  53.5 1.3 %collective-permute-start.9 = (f32[24,128]{1,0:T(8,128)S(1)}, f32[24,128]{1,0:T(8,128)S(1)}, u32[]{:S(2)}, u32[]{:S(2)}) collective-permute-start(f32[24,128]{1,0:T(8,128)S(1)} %solve.1), channel_id=1, source_target_pairs={{0,6},{1,7},{2,4},{3,5},{4,2},{5,3},{6,0},{7,1},{8,14},{9,15},{10,... | collective-permute-start | bytes 36872 | tf_op jit(solution)/shard_map/ppermute | solution.py:350
  54.8 0.6 collective-permute-start.8
  55.5 2.5 %collective-permute-start.7 = (f32[24,128]{1,0:T(8,128)S(1)}, f32[24,128]{1,0:T(8,128)S(1)}, u32[]{:S(2)}, u32[]{:S(2)}) collective-permute-start(f32[24,128]{1,0:T(8,128)S(1)} %solve.1), channel_id=1, source_target_pairs={{0,2},{1,3},{2,0},{3,1},{4,6},{5,7},{6,4},{7,5},{8,10},{9,11},{10,... | collective-permute-start | bytes 36872 | tf_op jit(solution)/shard_map/ppermute | solution.py:350
  58.0 1.1 %collective-permute-done.9 = f32[24,128]{1,0:T(8,128)S(1)} collective-permute-done((f32[24,128]{1,0:T(8,128)S(1)}, f32[24,128]{1,0:T(8,128)S(1)}, u32[]{:S(2)}, u32[]{:S(2)}) %collective-permute-start.9) | collective-permute-done | bytes 12320 | tf_op jit(solution)/shard_map/ppermute | solution.py:350
  59.1 0.4 collective-permute-done.8
  59.4 0.2 collective-permute-done.7
  59.7 1.4 %collective-permute-start.12 = (f32[4,24,128]{2,1,0:T(8,128)S(1)}, f32[4,24,128]{2,1,0:T(8,128)S(1)}, u32[]{:S(2)}, u32[]{:S(2)}) collective-permute-start(f32[4,24,128]{2,1,0:T(8,128)S(1)} %pad_maximum_fusion), channel_id=1, source_target_pairs={{0,24},{8,16},{16,8},{24,0},{1,25},{9,17},{17,9},{25,1},{2,26},{10... | collective-permute-start | bytes 147464 | tf_op jit(solution)/shard_map/ppermute | solution.py:350
  61.1 1.5 %collective-permute-start.11 = (f32[4,24,128]{2,1,0:T(8,128)S(1)}, f32[4,24,128]{2,1,0:T(8,128)S(1)}, u32[]{:S(2)}, u32[]{:S(2)}) collective-permute-start(f32[4,24,128]{2,1,0:T(8,128)S(1)} %pad_maximum_fusion), channel_id=1, source_target_pairs={{0,16},{8,24},{16,0},{24,8},{1,17},{9,25},{17,1},{25,9},{2,18},{10... | collective-permute-start | bytes 147464 | tf_op jit(solution)/shard_map/ppermute | solution.py:350
  62.6 0.5 collective-permute-start.10
  63.2 3.5 %collective-permute-done.10 = f32[4,24,128]{2,1,0:T(8,128)S(1)} collective-permute-done((f32[4,24,128]{2,1,0:T(8,128)S(1)}, f32[4,24,128]{2,1,0:T(8,128)S(1)}, u32[]{:S(2)}, u32[]{:S(2)}) %collective-permute-start.10) | collective-permute-done | bytes 49184 | tf_op jit(solution)/shard_map/ppermute | solution.py:350
  66.7 0.0 collective-permute-done.11
  66.7 0.0 collective-permute-done.12
  66.8 0.1 collective-permute-start.13
  66.8 1.4 %collective-permute-done.13.far_ref = f32[16,24,128]{2,1,0:T(8,128)S(1)} collective-permute-done((f32[16,24,128]{2,1,0:T(8,128)S(1)}, f32[16,24,128]{2,1,0:T(8,128)S(1)}, u32[]{:S(2)}, u32[]{:S(2)}) %collective-permute-start.13) | collective-permute-done | bytes 196640 | tf_op jit(solution)/shard_map/ppermute | solution.py:350
  68.3 6.1 %modes.1 = (f32[64,16,1024]{2,1,0:T(8,128)}, f32[8,64]{1,0:T(8,128)}) custom-call(bf16[64,128,1024]{2,1,0:T(8,128)(2,1)S(1)} %get-tuple-element.10.coef_ref, f32[16,24,128]{2,1,0:T(8,128)S(1)} %constant_dynamic-update-slice_fusion.near_ref, f32[16,24,128]{2,1,0:T(8,128)S(1)} %collective-permute-done.13.far_ref, f32[1,1024]{1,0:T(1,128)S(1)} %bitcast.16), custom_call_target="tpu_custom_call" | custom-call | tf_op jit(solution)/shard_map/modes/pallas_call | solution.py:327
  (13 shorter events, 0.2 us)
Async XLA Ops:
  0.6 1.0 %copy-start = (f32[64,2,63,8]{0,3,2,1:T(8,128)S(1)}, f32[64,2,63,8]{0,3,2,1:T(8,128)}, u32[]{:S(2)}) copy-start(f32[64,2,63,8]{0,3,2,1:T(8,128)} %param.8) | copy-start | bytes 774148
  2.1 0.9 %copy-start.1 = (bf16[128,256]{1,0:T(8,128)(2,1)S(1)}, bf16[128,256]{1,0:T(8,128)(2,1)}, u32[]{:S(2)}) copy-start(bf16[128,256]{1,0:T(8,128)(2,1)} %constant.25.table_ref) | copy-start | bytes 196612
  3.0 0.7 copy-start.2
  3.7 0.7 copy-start.3
  18.2 2.1 %collective-permute-start = (f32[32,32,128]{2,1,0:T(8,128)S(1)}, f32[32,32,128]{2,1,0:T(8,128)S(1)}, u32[]{:S(2)}, u32[]{:S(2)}) collective-permute-start(f32[32,32,128]{2,1,0:T(8,128)S(1)} %get-tuple-element.12), channel_id=1, source_target_pairs={{0,1},{1,0},{2,3},{3,2},{4,5},{5,4},{6,7},{7,6},{8,9},{9,8},{10,11... | collective-permute-start | bytes 1572872 | tf_op jit(solution)/shard_map/ppermute | solution.py:350
  20.4 7.0 %collective-permute-start.1 = (f32[8,32,128]{2,1,0:T(8,128)S(1)}, f32[8,32,128]{2,1,0:T(8,128)S(1)}, u32[]{:S(2)}, u32[]{:S(2)}) collective-permute-start(f32[8,32,128]{2,1,0:T(8,128)S(1)} %get-tuple-element.16), channel_id=1, source_target_pairs={{0,8},{8,0},{16,24},{24,16},{1,9},{9,1},{17,25},{25,17},{2,10},{10... | collective-permute-start | bytes 393224 | tf_op jit(solution)/shard_map/ppermute | solution.py:350
  23.3 7.9 %collective-permute-start.3 = (f32[8,32,128]{2,1,0:T(8,128)S(1)}, f32[8,32,128]{2,1,0:T(8,128)S(1)}, u32[]{:S(2)}, u32[]{:S(2)}) collective-permute-start(f32[8,32,128]{2,1,0:T(8,128)S(1)} %get-tuple-element.17), channel_id=1, source_target_pairs={{0,24},{8,16},{16,8},{24,0},{1,25},{9,17},{17,9},{25,1},{2,26},{10... | collective-permute-start | bytes 393224 | tf_op jit(solution)/shard_map/ppermute | solution.py:350
  24.8 7.8 %collective-permute-start.2 = (f32[8,32,128]{2,1,0:T(8,128)S(1)}, f32[8,32,128]{2,1,0:T(8,128)S(1)}, u32[]{:S(2)}, u32[]{:S(2)}) collective-permute-start(f32[8,32,128]{2,1,0:T(8,128)S(1)} %get-tuple-element.18), channel_id=1, source_target_pairs={{0,16},{8,24},{16,0},{24,8},{1,17},{9,25},{17,1},{25,9},{2,18},{10... | collective-permute-start | bytes 393224 | tf_op jit(solution)/shard_map/ppermute | solution.py:350
  32.6 4.2 %collective-permute-start.4 = (f32[2,32,128]{2,1,0:T(8,128)S(1)}, f32[2,32,128]{2,1,0:T(8,128)S(1)}, u32[]{:S(2)}, u32[]{:S(2)}) collective-permute-start(f32[2,32,128]{2,1,0:T(8,128)S(1)} %get-tuple-element.19), channel_id=1, source_target_pairs={{0,2},{1,3},{2,0},{3,1},{4,6},{5,7},{6,4},{7,5},{8,10},{9,11},{10,... | collective-permute-start | bytes 98312 | tf_op jit(solution)/shard_map/ppermute | solution.py:350
  34.2 5.7 %collective-permute-start.6 = (f32[2,32,128]{2,1,0:T(8,128)S(1)}, f32[2,32,128]{2,1,0:T(8,128)S(1)}, u32[]{:S(2)}, u32[]{:S(2)}) collective-permute-start(f32[2,32,128]{2,1,0:T(8,128)S(1)} %get-tuple-element.20), channel_id=1, source_target_pairs={{0,6},{1,7},{2,4},{3,5},{4,2},{5,3},{6,0},{7,1},{8,14},{9,15},{10,... | collective-permute-start | bytes 98312 | tf_op jit(solution)/shard_map/ppermute | solution.py:350
  36.7 5.2 %collective-permute-start.5 = (f32[2,32,128]{2,1,0:T(8,128)S(1)}, f32[2,32,128]{2,1,0:T(8,128)S(1)}, u32[]{:S(2)}, u32[]{:S(2)}) collective-permute-start(f32[2,32,128]{2,1,0:T(8,128)S(1)} %get-tuple-element.21), channel_id=1, source_target_pairs={{0,4},{1,5},{2,6},{3,7},{4,0},{5,1},{6,2},{7,3},{8,12},{9,13},{10,... | collective-permute-start | bytes 98312 | tf_op jit(solution)/shard_map/ppermute | solution.py:350
  53.5 5.6 %collective-permute-start.9 = (f32[24,128]{1,0:T(8,128)S(1)}, f32[24,128]{1,0:T(8,128)S(1)}, u32[]{:S(2)}, u32[]{:S(2)}) collective-permute-start(f32[24,128]{1,0:T(8,128)S(1)} %solve.1), channel_id=1, source_target_pairs={{0,6},{1,7},{2,4},{3,5},{4,2},{5,3},{6,0},{7,1},{8,14},{9,15},{10,... | collective-permute-start | bytes 36872 | tf_op jit(solution)/shard_map/ppermute | solution.py:350
  54.8 4.6 %collective-permute-start.8 = (f32[24,128]{1,0:T(8,128)S(1)}, f32[24,128]{1,0:T(8,128)S(1)}, u32[]{:S(2)}, u32[]{:S(2)}) collective-permute-start(f32[24,128]{1,0:T(8,128)S(1)} %solve.1), channel_id=1, source_target_pairs={{0,4},{1,5},{2,6},{3,7},{4,0},{5,1},{6,2},{7,3},{8,12},{9,13},{10,... | collective-permute-start | bytes 36872 | tf_op jit(solution)/shard_map/ppermute | solution.py:350
  55.5 4.2 %collective-permute-start.7 = (f32[24,128]{1,0:T(8,128)S(1)}, f32[24,128]{1,0:T(8,128)S(1)}, u32[]{:S(2)}, u32[]{:S(2)}) collective-permute-start(f32[24,128]{1,0:T(8,128)S(1)} %solve.1), channel_id=1, source_target_pairs={{0,2},{1,3},{2,0},{3,1},{4,6},{5,7},{6,4},{7,5},{8,10},{9,11},{10,... | collective-permute-start | bytes 36872 | tf_op jit(solution)/shard_map/ppermute | solution.py:350
  59.7 7.1 %collective-permute-start.12 = (f32[4,24,128]{2,1,0:T(8,128)S(1)}, f32[4,24,128]{2,1,0:T(8,128)S(1)}, u32[]{:S(2)}, u32[]{:S(2)}) collective-permute-start(f32[4,24,128]{2,1,0:T(8,128)S(1)} %pad_maximum_fusion), channel_id=1, source_target_pairs={{0,24},{8,16},{16,8},{24,0},{1,25},{9,17},{17,9},{25,1},{2,26},{10... | collective-permute-start | bytes 147464 | tf_op jit(solution)/shard_map/ppermute | solution.py:350
  61.1 5.6 %collective-permute-start.11 = (f32[4,24,128]{2,1,0:T(8,128)S(1)}, f32[4,24,128]{2,1,0:T(8,128)S(1)}, u32[]{:S(2)}, u32[]{:S(2)}) collective-permute-start(f32[4,24,128]{2,1,0:T(8,128)S(1)} %pad_maximum_fusion), channel_id=1, source_target_pairs={{0,16},{8,24},{16,0},{24,8},{1,17},{9,25},{17,1},{25,9},{2,18},{10... | collective-permute-start | bytes 147464 | tf_op jit(solution)/shard_map/ppermute | solution.py:350
  62.6 4.1 %collective-permute-start.10 = (f32[4,24,128]{2,1,0:T(8,128)S(1)}, f32[4,24,128]{2,1,0:T(8,128)S(1)}, u32[]{:S(2)}, u32[]{:S(2)}) collective-permute-start(f32[4,24,128]{2,1,0:T(8,128)S(1)} %pad_maximum_fusion), channel_id=1, source_target_pairs={{0,8},{8,0},{16,24},{24,16},{1,9},{9,1},{17,25},{25,17},{2,10},{10... | collective-permute-start | bytes 147464 | tf_op jit(solution)/shard_map/ppermute | solution.py:350
  66.8 1.5 %collective-permute-start.13 = (f32[16,24,128]{2,1,0:T(8,128)S(1)}, f32[16,24,128]{2,1,0:T(8,128)S(1)}, u32[]{:S(2)}, u32[]{:S(2)}) collective-permute-start(f32[16,24,128]{2,1,0:T(8,128)S(1)} %constant_dynamic-update-slice_fusion.near_ref), channel_id=1, source_target_pairs={{0,1},{1,0},{2,3},{3,2},{4,5},{5,4},{6,7},{7,6},{8,9},{9,8},{10,11... | collective-permute-start | bytes 589832 | tf_op jit(solution)/shard_map/ppermute | solution.py:350

commit v5 on v4

--- a/solution.py
+++ b/solution.py
@@ -17,10 +17,12 @@
 NM = 8
 ITERS = 12
 EPS = 1e-06
+LEAST_LEFT = 1e-03
 LANES = 128
 PITCH = 2 * NB + 1
 MIB = 1024 * 1024
 TRANSFORM_MIB, SOLVE_MIB, MODES_MIB = 28, 8, 8
+MODES_FREQS = 8
 
 
 def dft_table():
@@ -52,6 +54,14 @@
         if self.split_grp:
             owner = (lax.axis_index("grp") ^ grp_slot) * self.row + owner
         return owner * self.per
+
+    def slot_of(self, f):
+        owner = f // self.per
+        row_index = lax.axis_index("row")
+        slot = ((owner % self.row) ^ row_index) >> 1
+        if self.split_grp:
+            slot = ((owner // self.row) ^ lax.axis_index("grp")) * self.deep + slot
+        return slot, ((owner ^ row_index) & 1) == 0
 
 
 def lane_index(shape):
@@ -173,17 +183,75 @@
     return high, middle, low
 
 
-def solve_kernel(plan, total_rows, packed_ref, start_ref, out_ref):
+def turn(y):
+    swapped = pltpu.roll(y, NB, 1)
+    return jnp.where(lane_index(y.shape) < NB, -swapped, swapped)
+
+
+def lane_sum(x):
+    return jnp.broadcast_to(jnp.sum(x, axis=1, keepdims=True), x.shape)
+
+
+def spread(x, j):
+    return jnp.broadcast_to(x[j : j + 1], x.shape)
+
+
+def orthonormalize_checked(y, turned):
+    row = row_index_of(y.shape)
+    v = jnp.zeros_like(y)
+    for j in range(NM):
+        pivot, pivot_turned = spread(y, j), spread(turned, j)
+        size = lane_sum(pivot * pivot) + EPS
+        v = jnp.where(row == j, pivot * lax.rsqrt(size), v)
+        if j < NM - 1:
+            inverse = 1.0 / size
+            a = jnp.where(row > j, lane_sum(pivot * y) * inverse, 0.0)
+            c = jnp.where(row > j, lane_sum(pivot_turned * y) * inverse, 0.0)
+            y, turned = (
+                y - (a * pivot + c * pivot_turned),
+                turned - (a * pivot_turned - c * pivot),
+            )
+    return v
+
+
+def orthonormalize_quick(y, turned, worst):
+    row = row_index_of(y.shape)
+    real = [lane_sum(spread(y, j) * y) for j in range(NM)]
+    imag = [lane_sum(spread(turned, j) * y) for j in range(NM - 1)]
+    whole = [spread(real[j], j) + EPS for j in range(NM)]
+    v = jnp.zeros_like(y)
+    for j in range(NM):
+        pivot, pivot_turned = spread(y, j), spread(turned, j)
+        size = jnp.maximum(spread(real[j], j), 0.0) + EPS
+        worst = jnp.minimum(worst, size / whole[j])
+        v = jnp.where(row == j, pivot * lax.rsqrt(size), v)
+        if j < NM - 1:
+            inverse = 1.0 / size
+            scale = (size + EPS) * inverse * inverse
+            scaled_real, scaled_imag = real[j] * scale, imag[j] * scale
+            for l in range(j + 1, NM):
+                other_real, other_imag = spread(real[j], l), spread(imag[j], l)
+                real[l] = real[l] - (scaled_real * other_real + scaled_imag * other_imag)
+                if l < NM - 1:
+                    imag[l] = imag[l] - (scaled_imag * other_real - scaled_real * other_imag)
+            a = jnp.where(row > j, real[j] * inverse, 0.0)
+            c = jnp.where(row > j, imag[j] * inverse, 0.0)
+            y, turned = (
+                y - (a * pivot + c * pivot_turned),
+                turned - (a * pivot_turned - c * pivot),
+            )
+    return v, worst
+
+
+def solve_kernel(plan, total_rows, packed_ref, start_ref, out_ref, basis_ref):
     lane = lane_index((NB, LANES))
     row = row_index_of((NB, LANES))
     col = lane & (NB - 1)
     left = lane < NB
     inside = (row < NBLK) & (col < NBLK)
     lane8 = lane_index((NM, LANES))
-    row8 = row_index_of((NM, LANES))
-    left8 = lane8 < NB
-
-    systems, probes, basis = [], [], []
+
+    systems, probes = [], []
     for i in range(plan.per):
         folded = packed_ref[i]
         turned = pltpu.roll(folded, NB, 1)
@@ -193,22 +261,26 @@
         real = jnp.where(inside, jnp.where(row >= col, twice, flipped), 0.0) / total_rows
         imag = jnp.where(row < col, twice, jnp.where(row > col, -flipped, 0.0))
         imag = jnp.where(inside, imag, 0.0) / total_rows
-        system = jnp.concatenate([jnp.where(left, real, -imag), jnp.where(left, imag, real)], axis=0)
-        high, middle, low = split_three(system)
-        systems.append(
-            jnp.concatenate(
-                [
-                    jnp.concatenate([high, low], axis=1),
-                    jnp.concatenate([middle, jnp.zeros_like(low)], axis=1),
-                ],
-                axis=0,
+        straight = jnp.concatenate(
+            [jnp.where(left, real, -imag), jnp.where(left, imag, real)], axis=0
+        )
+        sides = []
+        for system in (straight, turn(straight)):
+            high, middle, low = split_three(system)
+            sides.append(
+                jnp.concatenate(
+                    [
+                        jnp.concatenate([high, low], axis=1),
+                        jnp.concatenate([middle, jnp.zeros_like(low)], axis=1),
+                    ],
+                    axis=0,
+                )
             )
-        )
+        systems.append(jnp.concatenate(sides, axis=1))
         along = twice[NB - 1 :]
         across = flipped[NB - 1 :]
         left1 = lane_index((1, LANES)) < NB
         probes.append((jnp.where(left1, along, across), jnp.where(left1, -across, along)))
-        basis.append(start_ref[i])
 
     def image_of(i, v):
         high, middle, low = split_three(v)
@@ -223,43 +295,44 @@
             axis=0,
         )
         out = jnp.dot(parts, systems[i], preferred_element_type=jnp.float32)
-        small = out[:NM, LANES:] + out[2 * NM : 3 * NM, :LANES]
-        return out[:NM, :LANES] + (out[NM : 2 * NM, :LANES] + small)
-
-    def lane_sum(x):
-        return jnp.sum(x, axis=1, keepdims=True)
-
-    def orthonormalize(y):
-        swapped = pltpu.roll(y, NB, 1)
-        turned = jnp.where(left8, -swapped, swapped)
-        v = jnp.zeros_like(y)
-        for j in range(NM):
-            pivot = jnp.broadcast_to(y[j : j + 1], y.shape)
-            pivot_turned = jnp.broadcast_to(turned[j : j + 1], y.shape)
-            size = lane_sum(pivot * pivot) + EPS
-            v = jnp.where(row8 == j, pivot * lax.rsqrt(size), v)
-            if j < NM - 1:
-                inner_real = lane_sum(pivot * y)
-                inner_imag = lane_sum(pivot_turned * y)
-                inverse = 1.0 / size
-                later = row8 > j
-                a = jnp.where(later, inner_real * inverse, 0.0)
-                c = jnp.where(later, inner_imag * inverse, 0.0)
-                y, turned = (
-                    y - (a * pivot + c * pivot_turned),
-                    turned - (a * pivot_turned - c * pivot),
-                )
-        return v
-
-    def sweep(index, current):
+
+        def total(out):
+            small = out[:NM, LANES:] + out[2 * NM : 3 * NM, :LANES]
+            return out[:NM, :LANES] + (out[NM : 2 * NM, :LANES] + small)
+
+        return total(out[:, : 2 * LANES]), total(out[:, 2 * LANES :])
+
+    start = tuple(start_ref[i] for i in range(plan.per))
+
+    def quick_sweep(index, carry):
+        current, worst = carry
         images = [image_of(i, v) for i, v in enumerate(current)]
-        return tuple(orthonormalize(y) for y in images)
-
-    basis = lax.fori_loop(0, ITERS, sweep, tuple(basis))
+        done = []
+        for y, turned in images:
+            v, worst = orthonormalize_quick(y, turned, worst)
+            done.append(v)
+        return tuple(done), worst
+
+    def checked_sweep(index, current):
+        images = [image_of(i, v) for i, v in enumerate(current)]
+        return tuple(orthonormalize_checked(y, turned) for y, turned in images)
+
+    basis, worst = lax.fori_loop(
+        0, ITERS, quick_sweep, (start, jnp.ones((NM, LANES), jnp.float32))
+    )
+    for i, v in enumerate(basis):
+        basis_ref[i] = v
+
+    @pl.when(jnp.logical_not(jnp.min(worst) >= LEAST_LEFT))
+    def _():
+        for i, v in enumerate(lax.fori_loop(0, ITERS, checked_sweep, start)):
+            basis_ref[i] = v
+
     extras = jnp.zeros((NM, LANES), jnp.float32)
     scale = 1.0 / math.sqrt(total_rows)
-    for i, v in enumerate(basis):
-        energy = lane_sum(v * image_of(i, v))
+    for i in range(plan.per):
+        v = basis_ref[i]
+        energy = lane_sum(v * image_of(i, v)[0])
         coef = v.astype(jnp.bfloat16).astype(jnp.float32)
         out_ref[i * NM : (i + 1) * NM] = coef
         gain = 1.0 / jnp.sqrt(energy + EPS)
@@ -278,68 +351,59 @@
         in_specs=[pl.BlockSpec(memory_space=pltpu.VMEM)] * 2,
         out_specs=pl.BlockSpec(memory_space=pltpu.VMEM),
         out_shape=jax.ShapeDtypeStruct(((plan.per + 1) * NM, LANES), jnp.float32),
+        scratch_shapes=[pltpu.VMEM((plan.per, NM, LANES), jnp.float32)],
         compiler_params=pltpu.CompilerParams(vmem_limit_bytes=SOLVE_MIB * MIB),
         name="solve",
     )(packed, start)
 
 
-def modes_kernel(plan, coef_ref, near_ref, far_ref, weight_ref, out_ref, energy_ref):
-    tile = out_ref.shape[2]
-    here = pl.ds(pl.multiple_of(pl.program_id(0) * tile, tile), tile)
+def modes_kernel(plan, coef_ref, near_ref, far_ref, weight_ref, out_hbm, energy_ref, out, sems):
     inverse_root = 1.0 / jnp.sqrt(weight_ref[...])
-    left = lane_index((NM, LANES)) < NB
     lane8 = lane_index((NM, LANES))
-
-    def one_slot(core_slot, pay_ref, slot, energies):
-        first = plan.first_freq(core_slot, slot // plan.deep, slot % plan.deep)
-        for j in range(plan.per):
-            f = first + j
-            c = pay_ref[slot, j * NM : (j + 1) * NM, :]
-            matrix = jnp.concatenate([jnp.where(left, c, -c), pltpu.roll(c, NB, 1)], axis=0)
-            extras = pay_ref[slot, plan.per * NM :, :]
-            factor_real = extras[:, 3 * j : 3 * j + 1]
-            factor_imag = extras[:, 3 * j + 1 : 3 * j + 2]
-            projected = jnp.dot(
-                matrix.astype(jnp.bfloat16), coef_ref[f, :, here], preferred_element_type=jnp.float32
-            )
-            real = projected[:NM]
-            imag = projected[NM:]
-            out_ref[f, :NM, :] = (real * factor_real - imag * factor_imag) * inverse_root
-            out_ref[f, NM:, :] = (real * factor_imag + imag * factor_real) * inverse_root
-            energies = jnp.where(lane8 == f, extras[:, 3 * j + 2 : 3 * j + 3], energies)
-        return energies
-
+    left = lane8 < NB
     energies = jnp.zeros((NM, LANES), jnp.float32)
-    for core_slot, pay_ref in ((0, near_ref), (1, far_ref)):
-        energies = lax.fori_loop(
-            0,
-            plan.g_slots * plan.deep,
-            functools.partial(one_slot, core_slot, pay_ref),
-            energies,
-            unroll=8,
-        )
+    copies = []
+    for f in range(NF):
+        slot, same_core = plan.slot_of(f)
+        packed = jnp.where(same_core, near_ref[slot], far_ref[slot])
+        j = f % plan.per
+        c = packed[j * NM : (j + 1) * NM]
+        extras = packed[plan.per * NM :]
+        factor_real = extras[:, 3 * j : 3 * j + 1]
+        factor_imag = extras[:, 3 * j + 1 : 3 * j + 2]
+        matrix = jnp.concatenate([jnp.where(left, c, -c), pltpu.roll(c, NB, 1)], axis=0)
+        projected = jnp.dot(
+            matrix.astype(jnp.bfloat16), coef_ref[f], preferred_element_type=jnp.float32
+        )
+        real = projected[:NM]
+        imag = projected[NM:]
+        out[f, :NM, :] = (real * factor_real - imag * factor_imag) * inverse_root
+        out[f, NM:, :] = (real * factor_imag + imag * factor_real) * inverse_root
+        energies = jnp.where(lane8 == f, extras[:, 3 * j + 2 : 3 * j + 3], energies)
+        if (f + 1) % MODES_FREQS == 0:
+            done = pl.ds(f + 1 - MODES_FREQS, MODES_FREQS)
+            copy = pltpu.make_async_copy(out.at[done], out_hbm.at[done], sems.at[len(copies)])
+            copy.start()
+            copies.append(copy)
     energy_ref[...] = energies[:, :NF]
+    for copy in copies:
+        copy.wait()
 
 
 def modes(plan, coeffs, near, far, weights):
     rows_here = coeffs.shape[2]
-    tile = min(256, rows_here)
+    whole = jax.ShapeDtypeStruct((NF, 2 * NM, rows_here), jnp.float32)
     return pl.pallas_call(
         functools.partial(modes_kernel, plan),
-        grid=(rows_here // tile,),
-        in_specs=[
+        in_specs=[pl.BlockSpec(memory_space=pltpu.VMEM)] * 4,
+        out_specs=[
+            pl.BlockSpec(memory_space=pltpu.HBM),
             pl.BlockSpec(memory_space=pltpu.VMEM),
-            pl.BlockSpec(memory_space=pltpu.VMEM),
-            pl.BlockSpec(memory_space=pltpu.VMEM),
-            pl.BlockSpec((1, tile), lambda i: (0, i)),
-        ],
-        out_specs=[
-            pl.BlockSpec((NF, 2 * NM, tile), lambda i: (0, 0, i)),
-            pl.BlockSpec((NM, NF), lambda i: (0, 0)),
-        ],
-        out_shape=[
-            jax.ShapeDtypeStruct((NF, 2 * NM, rows_here), jnp.float32),
-            jax.ShapeDtypeStruct((NM, NF), jnp.float32),
+        ],
+        out_shape=[whole, jax.ShapeDtypeStruct((NM, NF), jnp.float32)],
+        scratch_shapes=[
+            pltpu.VMEM(whole.shape, whole.dtype),
+            pltpu.SemaphoreType.DMA((NF // MODES_FREQS,)),
         ],
         compiler_params=pltpu.CompilerParams(vmem_limit_bytes=MODES_MIB * MIB),
         name="modes",

time: 74.6 us -> 66.5 us (0.89)
  Pallas kernels: 31.5 us -> 23.4 us
    pallas_call x1, Pallas kernels: 11.6 us -> 5.69 us  [solve(): pl.pallas_call(functools.partial(solve_kernel, plan, total_rows), in_spec...]
    pallas_call x1, Pallas kernels: 6.1 us -> 3.88 us  [modes(): pl.pallas_call(functools.partial(modes_kernel, plan), in_specs=[pl.BlockS...]
where the time goes in v5:
time: 66.5 us; the launch traced here: 66.2 us
  Pallas kernels  23.4 us (35%)
  waiting for transfers between devices  21 us (32%)
  starting transfers between devices  17.2 us (26%)
  local copies, waits for them, and re-layouts  3.77 us (6%)
  between operations  0.75 us (1%)
    ppermute x14, waiting for transfers between devices, swap(): return lax.ppermute(x, axis, [(i, i ^ offset) for i in range(size)])  21 us
    ppermute x14, starting transfers between devices, swap(): return lax.ppermute(x, axis, [(i, i ^ offset) for i in range(size)])  17.2 us
    pallas_call x1, Pallas kernels, transform(): pl.pallas_call(functools.partial(transform_kernel, plan), grid=(rows_here...  13.8 us
    pallas_call x1, Pallas kernels, solve(): pl.pallas_call(functools.partial(solve_kernel, plan, total_rows), in_spec...  5.69 us
    pallas_call x1, Pallas kernels, modes(): pl.pallas_call(functools.partial(modes_kernel, plan), in_specs=[pl.BlockS...  3.88 us
    unnamed x14, local copies, waits for them, and re-layouts  3.28 us
  transfers between devices with their start and end apart: 14, of which 11 were waited for; matrix products, arithmetic and copies ran while one was open for 0% of the time, Pallas kernels for 0%

profile of v5, /device:TPU:0, one launch (start us, length us, event | category | flops | bytes accessed | tf_op | source)
XLA Modules:
  0.0 66.2 jit_solution(18345793491397090136)
XLA Ops:
  0.6 0.0 copy-start
  0.7 1.0 %copy-done = f32[64,2,63,8]{0,3,2,1:T(8,128)S(1)} copy-done((f32[64,2,63,8]{0,3,2,1:T(8,128)S(1)}, f32[64,2,63,8]{0,3,2,1:T(8,128)}, u32[]{:S(2)}) %copy-start) | copy-done | bytes 258072
  1.7 0.2 constant_dynamic-slice_fusion
  1.9 0.2 copy.8.start_ref
  2.1 0.0 copy-start.1
  2.1 0.9 %copy-done.1 = bf16[128,256]{1,0:T(8,128)(2,1)S(1)} copy-done((bf16[128,256]{1,0:T(8,128)(2,1)S(1)}, bf16[128,256]{1,0:T(8,128)(2,1)}, u32[]{:S(2)}) %copy-start.1) | copy-done | bytes 65560
  3.0 0.0 copy-start.2
  3.0 0.7 %copy-done.2 = f32[1024]{0:T(1024)S(1)} copy-done((f32[1024]{0:T(1024)S(1)}, f32[1024]{0:T(1024)}, u32[]{:S(2)}) %copy-start.2) | copy-done | bytes 4120
  3.7 0.0 copy-start.3
  3.7 0.7 %copy-done.3 = f32[1024]{0:T(1024)S(1)} copy-done((f32[1024]{0:T(1024)S(1)}, f32[1024]{0:T(1024)}, u32[]{:S(2)}) %copy-start.3) | copy-done | bytes 4120
  4.4 13.8 %transform.1 = (bf16[64,128,1024]{2,1,0:T(8,128)(2,1)S(1)}, f32[32,32,128]{2,1,0:T(8,128)S(1)}, f32[32,32,128]{2,1,0:T(8,128)S(1)}) custom-call(bf16[8192,1024]{1,0:T(8,128)(2,1)} %snap_ref, f32[1,1024]{1,0:T(1,128)S(1)} %bitcast.15, f32[1,1024]{1,0:T(1,128)S(1)} %bitcast.17, bf16[128,256]{1,0:T(8,128)(2,1)S(1)} %copy-done.1), custom_call_target="tpu_custom_call" | custom-call | tf_op jit(solution)/shard_map/transform/pallas_call | solution.py:150
  18.2 0.5 collective-permute-start
  18.7 1.5 %collective-permute-done = f32[32,32,128]{2,1,0:T(8,128)S(1)} collective-permute-done((f32[32,32,128]{2,1,0:T(8,128)S(1)}, f32[32,32,128]{2,1,0:T(8,128)S(1)}, u32[]{:S(2)}, u32[]{:S(2)}) %collective-permute-start) | collective-permute-done | bytes 524320 | tf_op jit(solution)/shard_map/ppermute | solution.py:414
  20.2 0.1 add.35
  20.4 2.9 %collective-permute-start.1 = (f32[8,32,128]{2,1,0:T(8,128)S(1)}, f32[8,32,128]{2,1,0:T(8,128)S(1)}, u32[]{:S(2)}, u32[]{:S(2)}) collective-permute-start(f32[8,32,128]{2,1,0:T(8,128)S(1)} %get-tuple-element.16), channel_id=1, source_target_pairs={{0,8},{8,0},{16,24},{24,16},{1,9},{9,1},{17,25},{25,17},{2,10},{10... | collective-permute-start | bytes 393224 | tf_op jit(solution)/shard_map/ppermute | solution.py:414
  23.3 1.5 %collective-permute-start.3 = (f32[8,32,128]{2,1,0:T(8,128)S(1)}, f32[8,32,128]{2,1,0:T(8,128)S(1)}, u32[]{:S(2)}, u32[]{:S(2)}) collective-permute-start(f32[8,32,128]{2,1,0:T(8,128)S(1)} %get-tuple-element.17), channel_id=1, source_target_pairs={{0,24},{8,16},{16,8},{24,0},{1,25},{9,17},{17,9},{25,1},{2,26},{10... | collective-permute-start | bytes 393224 | tf_op jit(solution)/shard_map/ppermute | solution.py:414
  24.8 0.1 collective-permute-start.2
  24.8 2.6 %collective-permute-done.1 = f32[8,32,128]{2,1,0:T(8,128)S(1)} collective-permute-done((f32[8,32,128]{2,1,0:T(8,128)S(1)}, f32[8,32,128]{2,1,0:T(8,128)S(1)}, u32[]{:S(2)}, u32[]{:S(2)}) %collective-permute-start.1) | collective-permute-done | bytes 131104 | tf_op jit(solution)/shard_map/ppermute | solution.py:414
  27.4 3.8 %collective-permute-done.3 = f32[8,32,128]{2,1,0:T(8,128)S(1)} collective-permute-done((f32[8,32,128]{2,1,0:T(8,128)S(1)}, f32[8,32,128]{2,1,0:T(8,128)S(1)}, u32[]{:S(2)}, u32[]{:S(2)}) %collective-permute-start.3) | collective-permute-done | bytes 131104 | tf_op jit(solution)/shard_map/ppermute | solution.py:414
  31.2 1.4 %collective-permute-done.2 = f32[8,32,128]{2,1,0:T(8,128)S(1)} collective-permute-done((f32[8,32,128]{2,1,0:T(8,128)S(1)}, f32[8,32,128]{2,1,0:T(8,128)S(1)}, u32[]{:S(2)}, u32[]{:S(2)}) %collective-permute-start.2) | collective-permute-done | bytes 131104 | tf_op jit(solution)/shard_map/ppermute | solution.py:414
  32.6 1.6 %collective-permute-start.4 = (f32[2,32,128]{2,1,0:T(8,128)S(1)}, f32[2,32,128]{2,1,0:T(8,128)S(1)}, u32[]{:S(2)}, u32[]{:S(2)}) collective-permute-start(f32[2,32,128]{2,1,0:T(8,128)S(1)} %get-tuple-element.19), channel_id=1, source_target_pairs={{0,2},{1,3},{2,0},{3,1},{4,6},{5,7},{6,4},{7,5},{8,10},{9,11},{10,... | collective-permute-start | bytes 98312 | tf_op jit(solution)/shard_map/ppermute | solution.py:414
  34.2 2.5 %collective-permute-start.6 = (f32[2,32,128]{2,1,0:T(8,128)S(1)}, f32[2,32,128]{2,1,0:T(8,128)S(1)}, u32[]{:S(2)}, u32[]{:S(2)}) collective-permute-start(f32[2,32,128]{2,1,0:T(8,128)S(1)} %get-tuple-element.20), channel_id=1, source_target_pairs={{0,6},{1,7},{2,4},{3,5},{4,2},{5,3},{6,0},{7,1},{8,14},{9,15},{10,... | collective-permute-start | bytes 98312 | tf_op jit(solution)/shard_map/ppermute | solution.py:414
  36.7 0.1 collective-permute-start.5
  36.8 0.0 collective-permute-done.4
  36.8 3.1 %collective-permute-done.6 = f32[2,32,128]{2,1,0:T(8,128)S(1)} collective-permute-done((f32[2,32,128]{2,1,0:T(8,128)S(1)}, f32[2,32,128]{2,1,0:T(8,128)S(1)}, u32[]{:S(2)}, u32[]{:S(2)}) %collective-permute-start.6) | collective-permute-done | bytes 32800 | tf_op jit(solution)/shard_map/ppermute | solution.py:414
  40.0 1.9 %collective-permute-done.5 = f32[2,32,128]{2,1,0:T(8,128)S(1)} collective-permute-done((f32[2,32,128]{2,1,0:T(8,128)S(1)}, f32[2,32,128]{2,1,0:T(8,128)S(1)}, u32[]{:S(2)}, u32[]{:S(2)}) %collective-permute-start.5) | collective-permute-done | bytes 32800 | tf_op jit(solution)/shard_map/ppermute | solution.py:414
  41.9 5.7 %solve.1 = f32[24,128]{1,0:T(8,128)S(1)} custom-call(f32[2,32,128]{2,1,0:T(8,128)S(1)} %fusion.3.packed_ref, f32[2,8,128]{2,1,0:T(8,128)S(1)} %copy.8.start_ref), custom_call_target="tpu_custom_call" | custom-call | tf_op jit(solution)/shard_map/solve/pallas_call | solution.py:349
  47.6 1.3 %collective-permute-start.9 = (f32[24,128]{1,0:T(8,128)S(1)}, f32[24,128]{1,0:T(8,128)S(1)}, u32[]{:S(2)}, u32[]{:S(2)}) collective-permute-start(f32[24,128]{1,0:T(8,128)S(1)} %solve.1), channel_id=1, source_target_pairs={{0,6},{1,7},{2,4},{3,5},{4,2},{5,3},{6,0},{7,1},{8,14},{9,15},{10,... | collective-permute-start | bytes 36872 | tf_op jit(solution)/shard_map/ppermute | solution.py:414
  48.9 0.6 collective-permute-start.8
  49.6 2.5 %collective-permute-start.7 = (f32[24,128]{1,0:T(8,128)S(1)}, f32[24,128]{1,0:T(8,128)S(1)}, u32[]{:S(2)}, u32[]{:S(2)}) collective-permute-start(f32[24,128]{1,0:T(8,128)S(1)} %solve.1), channel_id=1, source_target_pairs={{0,2},{1,3},{2,0},{3,1},{4,6},{5,7},{6,4},{7,5},{8,10},{9,11},{10,... | collective-permute-start | bytes 36872 | tf_op jit(solution)/shard_map/ppermute | solution.py:414
  52.1 1.1 %collective-permute-done.9 = f32[24,128]{1,0:T(8,128)S(1)} collective-permute-done((f32[24,128]{1,0:T(8,128)S(1)}, f32[24,128]{1,0:T(8,128)S(1)}, u32[]{:S(2)}, u32[]{:S(2)}) %collective-permute-start.9) | collective-permute-done | bytes 12320 | tf_op jit(solution)/shard_map/ppermute | solution.py:414
  53.2 0.4 collective-permute-done.8
  53.5 0.2 collective-permute-done.7
  53.7 1.4 %collective-permute-start.12 = (f32[4,24,128]{2,1,0:T(8,128)S(1)}, f32[4,24,128]{2,1,0:T(8,128)S(1)}, u32[]{:S(2)}, u32[]{:S(2)}) collective-permute-start(f32[4,24,128]{2,1,0:T(8,128)S(1)} %pad_maximum_fusion), channel_id=1, source_target_pairs={{0,24},{8,16},{16,8},{24,0},{1,25},{9,17},{17,9},{25,1},{2,26},{10... | collective-permute-start | bytes 147464 | tf_op jit(solution)/shard_map/ppermute | solution.py:414
  55.2 1.5 %collective-permute-start.11 = (f32[4,24,128]{2,1,0:T(8,128)S(1)}, f32[4,24,128]{2,1,0:T(8,128)S(1)}, u32[]{:S(2)}, u32[]{:S(2)}) collective-permute-start(f32[4,24,128]{2,1,0:T(8,128)S(1)} %pad_maximum_fusion), channel_id=1, source_target_pairs={{0,16},{8,24},{16,0},{24,8},{1,17},{9,25},{17,1},{25,9},{2,18},{10... | collective-permute-start | bytes 147464 | tf_op jit(solution)/shard_map/ppermute | solution.py:414
  56.7 0.5 collective-permute-start.10
  57.2 3.5 %collective-permute-done.10 = f32[4,24,128]{2,1,0:T(8,128)S(1)} collective-permute-done((f32[4,24,128]{2,1,0:T(8,128)S(1)}, f32[4,24,128]{2,1,0:T(8,128)S(1)}, u32[]{:S(2)}, u32[]{:S(2)}) %collective-permute-start.10) | collective-permute-done | bytes 49184 | tf_op jit(solution)/shard_map/ppermute | solution.py:414
  60.8 0.0 collective-permute-done.11
  60.8 0.0 collective-permute-done.12
  60.8 0.1 collective-permute-start.13
  60.9 1.4 %collective-permute-done.13.far_ref = f32[16,24,128]{2,1,0:T(8,128)S(1)} collective-permute-done((f32[16,24,128]{2,1,0:T(8,128)S(1)}, f32[16,24,128]{2,1,0:T(8,128)S(1)}, u32[]{:S(2)}, u32[]{:S(2)}) %collective-permute-start.13) | collective-permute-done | bytes 196640 | tf_op jit(solution)/shard_map/ppermute | solution.py:414
  62.3 3.9 %modes.1 = (f32[64,16,1024]{2,1,0:T(8,128)}, f32[8,64]{1,0:T(8,128)}) custom-call(bf16[64,128,1024]{2,1,0:T(8,128)(2,1)S(1)} %get-tuple-element.10.coef_ref, f32[16,24,128]{2,1,0:T(8,128)S(1)} %constant_dynamic-update-slice_fusion.near_ref, f32[16,24,128]{2,1,0:T(8,128)S(1)} %collective-permute-done.13.far_ref, f32[1,1024]{1,0:T(1,128)S(1)} %bitcast.16), custom_call_target="tpu_custom_call" | custom-call | tf_op jit(solution)/shard_map/modes/pallas_call | solution.py:396
  (13 shorter events, 0.2 us)
Async XLA Ops:
  0.6 1.0 %copy-start = (f32[64,2,63,8]{0,3,2,1:T(8,128)S(1)}, f32[64,2,63,8]{0,3,2,1:T(8,128)}, u32[]{:S(2)}) copy-start(f32[64,2,63,8]{0,3,2,1:T(8,128)} %param.8) | copy-start | bytes 774148
  2.1 0.9 %copy-start.1 = (bf16[128,256]{1,0:T(8,128)(2,1)S(1)}, bf16[128,256]{1,0:T(8,128)(2,1)}, u32[]{:S(2)}) copy-start(bf16[128,256]{1,0:T(8,128)(2,1)} %constant.25.table_ref) | copy-start | bytes 196612
  3.0 0.7 %copy-start.2 = (f32[1024]{0:T(1024)S(1)}, f32[1024]{0:T(1024)}, u32[]{:S(2)}) copy-start(f32[1024]{0:T(1024)} %param.6) | copy-start | bytes 12292
  3.7 0.7 %copy-start.3 = (f32[1024]{0:T(1024)S(1)}, f32[1024]{0:T(1024)}, u32[]{:S(2)}) copy-start(f32[1024]{0:T(1024)} %param.7) | copy-start | bytes 12292
  18.2 2.1 %collective-permute-start = (f32[32,32,128]{2,1,0:T(8,128)S(1)}, f32[32,32,128]{2,1,0:T(8,128)S(1)}, u32[]{:S(2)}, u32[]{:S(2)}) collective-permute-start(f32[32,32,128]{2,1,0:T(8,128)S(1)} %get-tuple-element.12), channel_id=1, source_target_pairs={{0,1},{1,0},{2,3},{3,2},{4,5},{5,4},{6,7},{7,6},{8,9},{9,8},{10,11... | collective-permute-start | bytes 1572872 | tf_op jit(solution)/shard_map/ppermute | solution.py:414
  20.4 7.0 %collective-permute-start.1 = (f32[8,32,128]{2,1,0:T(8,128)S(1)}, f32[8,32,128]{2,1,0:T(8,128)S(1)}, u32[]{:S(2)}, u32[]{:S(2)}) collective-permute-start(f32[8,32,128]{2,1,0:T(8,128)S(1)} %get-tuple-element.16), channel_id=1, source_target_pairs={{0,8},{8,0},{16,24},{24,16},{1,9},{9,1},{17,25},{25,17},{2,10},{10... | collective-permute-start | bytes 393224 | tf_op jit(solution)/shard_map/ppermute | solution.py:414
  23.3 7.9 %collective-permute-start.3 = (f32[8,32,128]{2,1,0:T(8,128)S(1)}, f32[8,32,128]{2,1,0:T(8,128)S(1)}, u32[]{:S(2)}, u32[]{:S(2)}) collective-permute-start(f32[8,32,128]{2,1,0:T(8,128)S(1)} %get-tuple-element.17), channel_id=1, source_target_pairs={{0,24},{8,16},{16,8},{24,0},{1,25},{9,17},{17,9},{25,1},{2,26},{10... | collective-permute-start | bytes 393224 | tf_op jit(solution)/shard_map/ppermute | solution.py:414
  24.8 7.8 %collective-permute-start.2 = (f32[8,32,128]{2,1,0:T(8,128)S(1)}, f32[8,32,128]{2,1,0:T(8,128)S(1)}, u32[]{:S(2)}, u32[]{:S(2)}) collective-permute-start(f32[8,32,128]{2,1,0:T(8,128)S(1)} %get-tuple-element.18), channel_id=1, source_target_pairs={{0,16},{8,24},{16,0},{24,8},{1,17},{9,25},{17,1},{25,9},{2,18},{10... | collective-permute-start | bytes 393224 | tf_op jit(solution)/shard_map/ppermute | solution.py:414
  32.6 4.2 %collective-permute-start.4 = (f32[2,32,128]{2,1,0:T(8,128)S(1)}, f32[2,32,128]{2,1,0:T(8,128)S(1)}, u32[]{:S(2)}, u32[]{:S(2)}) collective-permute-start(f32[2,32,128]{2,1,0:T(8,128)S(1)} %get-tuple-element.19), channel_id=1, source_target_pairs={{0,2},{1,3},{2,0},{3,1},{4,6},{5,7},{6,4},{7,5},{8,10},{9,11},{10,... | collective-permute-start | bytes 98312 | tf_op jit(solution)/shard_map/ppermute | solution.py:414
  34.2 5.7 %collective-permute-start.6 = (f32[2,32,128]{2,1,0:T(8,128)S(1)}, f32[2,32,128]{2,1,0:T(8,128)S(1)}, u32[]{:S(2)}, u32[]{:S(2)}) collective-permute-start(f32[2,32,128]{2,1,0:T(8,128)S(1)} %get-tuple-element.20), channel_id=1, source_target_pairs={{0,6},{1,7},{2,4},{3,5},{4,2},{5,3},{6,0},{7,1},{8,14},{9,15},{10,... | collective-permute-start | bytes 98312 | tf_op jit(solution)/shard_map/ppermute | solution.py:414
  36.7 5.2 %collective-permute-start.5 = (f32[2,32,128]{2,1,0:T(8,128)S(1)}, f32[2,32,128]{2,1,0:T(8,128)S(1)}, u32[]{:S(2)}, u32[]{:S(2)}) collective-permute-start(f32[2,32,128]{2,1,0:T(8,128)S(1)} %get-tuple-element.21), channel_id=1, source_target_pairs={{0,4},{1,5},{2,6},{3,7},{4,0},{5,1},{6,2},{7,3},{8,12},{9,13},{10,... | collective-permute-start | bytes 98312 | tf_op jit(solution)/shard_map/ppermute | solution.py:414
  47.6 5.6 %collective-permute-start.9 = (f32[24,128]{1,0:T(8,128)S(1)}, f32[24,128]{1,0:T(8,128)S(1)}, u32[]{:S(2)}, u32[]{:S(2)}) collective-permute-start(f32[24,128]{1,0:T(8,128)S(1)} %solve.1), channel_id=1, source_target_pairs={{0,6},{1,7},{2,4},{3,5},{4,2},{5,3},{6,0},{7,1},{8,14},{9,15},{10,... | collective-permute-start | bytes 36872 | tf_op jit(solution)/shard_map/ppermute | solution.py:414
  48.9 4.6 %collective-permute-start.8 = (f32[24,128]{1,0:T(8,128)S(1)}, f32[24,128]{1,0:T(8,128)S(1)}, u32[]{:S(2)}, u32[]{:S(2)}) collective-permute-start(f32[24,128]{1,0:T(8,128)S(1)} %solve.1), channel_id=1, source_target_pairs={{0,4},{1,5},{2,6},{3,7},{4,0},{5,1},{6,2},{7,3},{8,12},{9,13},{10,... | collective-permute-start | bytes 36872 | tf_op jit(solution)/shard_map/ppermute | solution.py:414
  49.6 4.2 %collective-permute-start.7 = (f32[24,128]{1,0:T(8,128)S(1)}, f32[24,128]{1,0:T(8,128)S(1)}, u32[]{:S(2)}, u32[]{:S(2)}) collective-permute-start(f32[24,128]{1,0:T(8,128)S(1)} %solve.1), channel_id=1, source_target_pairs={{0,2},{1,3},{2,0},{3,1},{4,6},{5,7},{6,4},{7,5},{8,10},{9,11},{10,... | collective-permute-start | bytes 36872 | tf_op jit(solution)/shard_map/ppermute | solution.py:414
  53.7 7.1 %collective-permute-start.12 = (f32[4,24,128]{2,1,0:T(8,128)S(1)}, f32[4,24,128]{2,1,0:T(8,128)S(1)}, u32[]{:S(2)}, u32[]{:S(2)}) collective-permute-start(f32[4,24,128]{2,1,0:T(8,128)S(1)} %pad_maximum_fusion), channel_id=1, source_target_pairs={{0,24},{8,16},{16,8},{24,0},{1,25},{9,17},{17,9},{25,1},{2,26},{10... | collective-permute-start | bytes 147464 | tf_op jit(solution)/shard_map/ppermute | solution.py:414
  55.2 5.6 %collective-permute-start.11 = (f32[4,24,128]{2,1,0:T(8,128)S(1)}, f32[4,24,128]{2,1,0:T(8,128)S(1)}, u32[]{:S(2)}, u32[]{:S(2)}) collective-permute-start(f32[4,24,128]{2,1,0:T(8,128)S(1)} %pad_maximum_fusion), channel_id=1, source_target_pairs={{0,16},{8,24},{16,0},{24,8},{1,17},{9,25},{17,1},{25,9},{2,18},{10... | collective-permute-start | bytes 147464 | tf_op jit(solution)/shard_map/ppermute | solution.py:414
  56.7 4.1 %collective-permute-start.10 = (f32[4,24,128]{2,1,0:T(8,128)S(1)}, f32[4,24,128]{2,1,0:T(8,128)S(1)}, u32[]{:S(2)}, u32[]{:S(2)}) collective-permute-start(f32[4,24,128]{2,1,0:T(8,128)S(1)} %pad_maximum_fusion), channel_id=1, source_target_pairs={{0,8},{8,0},{16,24},{24,16},{1,9},{9,1},{17,25},{25,17},{2,10},{10... | collective-permute-start | bytes 147464 | tf_op jit(solution)/shard_map/ppermute | solution.py:414
  60.8 1.5 %collective-permute-start.13 = (f32[16,24,128]{2,1,0:T(8,128)S(1)}, f32[16,24,128]{2,1,0:T(8,128)S(1)}, u32[]{:S(2)}, u32[]{:S(2)}) collective-permute-start(f32[16,24,128]{2,1,0:T(8,128)S(1)} %constant_dynamic-update-slice_fusion.near_ref), channel_id=1, source_target_pairs={{0,1},{1,0},{2,3},{3,2},{4,5},{5,4},{6,7},{7,6},{8,9},{9,8},{10,11... | collective-permute-start | bytes 589832 | tf_op jit(solution)/shard_map/ppermute | solution.py:414

commit v6 on v5

--- a/solution.py
+++ b/solution.py
@@ -22,7 +22,6 @@
 PITCH = 2 * NB + 1
 MIB = 1024 * 1024
 TRANSFORM_MIB, SOLVE_MIB, MODES_MIB = 28, 8, 8
-MODES_FREQS = 8
 
 
 def dft_table():
@@ -46,22 +45,24 @@
         self.owners = row * self.g_slots
         self.per = NF // self.owners
 
-    def first_freq(self, core_slot, grp_slot, z_slot):
+    def half(self, other_core):
         row_index = lax.axis_index("row")
-        core = (row_index & 1) ^ core_slot
-        deep = (row_index >> 1) ^ z_slot
-        owner = deep * 2 + core
+        core = (row_index & 1) ^ int(other_core)
+        listed = []
+        for q in range(self.owners // 2):
+            owner = 2 * q + core
+            slot = ((owner % self.row) >> 1) ^ (row_index >> 1)
+            if self.split_grp:
+                slot = ((owner // self.row) ^ lax.axis_index("grp")) * self.deep + slot
+            for j in range(self.per):
+                listed.append((q * self.per + j, owner * self.per + j, slot))
+        return listed
+
+    def first_freq(self):
+        owner = lax.axis_index("row")
         if self.split_grp:
-            owner = (lax.axis_index("grp") ^ grp_slot) * self.row + owner
+            owner = lax.axis_index("grp") * self.row + owner
         return owner * self.per
-
-    def slot_of(self, f):
-        owner = f // self.per
-        row_index = lax.axis_index("row")
-        slot = ((owner % self.row) ^ row_index) >> 1
-        if self.split_grp:
-            slot = ((owner // self.row) ^ lax.axis_index("grp")) * self.deep + slot
-        return slot, ((owner ^ row_index) & 1) == 0
 
 
 def lane_index(shape):
@@ -72,7 +73,25 @@
     return lax.broadcasted_iota(jnp.int32, shape, 0)
 
 
-def transform_kernel(plan, snap_ref, weight_ref, field_ref, table_ref, coef_ref, keep_ref, send_ref, flip, gram):
+def pack(top, low):
+    row = row_index_of((NB, LANES))
+    lane = lane_index((NB, LANES))
+    left = lane < NB
+    upper = row < (lane & (NB - 1))
+    parts = jnp.where(left, jnp.where(upper, -low, top), jnp.where(upper, top, low))
+    first, second = parts[: NB // 2], parts[NB // 2 :]
+    left_half = left[: NB // 2]
+    other = pltpu.roll(jnp.where(left_half, second, first), NB, 1)
+    return jnp.where(left_half, first, second) + other
+
+
+def square(coefs):
+    return lax.dot_general(
+        coefs, coefs, (((1,), (1,)), ((), ())), preferred_element_type=jnp.float32
+    )
+
+
+def transform_kernel(plan, snap_ref, weight_ref, field_ref, table_ref, coef_ref, send_ref, flip, gram):
     step = pl.program_id(0)
     tile = snap_ref.shape[1]
     pieces = tile // LANES
@@ -91,7 +110,7 @@
                 ]
         return carry
 
-    lax.fori_loop(0, NBLK, one_block, 0, unroll=63)
+    lax.fori_loop(0, NBLK, one_block, 0, unroll=NBLK)
     for piece in range(pieces):
         probe = probe_row[:, piece * LANES : (piece + 1) * LANES]
         flip[piece, pl.ds(NB - 1, NF, stride=PITCH), :] = jnp.broadcast_to(probe, (NF, LANES))
@@ -101,52 +120,31 @@
     def _():
         gram[...] = jnp.zeros_like(gram)
 
-    def one_freq(f, carry):
+    def rounded(f):
         wide = jnp.concatenate(
             [flip[piece, pl.ds(f * PITCH, 2 * NB), :] for piece in range(pieces)], axis=1
         )
         coefs = wide.astype(jnp.bfloat16)
         coef_ref[f, :, here] = coefs
-        gram[f] += lax.dot_general(
-            coefs, coefs, (((1,), (1,)), ((), ())), preferred_element_type=jnp.float32
-        )
+        return coefs
+
+    def one_freq(f, carry):
+        rounded(f)
         return carry
 
-    lax.fori_loop(0, NF, one_freq, 0, unroll=64)
+    lax.fori_loop(0, NF, one_freq, 0, unroll=NF)
 
     @pl.when(step == pl.num_programs(0) - 1)
     def _():
-        row = row_index_of((NB, LANES))
-        lane = lane_index((NB, LANES))
-        left = lane < NB
-        upper = row < (lane & (NB - 1))
-        left_half = left[: NB // 2]
-
-        def pack(f):
-            top = gram[f, :NB, :]
-            low = gram[f, NB:, :]
-            parts = jnp.where(left, jnp.where(upper, -low, top), jnp.where(upper, top, low))
-            first, second = parts[: NB // 2], parts[NB // 2 :]
-            other = pltpu.roll(jnp.where(left_half, second, first), NB, 1)
-            return jnp.where(left_half, first, second) + other
-
-        for core_slot, out_ref in ((0, keep_ref), (1, send_ref)):
-
-            def one_slot(slot, carry):
-                first = plan.first_freq(core_slot, slot // plan.deep, slot % plan.deep)
-                for j in range(plan.per):
-                    out_ref[slot * plan.per + j] = pack(first + j)
-                return carry
-
-            lax.fori_loop(0, plan.g_slots * plan.deep, one_slot, 0, unroll=8)
+        for n, f, slot in plan.half(True):
+            whole = square(coef_ref[f])
+            send_ref[slot * plan.per + n % plan.per] = pack(whole[:NB], whole[NB:])
 
 
 def transform(plan, snapshots, weights, reference_field):
     rows_here = snapshots.shape[1]
     tile = min(256, rows_here)
     half_freqs = NF // 2
-    packed = jax.ShapeDtypeStruct((half_freqs, NB // 2, LANES), jnp.float32)
-    packed_spec = pl.BlockSpec((half_freqs, NB // 2, LANES), lambda i: (0, 0, 0))
     return pl.pallas_call(
         functools.partial(transform_kernel, plan),
         grid=(rows_here // tile,),
@@ -156,23 +154,63 @@
             pl.BlockSpec((1, tile), lambda i: (0, i)),
             pl.BlockSpec((2 * NF, NFFT), lambda i: (0, 0)),
         ],
-        out_specs=[
-            pl.BlockSpec(memory_space=pltpu.VMEM),
-            packed_spec,
-            packed_spec,
-        ],
+        out_specs=[pl.BlockSpec(memory_space=pltpu.VMEM)] * 2,
         out_shape=[
             jax.ShapeDtypeStruct((NF, 2 * NB, rows_here), jnp.bfloat16),
-            packed,
-            packed,
+            jax.ShapeDtypeStruct((half_freqs, NB // 2, LANES), jnp.float32),
         ],
         scratch_shapes=[
             pltpu.VMEM((tile // LANES, NF * PITCH, LANES), jnp.float32),
-            pltpu.VMEM((NF, 2 * NB, LANES), jnp.float32),
+            pltpu.VMEM((half_freqs, 2 * NB, LANES), jnp.float32),
         ],
         compiler_params=pltpu.CompilerParams(vmem_limit_bytes=TRANSFORM_MIB * MIB),
         name="transform",
     )(snapshots, weights[None], reference_field[None], dft_table())
+
+
+def own_gram_kernel(plan, coef_ref, keep_ref):
+    for n, f, slot in plan.half(False):
+        whole = square(coef_ref[f])
+        keep_ref[slot * plan.per + n % plan.per] = pack(whole[:NB], whole[NB:])
+
+
+def own_gram(plan, coeffs):
+    freqs, rows, columns = coeffs.shape
+    return pl.pallas_call(
+        functools.partial(own_gram_kernel, plan),
+        in_specs=[pl.BlockSpec(memory_space=pltpu.VMEM)],
+        out_specs=pl.BlockSpec(memory_space=pltpu.VMEM),
+        out_shape=jax.ShapeDtypeStruct((NF // 2, NB // 2, LANES), jnp.float32),
+        cost_estimate=pl.CostEstimate(
+            flops=freqs * rows * rows * columns, bytes_accessed=freqs * rows * columns, transcendentals=0
+        ),
+        compiler_params=pltpu.CompilerParams(vmem_limit_bytes=SOLVE_MIB * MIB),
+        name="own_gram",
+    )(coeffs)
+
+
+def start_kernel(plan, basis_ref, out_ref):
+    lane = lane_index((NM, LANES))
+    lane_in = lane_index((NM, basis_ref.shape[3]))
+    for j in range(plan.per):
+        chosen = lane_in == plan.first_freq() + j
+        rows = jnp.zeros((NM, LANES), jnp.float32)
+        for part in range(2):
+            for b in range(NBLK):
+                value = jnp.sum(jnp.where(chosen, basis_ref[part, b], 0.0), axis=1, keepdims=True)
+                rows = jnp.where(lane == part * NB + b, value, rows)
+        out_ref[j] = rows
+
+
+def start_rows(plan, start_basis):
+    return pl.pallas_call(
+        functools.partial(start_kernel, plan),
+        in_specs=[pl.BlockSpec(memory_space=pltpu.VMEM)],
+        out_specs=pl.BlockSpec(memory_space=pltpu.VMEM),
+        out_shape=jax.ShapeDtypeStruct((plan.per, NM, LANES), jnp.float32),
+        compiler_params=pltpu.CompilerParams(vmem_limit_bytes=SOLVE_MIB * MIB),
+        name="start_rows",
+    )(jnp.transpose(start_basis, (1, 2, 3, 0)))
 
 
 def split_three(x):
@@ -357,18 +395,17 @@
     )(packed, start)
 
 
-def modes_kernel(plan, coef_ref, near_ref, far_ref, weight_ref, out_hbm, energy_ref, out, sems):
+def modes_kernel(plan, other_core, coef_ref, pay_ref, weight_ref, *refs):
+    out_hbm, energy_ref, out, sems = refs[-4:]
     inverse_root = 1.0 / jnp.sqrt(weight_ref[...])
     lane8 = lane_index((NM, LANES))
     left = lane8 < NB
     energies = jnp.zeros((NM, LANES), jnp.float32)
     copies = []
-    for f in range(NF):
-        slot, same_core = plan.slot_of(f)
-        packed = jnp.where(same_core, near_ref[slot], far_ref[slot])
-        j = f % plan.per
-        c = packed[j * NM : (j + 1) * NM]
-        extras = packed[plan.per * NM :]
+    for n, f, slot in plan.half(other_core):
+        j = n % plan.per
+        c = pay_ref[slot, j * NM : (j + 1) * NM]
+        extras = pay_ref[slot, plan.per * NM :]
         factor_real = extras[:, 3 * j : 3 * j + 1]
         factor_imag = extras[:, 3 * j + 1 : 3 * j + 2]
         matrix = jnp.concatenate([jnp.where(left, c, -c), pltpu.roll(c, NB, 1)], axis=0)
@@ -377,37 +414,46 @@
         )
         real = projected[:NM]
         imag = projected[NM:]
-        out[f, :NM, :] = (real * factor_real - imag * factor_imag) * inverse_root
-        out[f, NM:, :] = (real * factor_imag + imag * factor_real) * inverse_root
+        out[n, :NM, :] = (real * factor_real - imag * factor_imag) * inverse_root
+        out[n, NM:, :] = (real * factor_imag + imag * factor_real) * inverse_root
         energies = jnp.where(lane8 == f, extras[:, 3 * j + 2 : 3 * j + 3], energies)
-        if (f + 1) % MODES_FREQS == 0:
-            done = pl.ds(f + 1 - MODES_FREQS, MODES_FREQS)
-            copy = pltpu.make_async_copy(out.at[done], out_hbm.at[done], sems.at[len(copies)])
+        if j == plan.per - 1:
+            copy = pltpu.make_async_copy(
+                out.at[pl.ds(n - j, plan.per)],
+                out_hbm.at[pl.ds(f - j, plan.per)],
+                sems.at[len(copies)],
+            )
             copy.start()
             copies.append(copy)
-    energy_ref[...] = energies[:, :NF]
+    energies = energies[:, :NF]
+    energy_ref[...] = energies + refs[1][...] if other_core else energies
     for copy in copies:
         copy.wait()
 
 
-def modes(plan, coeffs, near, far, weights):
+def modes(plan, coeffs, payload, weights, earlier=()):
     rows_here = coeffs.shape[2]
     whole = jax.ShapeDtypeStruct((NF, 2 * NM, rows_here), jnp.float32)
+    places = [pltpu.HBM, pltpu.VMEM]
     return pl.pallas_call(
-        functools.partial(modes_kernel, plan),
-        in_specs=[pl.BlockSpec(memory_space=pltpu.VMEM)] * 4,
-        out_specs=[
-            pl.BlockSpec(memory_space=pltpu.HBM),
-            pl.BlockSpec(memory_space=pltpu.VMEM),
+        functools.partial(modes_kernel, plan, bool(earlier)),
+        in_specs=[pl.BlockSpec(memory_space=pltpu.VMEM)] * 3
+        + [pl.BlockSpec(memory_space=place) for place in places[: len(earlier)]],
+        out_specs=[pl.BlockSpec(memory_space=place) for place in places],
+        out_shape=[whole, jax.ShapeDtypeStruct((NM, NF), jnp.float32)],
+        input_output_aliases={3: 0} if earlier else {},
+        scratch_shapes=[
+            pltpu.VMEM((NF // 2,) + whole.shape[1:], whole.dtype),
+            pltpu.SemaphoreType.DMA((plan.owners // 2,)),
         ],
-        out_shape=[whole, jax.ShapeDtypeStruct((NM, NF), jnp.float32)],
-        scratch_shapes=[
-            pltpu.VMEM(whole.shape, whole.dtype),
-            pltpu.SemaphoreType.DMA((NF // MODES_FREQS,)),
-        ],
+        cost_estimate=pl.CostEstimate(
+            flops=2 * NF * NM * 2 * NB * rows_here,
+            bytes_accessed=2 * NF * NM * 4 * rows_here,
+            transcendentals=0,
+        ),
         compiler_params=pltpu.CompilerParams(vmem_limit_bytes=MODES_MIB * MIB),
-        name="modes",
-    )(coeffs, near, far, weights[None])
+        name="other_modes" if earlier else "own_modes",
+    )(coeffs, payload, weights[None], *earlier)
 
 
 def swap(x, axis, size, offset):
@@ -416,14 +462,12 @@
 
 def shards(plan, snapshots, weights, reference_field, start_basis):
     total_rows = snapshots.shape[1] * plan.grp * plan.row
-    start = lax.dynamic_slice_in_dim(start_basis, plan.first_freq(0, 0, 0), plan.per, 0)
-    start = jnp.pad(start, ((0, 0), (0, 0), (0, NB - NBLK), (0, 0)))
-    start = jnp.transpose(start, (0, 3, 1, 2)).reshape(plan.per, NM, 2 * NB)
-    snapshots, start = lax.optimization_barrier((snapshots, start))
-
-    coeffs, keep, send = transform(plan, snapshots, weights, reference_field)
-
-    held = keep + swap(send, "row", plan.row, 1)
+    coeffs, send = transform(plan, snapshots, weights, reference_field)
+    start_basis, send = lax.optimization_barrier((start_basis, send))
+    start = start_rows(plan, start_basis)
+
+    arrived = swap(send, "row", plan.row, 1)
+    held = own_gram(plan, coeffs) + arrived
     if plan.split_grp:
         held = held.reshape((plan.grp, plan.deep * plan.per) + held.shape[1:])
         arrived = [swap(held[d], "grp", plan.grp, d) for d in range(1, plan.grp)]
@@ -444,7 +488,8 @@
             [payload] + [swap(payload, "grp", plan.grp, d) for d in range(1, plan.grp)]
         )
     far = swap(payload, "row", plan.row, 1)
-    spod_modes, energies = modes(plan, coeffs, payload, far, weights)
+    own = modes(plan, coeffs, payload, weights)
+    spod_modes, energies = modes(plan, coeffs, far, weights, own)
     return spod_modes, jnp.transpose(energies)
 
 

time: 66.5 us -> 64.3 us (0.967)
  waiting for transfers between devices: 21 us -> 18 us
  Pallas kernels: 23.4 us -> 26 us
  local copies, waits for them, and re-layouts: 3.77 us -> 2.27 us
    pallas_call x1 -> x4, Pallas kernels: 3.88 us -> 7.58 us  [the longest x2 4.79 us: modes(): pl.pallas_call(functools.partial(modes_kernel, plan, bool(earlier)), in_s...]
    ppermute x14, waiting for transfers between devices: 21 us -> 18 us  [swap(): return lax.ppermute(x, axis, [(i, i ^ offset) for i in range(size)])]
    pallas_call x1, Pallas kernels: 13.8 us -> 12.7 us  [transform(): pl.pallas_call(functools.partial(transform_kernel, plan), grid=(rows_here...]
    unnamed x14, local copies, waits for them, and re-layouts: 3.28 us -> 2.23 us
  transfers between devices with their start and end apart: 14 -> 14, of which waited for: 11 -> 9; matrix products, arithmetic and copies ran while one was open for 0% -> 0% of each run, Pallas kernels for 0% -> 8%
where the time goes in v6:
time: 64.3 us; the launch traced here: 64 us
  Pallas kernels  26 us (40%)
  waiting for transfers between devices  18 us (28%)
  starting transfers between devices  16.9 us (26%)
  local copies, waits for them, and re-layouts  2.27 us (4%)
  between operations  0.77 us (1%)
    ppermute x14, waiting for transfers between devices, swap(): return lax.ppermute(x, axis, [(i, i ^ offset) for i in range(size)])  18 us
    ppermute x14, starting transfers between devices, swap(): return lax.ppermute(x, axis, [(i, i ^ offset) for i in range(size)])  16.9 us
    pallas_call x1, Pallas kernels, transform(): pl.pallas_call(functools.partial(transform_kernel, plan), grid=(rows_here...  12.7 us
    pallas_call x1, Pallas kernels, solve(): pl.pallas_call(functools.partial(solve_kernel, plan, total_rows), in_spec...  5.69 us
    pallas_call x2, Pallas kernels, modes(): pl.pallas_call(functools.partial(modes_kernel, plan, bool(earlier)), in_s...  4.79 us
    pallas_call x1, Pallas kernels, own_gram(): pl.pallas_call(functools.partial(own_gram_kernel, plan), in_specs=[pl.Blo...  2.45 us
    unnamed x14, local copies, waits for them, and re-layouts  2.23 us
  transfers between devices with their start and end apart: 14, of which 9 were waited for; matrix products, arithmetic and copies ran while one was open for 0% of the time, Pallas kernels for 8%

profile of v6, /device:TPU:0, one launch (start us, length us, event | category | flops | bytes accessed | tf_op | source)
XLA Modules:
  0.0 64.0 jit_solution(13802427352890083345)
XLA Ops:
  0.6 0.0 copy-start.1
  0.6 0.8 %copy-done.1 = bf16[128,256]{1,0:T(8,128)(2,1)S(1)} copy-done((bf16[128,256]{1,0:T(8,128)(2,1)S(1)}, bf16[128,256]{1,0:T(8,128)(2,1)}, u32[]{:S(2)}) %copy-start.1) | copy-done | bytes 65560
  1.5 0.0 copy-start.2
  1.5 0.7 %copy-done.2 = f32[1024]{0:T(1024)S(1)} copy-done((f32[1024]{0:T(1024)S(1)}, f32[1024]{0:T(1024)}, u32[]{:S(2)}) %copy-start.2) | copy-done | bytes 4120
  2.2 0.0 copy-start.3
  2.2 0.7 %copy-done.3 = f32[1024]{0:T(1024)S(1)} copy-done((f32[1024]{0:T(1024)S(1)}, f32[1024]{0:T(1024)}, u32[]{:S(2)}) %copy-start.3) | copy-done | bytes 4120
  2.8 0.0 copy-start
  2.9 12.7 %transform.1 = (bf16[64,128,1024]{2,1,0:T(8,128)(2,1)S(1)}, f32[32,32,128]{2,1,0:T(8,128)S(1)}) custom-call(bf16[8192,1024]{1,0:T(8,128)(2,1)} %snap_ref.1, f32[1,1024]{1,0:T(1,128)S(1)} %bitcast.14, f32[1,1024]{1,0:T(1,128)S(1)} %bitcast.17, bf16[128,256]{1,0:T(8,128)(2,1)S(1)} %copy-done.1), custom_call_target="tpu_custom_call" | custom-call | tf_op jit(solution)/shard_map/transform/pallas_call | solution.py:148
  15.5 0.5 collective-permute-start
  16.1 2.4 %own_gram.1 = f32[32,32,128]{2,1,0:T(8,128)S(1)} custom-call(bf16[64,128,1024]{2,1,0:T(8,128)(2,1)S(1)} %get-tuple-element.10.coef_ref), custom_call_target="tpu_custom_call" | custom-call | flops 1073741824 | bytes 8388608 | tf_op jit(solution)/shard_map/own_gram/pallas_call | solution.py:179
  18.5 0.0 collective-permute-done
  18.5 0.1 add.21
  18.7 2.6 %collective-permute-start.1 = (f32[8,32,128]{2,1,0:T(8,128)S(1)}, f32[8,32,128]{2,1,0:T(8,128)S(1)}, u32[]{:S(2)}, u32[]{:S(2)}) collective-permute-start(f32[8,32,128]{2,1,0:T(8,128)S(1)} %get-tuple-element.18), channel_id=1, source_target_pairs={{0,8},{8,0},{16,24},{24,16},{1,9},{9,1},{17,25},{25,17},{2,10},{10... | collective-permute-start | bytes 393224 | tf_op jit(solution)/shard_map/ppermute | solution.py:460
  21.2 1.5 %collective-permute-start.3 = (f32[8,32,128]{2,1,0:T(8,128)S(1)}, f32[8,32,128]{2,1,0:T(8,128)S(1)}, u32[]{:S(2)}, u32[]{:S(2)}) collective-permute-start(f32[8,32,128]{2,1,0:T(8,128)S(1)} %get-tuple-element.19), channel_id=1, source_target_pairs={{0,24},{8,16},{16,8},{24,0},{1,25},{9,17},{17,9},{25,1},{2,26},{10... | collective-permute-start | bytes 393224 | tf_op jit(solution)/shard_map/ppermute | solution.py:460
  22.7 0.1 collective-permute-start.2
  22.8 2.8 %collective-permute-done.1 = f32[8,32,128]{2,1,0:T(8,128)S(1)} collective-permute-done((f32[8,32,128]{2,1,0:T(8,128)S(1)}, f32[8,32,128]{2,1,0:T(8,128)S(1)}, u32[]{:S(2)}, u32[]{:S(2)}) %collective-permute-start.1) | collective-permute-done | bytes 131104 | tf_op jit(solution)/shard_map/ppermute | solution.py:460
  25.6 3.9 %collective-permute-done.3 = f32[8,32,128]{2,1,0:T(8,128)S(1)} collective-permute-done((f32[8,32,128]{2,1,0:T(8,128)S(1)}, f32[8,32,128]{2,1,0:T(8,128)S(1)}, u32[]{:S(2)}, u32[]{:S(2)}) %collective-permute-start.3) | collective-permute-done | bytes 131104 | tf_op jit(solution)/shard_map/ppermute | solution.py:460
  29.5 1.4 %collective-permute-done.2 = f32[8,32,128]{2,1,0:T(8,128)S(1)} collective-permute-done((f32[8,32,128]{2,1,0:T(8,128)S(1)}, f32[8,32,128]{2,1,0:T(8,128)S(1)}, u32[]{:S(2)}, u32[]{:S(2)}) %collective-permute-start.2) | collective-permute-done | bytes 131104 | tf_op jit(solution)/shard_map/ppermute | solution.py:460
  30.9 1.6 %collective-permute-start.4 = (f32[2,32,128]{2,1,0:T(8,128)S(1)}, f32[2,32,128]{2,1,0:T(8,128)S(1)}, u32[]{:S(2)}, u32[]{:S(2)}) collective-permute-start(f32[2,32,128]{2,1,0:T(8,128)S(1)} %get-tuple-element.21), channel_id=1, source_target_pairs={{0,2},{1,3},{2,0},{3,1},{4,6},{5,7},{6,4},{7,5},{8,10},{9,11},{10,... | collective-permute-start | bytes 98312 | tf_op jit(solution)/shard_map/ppermute | solution.py:460
  32.6 2.5 %collective-permute-start.6 = (f32[2,32,128]{2,1,0:T(8,128)S(1)}, f32[2,32,128]{2,1,0:T(8,128)S(1)}, u32[]{:S(2)}, u32[]{:S(2)}) collective-permute-start(f32[2,32,128]{2,1,0:T(8,128)S(1)} %get-tuple-element.22), channel_id=1, source_target_pairs={{0,6},{1,7},{2,4},{3,5},{4,2},{5,3},{6,0},{7,1},{8,14},{9,15},{10,... | collective-permute-start | bytes 98312 | tf_op jit(solution)/shard_map/ppermute | solution.py:460
  35.0 0.1 collective-permute-start.5
  35.2 0.0 copy-done
  35.2 0.3 start_rows.1.start_ref
  35.5 0.0 collective-permute-done.4
  35.5 2.7 %collective-permute-done.6 = f32[2,32,128]{2,1,0:T(8,128)S(1)} collective-permute-done((f32[2,32,128]{2,1,0:T(8,128)S(1)}, f32[2,32,128]{2,1,0:T(8,128)S(1)}, u32[]{:S(2)}, u32[]{:S(2)}) %collective-permute-start.6) | collective-permute-done | bytes 32800 | tf_op jit(solution)/shard_map/ppermute | solution.py:460
  38.3 1.9 %collective-permute-done.5 = f32[2,32,128]{2,1,0:T(8,128)S(1)} collective-permute-done((f32[2,32,128]{2,1,0:T(8,128)S(1)}, f32[2,32,128]{2,1,0:T(8,128)S(1)}, u32[]{:S(2)}, u32[]{:S(2)}) %collective-permute-start.5) | collective-permute-done | bytes 32800 | tf_op jit(solution)/shard_map/ppermute | solution.py:460
  40.2 5.7 %solve.1 = f32[24,128]{1,0:T(8,128)S(1)} custom-call(f32[2,32,128]{2,1,0:T(8,128)S(1)} %fusion.3.packed_ref, f32[2,8,128]{2,1,0:T(8,128)S(1)} %start_rows.1.start_ref), custom_call_target="tpu_custom_call" | custom-call | tf_op jit(solution)/shard_map/solve/pallas_call | solution.py:387
  45.9 1.3 %collective-permute-start.9 = (f32[24,128]{1,0:T(8,128)S(1)}, f32[24,128]{1,0:T(8,128)S(1)}, u32[]{:S(2)}, u32[]{:S(2)}) collective-permute-start(f32[24,128]{1,0:T(8,128)S(1)} %solve.1), channel_id=1, source_target_pairs={{0,6},{1,7},{2,4},{3,5},{4,2},{5,3},{6,0},{7,1},{8,14},{9,15},{10,... | collective-permute-start | bytes 36872 | tf_op jit(solution)/shard_map/ppermute | solution.py:460
  47.2 0.6 %collective-permute-start.8 = (f32[24,128]{1,0:T(8,128)S(1)}, f32[24,128]{1,0:T(8,128)S(1)}, u32[]{:S(2)}, u32[]{:S(2)}) collective-permute-start(f32[24,128]{1,0:T(8,128)S(1)} %solve.1), channel_id=1, source_target_pairs={{0,4},{1,5},{2,6},{3,7},{4,0},{5,1},{6,2},{7,3},{8,12},{9,13},{10,... | collective-permute-start | bytes 36872 | tf_op jit(solution)/shard_map/ppermute | solution.py:460
  47.9 2.5 %collective-permute-start.7 = (f32[24,128]{1,0:T(8,128)S(1)}, f32[24,128]{1,0:T(8,128)S(1)}, u32[]{:S(2)}, u32[]{:S(2)}) collective-permute-start(f32[24,128]{1,0:T(8,128)S(1)} %solve.1), channel_id=1, source_target_pairs={{0,2},{1,3},{2,0},{3,1},{4,6},{5,7},{6,4},{7,5},{8,10},{9,11},{10,... | collective-permute-start | bytes 36872 | tf_op jit(solution)/shard_map/ppermute | solution.py:460
  50.4 1.1 %collective-permute-done.9 = f32[24,128]{1,0:T(8,128)S(1)} collective-permute-done((f32[24,128]{1,0:T(8,128)S(1)}, f32[24,128]{1,0:T(8,128)S(1)}, u32[]{:S(2)}, u32[]{:S(2)}) %collective-permute-start.9) | collective-permute-done | bytes 12320 | tf_op jit(solution)/shard_map/ppermute | solution.py:460
  51.5 0.3 collective-permute-done.8
  51.8 0.2 collective-permute-done.7
  52.0 1.4 %collective-permute-start.12 = (f32[4,24,128]{2,1,0:T(8,128)S(1)}, f32[4,24,128]{2,1,0:T(8,128)S(1)}, u32[]{:S(2)}, u32[]{:S(2)}) collective-permute-start(f32[4,24,128]{2,1,0:T(8,128)S(1)} %pad_maximum_fusion), channel_id=1, source_target_pairs={{0,24},{8,16},{16,8},{24,0},{1,25},{9,17},{17,9},{25,1},{2,26},{10... | collective-permute-start | bytes 147464 | tf_op jit(solution)/shard_map/ppermute | solution.py:460
  53.5 1.5 %collective-permute-start.11 = (f32[4,24,128]{2,1,0:T(8,128)S(1)}, f32[4,24,128]{2,1,0:T(8,128)S(1)}, u32[]{:S(2)}, u32[]{:S(2)}) collective-permute-start(f32[4,24,128]{2,1,0:T(8,128)S(1)} %pad_maximum_fusion), channel_id=1, source_target_pairs={{0,16},{8,24},{16,0},{24,8},{1,17},{9,25},{17,1},{25,9},{2,18},{10... | collective-permute-start | bytes 147464 | tf_op jit(solution)/shard_map/ppermute | solution.py:460
  55.0 0.5 collective-permute-start.10
  55.5 3.5 %collective-permute-done.10 = f32[4,24,128]{2,1,0:T(8,128)S(1)} collective-permute-done((f32[4,24,128]{2,1,0:T(8,128)S(1)}, f32[4,24,128]{2,1,0:T(8,128)S(1)}, u32[]{:S(2)}, u32[]{:S(2)}) %collective-permute-start.10) | collective-permute-done | bytes 49184 | tf_op jit(solution)/shard_map/ppermute | solution.py:460
  59.1 0.0 collective-permute-done.11
  59.1 0.0 collective-permute-done.12
  59.1 0.1 collective-permute-start.13
  59.2 2.1 %own_modes.1 = (f32[64,16,1024]{2,1,0:T(8,128)}, f32[8,64]{1,0:T(8,128)S(1)}) custom-call(bf16[64,128,1024]{2,1,0:T(8,128)(2,1)S(1)} %get-tuple-element.10.coef_ref, f32[16,24,128]{2,1,0:T(8,128)S(1)} %constant_dynamic-update-slice_fusion.pay_ref, f32[1,1024]{1,0:T(1,128)S(1)} %bitcast.15), custom_call_target="tpu_custom_call" | custom-call | flops 134217728 | bytes 4194304 | tf_op jit(solution)/shard_map/own_modes/pallas_call | solution.py:438
  61.3 0.0 collective-permute-done.13.pay_ref
  61.3 2.7 %other_modes.1 = (f32[64,16,1024]{2,1,0:T(8,128)}, f32[8,64]{1,0:T(8,128)}) custom-call(bf16[64,128,1024]{2,1,0:T(8,128)(2,1)S(1)} %get-tuple-element.10.coef_ref, f32[16,24,128]{2,1,0:T(8,128)S(1)} %collective-permute-done.13.pay_ref, f32[1,1024]{1,0:T(1,128)S(1)} %bitcast.16, ...), custom_call_target="tpu_custom_call", output_to_operand_aliasing={{0}: (3, {})} | custom-call | flops 134217728 | bytes 4194304 | tf_op jit(solution)/shard_map/other_modes/pallas_call | solution.py:438
  (12 shorter events, 0.1 us)
Async XLA Ops:
  0.6 0.8 %copy-start.1 = (bf16[128,256]{1,0:T(8,128)(2,1)S(1)}, bf16[128,256]{1,0:T(8,128)(2,1)}, u32[]{:S(2)}) copy-start(bf16[128,256]{1,0:T(8,128)(2,1)} %constant.3.table_ref) | copy-start | bytes 196612
  1.5 0.7 %copy-start.2 = (f32[1024]{0:T(1024)S(1)}, f32[1024]{0:T(1024)}, u32[]{:S(2)}) copy-start(f32[1024]{0:T(1024)} %param.6) | copy-start | bytes 12292
  2.2 0.7 %copy-start.3 = (f32[1024]{0:T(1024)S(1)}, f32[1024]{0:T(1024)}, u32[]{:S(2)}) copy-start(f32[1024]{0:T(1024)} %param.7) | copy-start | bytes 12292
  2.8 32.3 %copy-start = (f32[64,2,63,8]{0,3,2,1:T(8,128)S(1)}, f32[64,2,63,8]{0,3,2,1:T(8,128)}, u32[]{:S(2)}) copy-start(f32[64,2,63,8]{0,3,2,1:T(8,128)} %param.8) | copy-start | bytes 774148
  15.5 3.0 %collective-permute-start = (f32[32,32,128]{2,1,0:T(8,128)S(1)}, f32[32,32,128]{2,1,0:T(8,128)S(1)}, u32[]{:S(2)}, u32[]{:S(2)}) collective-permute-start(f32[32,32,128]{2,1,0:T(8,128)S(1)} %get-tuple-element.12), channel_id=1, source_target_pairs={{0,1},{1,0},{2,3},{3,2},{4,5},{5,4},{6,7},{7,6},{8,9},{9,8},{10,11... | collective-permute-start | bytes 1572872 | tf_op jit(solution)/shard_map/ppermute | solution.py:460
  18.7 6.9 %collective-permute-start.1 = (f32[8,32,128]{2,1,0:T(8,128)S(1)}, f32[8,32,128]{2,1,0:T(8,128)S(1)}, u32[]{:S(2)}, u32[]{:S(2)}) collective-permute-start(f32[8,32,128]{2,1,0:T(8,128)S(1)} %get-tuple-element.18), channel_id=1, source_target_pairs={{0,8},{8,0},{16,24},{24,16},{1,9},{9,1},{17,25},{25,17},{2,10},{10... | collective-permute-start | bytes 393224 | tf_op jit(solution)/shard_map/ppermute | solution.py:460
  21.2 8.3 %collective-permute-start.3 = (f32[8,32,128]{2,1,0:T(8,128)S(1)}, f32[8,32,128]{2,1,0:T(8,128)S(1)}, u32[]{:S(2)}, u32[]{:S(2)}) collective-permute-start(f32[8,32,128]{2,1,0:T(8,128)S(1)} %get-tuple-element.19), channel_id=1, source_target_pairs={{0,24},{8,16},{16,8},{24,0},{1,25},{9,17},{17,9},{25,1},{2,26},{10... | collective-permute-start | bytes 393224 | tf_op jit(solution)/shard_map/ppermute | solution.py:460
  22.7 8.1 %collective-permute-start.2 = (f32[8,32,128]{2,1,0:T(8,128)S(1)}, f32[8,32,128]{2,1,0:T(8,128)S(1)}, u32[]{:S(2)}, u32[]{:S(2)}) collective-permute-start(f32[8,32,128]{2,1,0:T(8,128)S(1)} %get-tuple-element.20), channel_id=1, source_target_pairs={{0,16},{8,24},{16,0},{24,8},{1,17},{9,25},{17,1},{25,9},{2,18},{10... | collective-permute-start | bytes 393224 | tf_op jit(solution)/shard_map/ppermute | solution.py:460
  30.9 4.6 %collective-permute-start.4 = (f32[2,32,128]{2,1,0:T(8,128)S(1)}, f32[2,32,128]{2,1,0:T(8,128)S(1)}, u32[]{:S(2)}, u32[]{:S(2)}) collective-permute-start(f32[2,32,128]{2,1,0:T(8,128)S(1)} %get-tuple-element.21), channel_id=1, source_target_pairs={{0,2},{1,3},{2,0},{3,1},{4,6},{5,7},{6,4},{7,5},{8,10},{9,11},{10,... | collective-permute-start | bytes 98312 | tf_op jit(solution)/shard_map/ppermute | solution.py:460
  32.6 5.7 %collective-permute-start.6 = (f32[2,32,128]{2,1,0:T(8,128)S(1)}, f32[2,32,128]{2,1,0:T(8,128)S(1)}, u32[]{:S(2)}, u32[]{:S(2)}) collective-permute-start(f32[2,32,128]{2,1,0:T(8,128)S(1)} %get-tuple-element.22), channel_id=1, source_target_pairs={{0,6},{1,7},{2,4},{3,5},{4,2},{5,3},{6,0},{7,1},{8,14},{9,15},{10,... | collective-permute-start | bytes 98312 | tf_op jit(solution)/shard_map/ppermute | solution.py:460
  35.0 5.2 %collective-permute-start.5 = (f32[2,32,128]{2,1,0:T(8,128)S(1)}, f32[2,32,128]{2,1,0:T(8,128)S(1)}, u32[]{:S(2)}, u32[]{:S(2)}) collective-permute-start(f32[2,32,128]{2,1,0:T(8,128)S(1)} %get-tuple-element.23), channel_id=1, source_target_pairs={{0,4},{1,5},{2,6},{3,7},{4,0},{5,1},{6,2},{7,3},{8,12},{9,13},{10,... | collective-permute-start | bytes 98312 | tf_op jit(solution)/shard_map/ppermute | solution.py:460
  45.9 5.6 %collective-permute-start.9 = (f32[24,128]{1,0:T(8,128)S(1)}, f32[24,128]{1,0:T(8,128)S(1)}, u32[]{:S(2)}, u32[]{:S(2)}) collective-permute-start(f32[24,128]{1,0:T(8,128)S(1)} %solve.1), channel_id=1, source_target_pairs={{0,6},{1,7},{2,4},{3,5},{4,2},{5,3},{6,0},{7,1},{8,14},{9,15},{10,... | collective-permute-start | bytes 36872 | tf_op jit(solution)/shard_map/ppermute | solution.py:460
  47.2 4.6 %collective-permute-start.8 = (f32[24,128]{1,0:T(8,128)S(1)}, f32[24,128]{1,0:T(8,128)S(1)}, u32[]{:S(2)}, u32[]{:S(2)}) collective-permute-start(f32[24,128]{1,0:T(8,128)S(1)} %solve.1), channel_id=1, source_target_pairs={{0,4},{1,5},{2,6},{3,7},{4,0},{5,1},{6,2},{7,3},{8,12},{9,13},{10,... | collective-permute-start | bytes 36872 | tf_op jit(solution)/shard_map/ppermute | solution.py:460
  47.9 4.2 %collective-permute-start.7 = (f32[24,128]{1,0:T(8,128)S(1)}, f32[24,128]{1,0:T(8,128)S(1)}, u32[]{:S(2)}, u32[]{:S(2)}) collective-permute-start(f32[24,128]{1,0:T(8,128)S(1)} %solve.1), channel_id=1, source_target_pairs={{0,2},{1,3},{2,0},{3,1},{4,6},{5,7},{6,4},{7,5},{8,10},{9,11},{10,... | collective-permute-start | bytes 36872 | tf_op jit(solution)/shard_map/ppermute | solution.py:460
  52.0 7.1 %collective-permute-start.12 = (f32[4,24,128]{2,1,0:T(8,128)S(1)}, f32[4,24,128]{2,1,0:T(8,128)S(1)}, u32[]{:S(2)}, u32[]{:S(2)}) collective-permute-start(f32[4,24,128]{2,1,0:T(8,128)S(1)} %pad_maximum_fusion), channel_id=1, source_target_pairs={{0,24},{8,16},{16,8},{24,0},{1,25},{9,17},{17,9},{25,1},{2,26},{10... | collective-permute-start | bytes 147464 | tf_op jit(solution)/shard_map/ppermute | solution.py:460
  53.5 5.6 %collective-permute-start.11 = (f32[4,24,128]{2,1,0:T(8,128)S(1)}, f32[4,24,128]{2,1,0:T(8,128)S(1)}, u32[]{:S(2)}, u32[]{:S(2)}) collective-permute-start(f32[4,24,128]{2,1,0:T(8,128)S(1)} %pad_maximum_fusion), channel_id=1, source_target_pairs={{0,16},{8,24},{16,0},{24,8},{1,17},{9,25},{17,1},{25,9},{2,18},{10... | collective-permute-start | bytes 147464 | tf_op jit(solution)/shard_map/ppermute | solution.py:460
  55.0 4.1 %collective-permute-start.10 = (f32[4,24,128]{2,1,0:T(8,128)S(1)}, f32[4,24,128]{2,1,0:T(8,128)S(1)}, u32[]{:S(2)}, u32[]{:S(2)}) collective-permute-start(f32[4,24,128]{2,1,0:T(8,128)S(1)} %pad_maximum_fusion), channel_id=1, source_target_pairs={{0,8},{8,0},{16,24},{24,16},{1,9},{9,1},{17,25},{25,17},{2,10},{10... | collective-permute-start | bytes 147464 | tf_op jit(solution)/shard_map/ppermute | solution.py:460
  59.1 2.2 %collective-permute-start.13 = (f32[16,24,128]{2,1,0:T(8,128)S(1)}, f32[16,24,128]{2,1,0:T(8,128)S(1)}, u32[]{:S(2)}, u32[]{:S(2)}) collective-permute-start(f32[16,24,128]{2,1,0:T(8,128)S(1)} %constant_dynamic-update-slice_fusion.pay_ref), channel_id=1, source_target_pairs={{0,1},{1,0},{2,3},{3,2},{4,5},{5,4},{6,7},{7,6},{8,9},{9,8},{10,11... | collective-permute-start | bytes 589832 | tf_op jit(solution)/shard_map/ppermute | solution.py:460

commit v7 on v6

--- a/solution.py
+++ b/solution.py
@@ -7,6 +7,7 @@
 from jax import lax
 from jax.experimental import pallas as pl
 from jax.experimental.pallas import tpu as pltpu
+from jax.sharding import Mesh
 from jax.sharding import PartitionSpec as P
 
 NFFT = 256
@@ -39,30 +40,26 @@
 
 class Plan:
     def __init__(self, grp, row):
-        self.grp, self.row, self.deep = grp, row, row // 2
+        self.grp, self.deep = grp, row // 2
         self.split_grp = NF % (grp * row) == 0
-        self.g_slots = grp if self.split_grp else 1
-        self.owners = row * self.g_slots
-        self.per = NF // self.owners
+        self.chips = self.deep * (grp if self.split_grp else 1)
+        self.chip_axes = ("grp", "z") if self.split_grp else ("z",)
+        self.per = NF // (2 * self.chips)
+
+    def chip(self):
+        z = lax.axis_index("z")
+        return lax.axis_index("grp") * self.deep + z if self.split_grp else z
+
+    def first_freq(self):
+        return (self.chip() * 2 + lax.axis_index("core")) * self.per
 
     def half(self, other_core):
-        row_index = lax.axis_index("row")
-        core = (row_index & 1) ^ int(other_core)
-        listed = []
-        for q in range(self.owners // 2):
-            owner = 2 * q + core
-            slot = ((owner % self.row) >> 1) ^ (row_index >> 1)
-            if self.split_grp:
-                slot = ((owner // self.row) ^ lax.axis_index("grp")) * self.deep + slot
-            for j in range(self.per):
-                listed.append((q * self.per + j, owner * self.per + j, slot))
-        return listed
-
-    def first_freq(self):
-        owner = lax.axis_index("row")
-        if self.split_grp:
-            owner = lax.axis_index("grp") * self.row + owner
-        return owner * self.per
+        core = lax.axis_index("core") ^ int(other_core)
+        return [
+            (chip, (2 * chip + core) * self.per + j)
+            for chip in range(self.chips)
+            for j in range(self.per)
+        ]
 
 
 def lane_index(shape):
@@ -85,13 +82,17 @@
     return jnp.where(left_half, first, second) + other
 
 
-def square(coefs):
-    return lax.dot_general(
-        coefs, coefs, (((1,), (1,)), ((), ())), preferred_element_type=jnp.float32
-    )
-
-
-def transform_kernel(plan, snap_ref, weight_ref, field_ref, table_ref, coef_ref, send_ref, flip, gram):
+def pack_half(plan, other_core, coef_ref, out_ref):
+    for n, (chip, f) in enumerate(plan.half(other_core)):
+        coefs = coef_ref[f]
+        whole = lax.dot_general(
+            coefs, coefs, (((1,), (1,)), ((), ())), preferred_element_type=jnp.float32
+        )
+        place = (plan.chip() ^ chip) * plan.per + n % plan.per
+        out_ref[place] = pack(whole[:NB], whole[NB:])
+
+
+def transform_kernel(plan, snap_ref, weight_ref, field_ref, table_ref, coef_ref, send_ref, flip):
     step = pl.program_id(0)
     tile = snap_ref.shape[1]
     pieces = tile // LANES
@@ -116,29 +117,19 @@
         flip[piece, pl.ds(NB - 1, NF, stride=PITCH), :] = jnp.broadcast_to(probe, (NF, LANES))
         flip[piece, pl.ds(2 * NB - 1, NF, stride=PITCH), :] = jnp.zeros((NF, LANES), jnp.float32)
 
-    @pl.when(step == 0)
-    def _():
-        gram[...] = jnp.zeros_like(gram)
-
-    def rounded(f):
+    def one_freq(f, carry):
         wide = jnp.concatenate(
             [flip[piece, pl.ds(f * PITCH, 2 * NB), :] for piece in range(pieces)], axis=1
         )
         coefs = wide.astype(jnp.bfloat16)
         coef_ref[f, :, here] = coefs
-        return coefs
-
-    def one_freq(f, carry):
-        rounded(f)
         return carry
 
     lax.fori_loop(0, NF, one_freq, 0, unroll=NF)
 
     @pl.when(step == pl.num_programs(0) - 1)
     def _():
-        for n, f, slot in plan.half(True):
-            whole = square(coef_ref[f])
-            send_ref[slot * plan.per + n % plan.per] = pack(whole[:NB], whole[NB:])
+        pack_half(plan, True, coef_ref, send_ref)
 
 
 def transform(plan, snapshots, weights, reference_field):
@@ -161,17 +152,14 @@
         ],
         scratch_shapes=[
             pltpu.VMEM((tile // LANES, NF * PITCH, LANES), jnp.float32),
-            pltpu.VMEM((half_freqs, 2 * NB, LANES), jnp.float32),
         ],
         compiler_params=pltpu.CompilerParams(vmem_limit_bytes=TRANSFORM_MIB * MIB),
         name="transform",
-    )(snapshots, weights[None], reference_field[None], dft_table())
+    )(snapshots, *(pltpu.with_memory_space_constraint(x, pltpu.HBM) for x in (weights[None], reference_field[None])), dft_table())
 
 
 def own_gram_kernel(plan, coef_ref, keep_ref):
-    for n, f, slot in plan.half(False):
-        whole = square(coef_ref[f])
-        keep_ref[slot * plan.per + n % plan.per] = pack(whole[:NB], whole[NB:])
+    pack_half(plan, False, coef_ref, keep_ref)
 
 
 def own_gram(plan, coeffs):
@@ -402,10 +390,10 @@
     left = lane8 < NB
     energies = jnp.zeros((NM, LANES), jnp.float32)
     copies = []
-    for n, f, slot in plan.half(other_core):
+    for n, (chip, f) in enumerate(plan.half(other_core)):
         j = n % plan.per
-        c = pay_ref[slot, j * NM : (j + 1) * NM]
-        extras = pay_ref[slot, plan.per * NM :]
+        c = pay_ref[chip, j * NM : (j + 1) * NM]
+        extras = pay_ref[chip, plan.per * NM :]
         factor_real = extras[:, 3 * j : 3 * j + 1]
         factor_imag = extras[:, 3 * j + 1 : 3 * j + 2]
         matrix = jnp.concatenate([jnp.where(left, c, -c), pltpu.roll(c, NB, 1)], axis=0)
@@ -444,7 +432,7 @@
         input_output_aliases={3: 0} if earlier else {},
         scratch_shapes=[
             pltpu.VMEM((NF // 2,) + whole.shape[1:], whole.dtype),
-            pltpu.SemaphoreType.DMA((plan.owners // 2,)),
+            pltpu.SemaphoreType.DMA((plan.chips,)),
         ],
         cost_estimate=pl.CostEstimate(
             flops=2 * NF * NM * 2 * NB * rows_here,
@@ -461,33 +449,29 @@
 
 
 def shards(plan, snapshots, weights, reference_field, start_basis):
-    total_rows = snapshots.shape[1] * plan.grp * plan.row
+    total_rows = snapshots.shape[1] * plan.grp * plan.deep * 2
     coeffs, send = transform(plan, snapshots, weights, reference_field)
     start_basis, send = lax.optimization_barrier((start_basis, send))
     start = start_rows(plan, start_basis)
 
-    arrived = swap(send, "row", plan.row, 1)
+    arrived = swap(send, "core", 2, 1)
     held = own_gram(plan, coeffs) + arrived
     if plan.split_grp:
         held = held.reshape((plan.grp, plan.deep * plan.per) + held.shape[1:])
-        arrived = [swap(held[d], "grp", plan.grp, d) for d in range(1, plan.grp)]
+        arrived = [
+            swap(held[d].astype(jnp.bfloat16), "grp", plan.grp, d).astype(jnp.float32) for d in range(1, plan.grp)
+        ]
         held = functools.reduce(jnp.add, arrived, held[0])
     held = held.reshape((plan.deep, plan.per) + held.shape[1:])
-    arrived = [swap(held[d], "row", plan.row, 2 * d) for d in range(1, plan.deep)]
+    arrived = [swap(held[d], "z", plan.deep, d) for d in range(1, plan.deep)]
     held = functools.reduce(jnp.add, arrived, held[0])
     if not plan.split_grp:
         held = lax.psum(held, "grp")
 
     payload = solve(plan, total_rows, held, start)
-
-    payload = jnp.stack(
-        [payload] + [swap(payload, "row", plan.row, 2 * d) for d in range(1, plan.deep)]
-    )
-    if plan.split_grp:
-        payload = jnp.concatenate(
-            [payload] + [swap(payload, "grp", plan.grp, d) for d in range(1, plan.grp)]
-        )
-    far = swap(payload, "row", plan.row, 1)
+    payload = jnp.broadcast_to(payload, (plan.chips,) + payload.shape)
+    payload = lax.all_to_all(payload, plan.chip_axes, 0, 0, tiled=True)
+    far = swap(payload, "core", 2, 1)
     own = modes(plan, coeffs, payload, weights)
     spod_modes, energies = modes(plan, coeffs, far, weights, own)
     return spod_modes, jnp.transpose(energies)
@@ -495,11 +479,13 @@
 
 def solution(mesh):
     plan = Plan(mesh.shape["grp"], mesh.shape["row"])
-    in_specs = (P(None, ("grp", "row")), P(("grp", "row")), P(("grp", "row")), P())
-    out_specs = (P(None, None, ("grp", "row")), P())
+    parted = Mesh(mesh.devices.reshape(plan.grp, plan.deep, 2), ("grp", "z", "core"))
+    rows = ("grp", "z", "core")
+    in_specs = (P(None, rows), P(rows), P(rows), P())
+    out_specs = (P(None, None, rows), P())
     return jax.shard_map(
         functools.partial(shards, plan),
-        mesh=mesh,
+        mesh=parted,
         in_specs=in_specs,
         out_specs=out_specs,
         check_vma=False,

time: 64.3 us -> 58.3 us (0.907)
  blocking collectives: 0 us -> 11.8 us
  waiting for transfers between devices: 18 us -> 9.79 us
  starting transfers between devices: 16.9 us -> 8.87 us
  local copies, waits for them, and re-layouts: 2.27 us -> 0.88 us
    all_to_all x0 -> x1, blocking collectives: none -> 11.8 us  [shards(): payload = lax.all_to_all(payload, plan.chip_axes, 0, 0, tiled=True)]
    ppermute x14 -> x8, waiting for transfers between devices: 18 us -> 9.79 us  [swap(): return lax.ppermute(x, axis, [(i, i ^ offset) for i in range(size)])]
    ppermute x14 -> x8, starting transfers between devices: 16.9 us -> 8.87 us  [swap(): return lax.ppermute(x, axis, [(i, i ^ offset) for i in range(size)])]
    unnamed x14 -> x6, local copies, waits for them, and re-layouts: 2.23 us -> 0.84 us
  transfers between devices with their start and end apart: 14 -> 8, of which waited for: 9 -> 5; matrix products, arithmetic and copies ran while one was open for 0% -> 0% of each run, Pallas kernels for 8% -> 8%
where the time goes in v7:
time: 58.3 us; the launch traced here: 58 us
  Pallas kernels  25.8 us (44%)
  blocking collectives  11.8 us (20%)
  waiting for transfers between devices  9.79 us (17%)
  starting transfers between devices  8.87 us (15%)
  local copies, waits for them, and re-layouts  0.88 us (2%)
  between operations  0.74 us (1%)
    pallas_call x1, Pallas kernels, transform(): pl.pallas_call(functools.partial(transform_kernel, plan), grid=(rows_here...  12.6 us
    all_to_all x1, blocking collectives, shards(): payload = lax.all_to_all(payload, plan.chip_axes, 0, 0, tiled=True)  11.8 us
    ppermute x8, waiting for transfers between devices, swap(): return lax.ppermute(x, axis, [(i, i ^ offset) for i in range(size)])  9.79 us
    ppermute x8, starting transfers between devices, swap(): return lax.ppermute(x, axis, [(i, i ^ offset) for i in range(size)])  8.87 us
    pallas_call x1, Pallas kernels, solve(): pl.pallas_call(functools.partial(solve_kernel, plan, total_rows), in_spec...  5.69 us
    pallas_call x2, Pallas kernels, modes(): pl.pallas_call(functools.partial(modes_kernel, plan, bool(earlier)), in_s...  4.74 us
    pallas_call x1, Pallas kernels, own_gram(): pl.pallas_call(functools.partial(own_gram_kernel, plan), in_specs=[pl.Blo...  2.41 us
  transfers between devices with their start and end apart: 8, of which 5 were waited for; matrix products, arithmetic and copies ran while one was open for 0% of the time, Pallas kernels for 8%

profile of v7, /device:TPU:0, one launch (start us, length us, event | category | flops | bytes accessed | tf_op | source)
XLA Modules:
  0.0 58.0 jit_solution(12504462078873460598)
XLA Ops:
  0.6 0.0 copy-start.1
  0.6 0.8 %copy-done.1 = bf16[128,256]{1,0:T(8,128)(2,1)S(1)} copy-done((bf16[128,256]{1,0:T(8,128)(2,1)S(1)}, bf16[128,256]{1,0:T(8,128)(2,1)}, u32[]{:S(2)}) %copy-start.1) | copy-done | bytes 65560
  1.5 0.0 copy-start
  1.5 0.0 copy-start.2
  1.5 12.6 %transform.1 = (bf16[64,128,1024]{2,1,0:T(8,128)(2,1)S(1)}, f32[32,32,128]{2,1,0:T(8,128)S(1)}) custom-call(bf16[8192,1024]{1,0:T(8,128)(2,1)} %snap_ref.1, f32[1,1024]{1,0:T(1,128)} %bitcast.5, f32[1,1024]{1,0:T(1,128)} %bitcast.8, bf16[128,256]{1,0:T(8,128)(2,1)S(1)} %copy-done.1), custom_call_target="tpu_custom_call" | custom-call | tf_op jit(solution)/shard_map/transform/pallas_call | solution.py:139
  14.1 0.5 collective-permute-start
  14.6 2.4 %own_gram.1 = f32[32,32,128]{2,1,0:T(8,128)S(1)} custom-call(bf16[64,128,1024]{2,1,0:T(8,128)(2,1)S(1)} %get-tuple-element.10.coef_ref), custom_call_target="tpu_custom_call" | custom-call | flops 1073741824 | bytes 8388608 | tf_op jit(solution)/shard_map/own_gram/pallas_call | solution.py:167
  17.1 0.0 collective-permute-done
  17.1 0.1 fusion.4
  17.2 2.6 %collective-permute-start.1 = (bf16[8,32,128]{2,1,0:T(8,128)(2,1)S(1)}, bf16[8,32,128]{2,1,0:T(8,128)(2,1)S(1)}, u32[]{:S(2)}, u32[]{:S(2)}) collective-permute-start(bf16[8,32,128]{2,1,0:T(8,128)(2,1)S(1)} %get-tuple-element.20), channel_id=1, source_target_pairs={{0,8},{8,0},{16,24},{24,16},{1,9},{9,1},{17,25},{25,17},{2,10},{10... | collective-permute-start | bytes 196616 | tf_op jit(solution)/shard_map/ppermute | solution.py:448
  19.8 1.5 %collective-permute-start.3 = (bf16[8,32,128]{2,1,0:T(8,128)(2,1)S(1)}, bf16[8,32,128]{2,1,0:T(8,128)(2,1)S(1)}, u32[]{:S(2)}, u32[]{:S(2)}) collective-permute-start(bf16[8,32,128]{2,1,0:T(8,128)(2,1)S(1)} %get-tuple-element.21), channel_id=1, source_target_pairs={{0,24},{8,16},{16,8},{24,0},{1,25},{9,17},{17,9},{25,1},{2,26},{10... | collective-permute-start | bytes 196616 | tf_op jit(solution)/shard_map/ppermute | solution.py:448
  21.3 0.1 collective-permute-start.2
  21.3 1.2 %collective-permute-done.1 = bf16[8,32,128]{2,1,0:T(8,128)(2,1)S(1)} collective-permute-done((bf16[8,32,128]{2,1,0:T(8,128)(2,1)S(1)}, bf16[8,32,128]{2,1,0:T(8,128)(2,1)S(1)}, u32[]{:S(2)}, u32[]{:S(2)}) %collective-permute-start.1) | collective-permute-done | bytes 65568 | tf_op jit(solution)/shard_map/ppermute | solution.py:448
  22.5 2.7 %collective-permute-done.3 = bf16[8,32,128]{2,1,0:T(8,128)(2,1)S(1)} collective-permute-done((bf16[8,32,128]{2,1,0:T(8,128)(2,1)S(1)}, bf16[8,32,128]{2,1,0:T(8,128)(2,1)S(1)}, u32[]{:S(2)}, u32[]{:S(2)}) %collective-permute-start.3) | collective-permute-done | bytes 65568 | tf_op jit(solution)/shard_map/ppermute | solution.py:448
  25.2 1.2 %collective-permute-done.2 = bf16[8,32,128]{2,1,0:T(8,128)(2,1)S(1)} collective-permute-done((bf16[8,32,128]{2,1,0:T(8,128)(2,1)S(1)}, bf16[8,32,128]{2,1,0:T(8,128)(2,1)S(1)}, u32[]{:S(2)}, u32[]{:S(2)}) %collective-permute-start.2) | collective-permute-done | bytes 65568 | tf_op jit(solution)/shard_map/ppermute | solution.py:448
  26.5 1.6 %collective-permute-start.4 = (f32[2,32,128]{2,1,0:T(8,128)S(1)}, f32[2,32,128]{2,1,0:T(8,128)S(1)}, u32[]{:S(2)}, u32[]{:S(2)}) collective-permute-start(f32[2,32,128]{2,1,0:T(8,128)S(1)} %get-tuple-element.23), channel_id=1, source_target_pairs={{0,2},{2,0},{4,6},{6,4},{1,3},{3,1},{5,7},{7,5},{8,10},{10,8},{12,... | collective-permute-start | bytes 98312 | tf_op jit(solution)/shard_map/ppermute | solution.py:448
  28.1 2.5 %collective-permute-start.6 = (f32[2,32,128]{2,1,0:T(8,128)S(1)}, f32[2,32,128]{2,1,0:T(8,128)S(1)}, u32[]{:S(2)}, u32[]{:S(2)}) collective-permute-start(f32[2,32,128]{2,1,0:T(8,128)S(1)} %get-tuple-element.24), channel_id=1, source_target_pairs={{0,6},{2,4},{4,2},{6,0},{1,7},{3,5},{5,3},{7,1},{8,14},{10,12},{12... | collective-permute-start | bytes 98312 | tf_op jit(solution)/shard_map/ppermute | solution.py:448
  30.6 0.1 collective-permute-start.5
  30.7 0.0 copy-done
  30.7 0.3 start_rows.1.start_ref
  31.0 0.0 collective-permute-done.4
  31.0 3.1 %collective-permute-done.6 = f32[2,32,128]{2,1,0:T(8,128)S(1)} collective-permute-done((f32[2,32,128]{2,1,0:T(8,128)S(1)}, f32[2,32,128]{2,1,0:T(8,128)S(1)}, u32[]{:S(2)}, u32[]{:S(2)}) %collective-permute-start.6) | collective-permute-done | bytes 32800 | tf_op jit(solution)/shard_map/ppermute | solution.py:448
  34.2 1.5 %collective-permute-done.5 = f32[2,32,128]{2,1,0:T(8,128)S(1)} collective-permute-done((f32[2,32,128]{2,1,0:T(8,128)S(1)}, f32[2,32,128]{2,1,0:T(8,128)S(1)}, u32[]{:S(2)}, u32[]{:S(2)}) %collective-permute-start.5) | collective-permute-done | bytes 32800 | tf_op jit(solution)/shard_map/ppermute | solution.py:448
  35.7 5.7 %solve.1 = f32[24,128]{1,0:T(8,128)S(1)} custom-call(f32[2,32,128]{2,1,0:T(8,128)S(1)} %fusion.3.packed_ref, f32[2,8,128]{2,1,0:T(8,128)S(1)} %start_rows.1.start_ref), custom_call_target="tpu_custom_call" | custom-call | tf_op jit(solution)/shard_map/solve/pallas_call | solution.py:375
  41.5 11.8 %all_to_all.5.pay_ref = f32[16,24,128]{2,1,0:T(8,128)S(1)} all-to-all(f32[16,24,128]{2,1,0:T(8,128)S(1)} %broadcast_in_dim.13), channel_id=1, replica_groups=mesh['grp'=4,'z'=4,'core'=2] {'grp','z'}, dimensions={0} | all-to-all | bytes 393216 | tf_op jit(solution)/shard_map/all_to_all | solution.py:473
  53.2 0.0 collective-permute-start.7
  53.2 0.0 copy-done.2
  53.3 2.1 %own_modes.1 = (f32[64,16,1024]{2,1,0:T(8,128)}, f32[8,64]{1,0:T(8,128)S(1)}) custom-call(bf16[64,128,1024]{2,1,0:T(8,128)(2,1)S(1)} %get-tuple-element.10.coef_ref, f32[16,24,128]{2,1,0:T(8,128)S(1)} %all_to_all.5.pay_ref, f32[1,1024]{1,0:T(1,128)S(1)} %bitcast.6), custom_call_target="tpu_custom_call" | custom-call | flops 134217728 | bytes 4194304 | tf_op jit(solution)/shard_map/own_modes/pallas_call | solution.py:426
  55.3 0.0 collective-permute-done.7.pay_ref
  55.3 2.7 %other_modes.1 = (f32[64,16,1024]{2,1,0:T(8,128)}, f32[8,64]{1,0:T(8,128)}) custom-call(bf16[64,128,1024]{2,1,0:T(8,128)(2,1)S(1)} %get-tuple-element.10.coef_ref, f32[16,24,128]{2,1,0:T(8,128)S(1)} %collective-permute-done.7.pay_ref, f32[1,1024]{1,0:T(1,128)S(1)} %bitcast.7, ...), custom_call_target="tpu_custom_call", output_to_operand_aliasing={{0}: (3, {})} | custom-call | flops 134217728 | bytes 4194304 | tf_op jit(solution)/shard_map/other_modes/pallas_call | solution.py:426
  (5 shorter events, 0.1 us)
Async XLA Ops:
  0.6 0.8 %copy-start.1 = (bf16[128,256]{1,0:T(8,128)(2,1)S(1)}, bf16[128,256]{1,0:T(8,128)(2,1)}, u32[]{:S(2)}) copy-start(bf16[128,256]{1,0:T(8,128)(2,1)} %constant.3.table_ref) | copy-start | bytes 196612
  1.5 29.2 %copy-start = (f32[64,2,63,8]{0,3,2,1:T(8,128)S(1)}, f32[64,2,63,8]{0,3,2,1:T(8,128)}, u32[]{:S(2)}) copy-start(f32[64,2,63,8]{0,3,2,1:T(8,128)} %param.8) | copy-start | bytes 774148
  1.5 51.8 %copy-start.2 = (f32[1024]{0:T(1024)S(1)}, f32[1024]{0:T(1024)}, u32[]{:S(2)}) copy-start(f32[1024]{0:T(1024)} %param.6) | copy-start | bytes 12292
  14.1 2.9 %collective-permute-start = (f32[32,32,128]{2,1,0:T(8,128)S(1)}, f32[32,32,128]{2,1,0:T(8,128)S(1)}, u32[]{:S(2)}, u32[]{:S(2)}) collective-permute-start(f32[32,32,128]{2,1,0:T(8,128)S(1)} %get-tuple-element.12), channel_id=1, source_target_pairs={{0,1},{1,0},{2,3},{3,2},{4,5},{5,4},{6,7},{7,6},{8,9},{9,8},{10,11... | collective-permute-start | bytes 1572872 | tf_op jit(solution)/shard_map/ppermute | solution.py:448
  17.2 5.3 %collective-permute-start.1 = (bf16[8,32,128]{2,1,0:T(8,128)(2,1)S(1)}, bf16[8,32,128]{2,1,0:T(8,128)(2,1)S(1)}, u32[]{:S(2)}, u32[]{:S(2)}) collective-permute-start(bf16[8,32,128]{2,1,0:T(8,128)(2,1)S(1)} %get-tuple-element.20), channel_id=1, source_target_pairs={{0,8},{8,0},{16,24},{24,16},{1,9},{9,1},{17,25},{25,17},{2,10},{10... | collective-permute-start | bytes 196616 | tf_op jit(solution)/shard_map/ppermute | solution.py:448
  19.8 5.5 %collective-permute-start.3 = (bf16[8,32,128]{2,1,0:T(8,128)(2,1)S(1)}, bf16[8,32,128]{2,1,0:T(8,128)(2,1)S(1)}, u32[]{:S(2)}, u32[]{:S(2)}) collective-permute-start(bf16[8,32,128]{2,1,0:T(8,128)(2,1)S(1)} %get-tuple-element.21), channel_id=1, source_target_pairs={{0,24},{8,16},{16,8},{24,0},{1,25},{9,17},{17,9},{25,1},{2,26},{10... | collective-permute-start | bytes 196616 | tf_op jit(solution)/shard_map/ppermute | solution.py:448
  21.3 5.2 %collective-permute-start.2 = (bf16[8,32,128]{2,1,0:T(8,128)(2,1)S(1)}, bf16[8,32,128]{2,1,0:T(8,128)(2,1)S(1)}, u32[]{:S(2)}, u32[]{:S(2)}) collective-permute-start(bf16[8,32,128]{2,1,0:T(8,128)(2,1)S(1)} %get-tuple-element.22), channel_id=1, source_target_pairs={{0,16},{8,24},{16,0},{24,8},{1,17},{9,25},{17,1},{25,9},{2,18},{10... | collective-permute-start | bytes 196616 | tf_op jit(solution)/shard_map/ppermute | solution.py:448
  26.5 4.6 %collective-permute-start.4 = (f32[2,32,128]{2,1,0:T(8,128)S(1)}, f32[2,32,128]{2,1,0:T(8,128)S(1)}, u32[]{:S(2)}, u32[]{:S(2)}) collective-permute-start(f32[2,32,128]{2,1,0:T(8,128)S(1)} %get-tuple-element.23), channel_id=1, source_target_pairs={{0,2},{2,0},{4,6},{6,4},{1,3},{3,1},{5,7},{7,5},{8,10},{10,8},{12,... | collective-permute-start | bytes 98312 | tf_op jit(solution)/shard_map/ppermute | solution.py:448
  28.1 6.1 %collective-permute-start.6 = (f32[2,32,128]{2,1,0:T(8,128)S(1)}, f32[2,32,128]{2,1,0:T(8,128)S(1)}, u32[]{:S(2)}, u32[]{:S(2)}) collective-permute-start(f32[2,32,128]{2,1,0:T(8,128)S(1)} %get-tuple-element.24), channel_id=1, source_target_pairs={{0,6},{2,4},{4,2},{6,0},{1,7},{3,5},{5,3},{7,1},{8,14},{10,12},{12... | collective-permute-start | bytes 98312 | tf_op jit(solution)/shard_map/ppermute | solution.py:448
  30.6 5.2 %collective-permute-start.5 = (f32[2,32,128]{2,1,0:T(8,128)S(1)}, f32[2,32,128]{2,1,0:T(8,128)S(1)}, u32[]{:S(2)}, u32[]{:S(2)}) collective-permute-start(f32[2,32,128]{2,1,0:T(8,128)S(1)} %get-tuple-element.25), channel_id=1, source_target_pairs={{0,4},{2,6},{4,0},{6,2},{1,5},{3,7},{5,1},{7,3},{8,12},{10,14},{12... | collective-permute-start | bytes 98312 | tf_op jit(solution)/shard_map/ppermute | solution.py:448
  53.2 2.1 %collective-permute-start.7 = (f32[16,24,128]{2,1,0:T(8,128)S(1)}, f32[16,24,128]{2,1,0:T(8,128)S(1)}, u32[]{:S(2)}, u32[]{:S(2)}) collective-permute-start(f32[16,24,128]{2,1,0:T(8,128)S(1)} %all_to_all.5.pay_ref), channel_id=1, source_target_pairs={{0,1},{1,0},{2,3},{3,2},{4,5},{5,4},{6,7},{7,6},{8,9},{9,8},{10,11... | collective-permute-start | bytes 589832 | tf_op jit(solution)/shard_map/ppermute | solution.py:448

commit v8 on v7

--- a/solution.py
+++ b/solution.py
@@ -45,6 +45,7 @@
         self.chips = self.deep * (grp if self.split_grp else 1)
         self.chip_axes = ("grp", "z") if self.split_grp else ("z",)
         self.per = NF // (2 * self.chips)
+        self.near = self.deep if self.split_grp else 1
 
     def chip(self):
         z = lax.axis_index("z")
@@ -82,17 +83,19 @@
     return jnp.where(left_half, first, second) + other
 
 
-def pack_half(plan, other_core, coef_ref, out_ref):
-    for n, (chip, f) in enumerate(plan.half(other_core)):
-        coefs = coef_ref[f]
-        whole = lax.dot_general(
-            coefs, coefs, (((1,), (1,)), ((), ())), preferred_element_type=jnp.float32
-        )
-        place = (plan.chip() ^ chip) * plan.per + n % plan.per
-        out_ref[place] = pack(whole[:NB], whole[NB:])
-
-
-def transform_kernel(plan, snap_ref, weight_ref, field_ref, table_ref, coef_ref, send_ref, flip):
+def pack_some(plan, other_core, offsets, coef_ref, out_ref):
+    core = lax.axis_index("core") ^ int(other_core)
+    for n, offset in enumerate(offsets):
+        first = (2 * (plan.chip() ^ offset) + core) * plan.per
+        for j in range(plan.per):
+            coefs = coef_ref[first + j]
+            whole = lax.dot_general(
+                coefs, coefs, (((1,), (1,)), ((), ())), preferred_element_type=jnp.float32
+            )
+            out_ref[n * plan.per + j] = pack(whole[:NB], whole[NB:])
+
+
+def transform_kernel(plan, table_ref, weight_ref, field_ref, snap_ref, coef_ref, send_ref, flip):
     step = pl.program_id(0)
     tile = snap_ref.shape[1]
     pieces = tile // LANES
@@ -129,51 +132,57 @@
 
     @pl.when(step == pl.num_programs(0) - 1)
     def _():
-        pack_half(plan, True, coef_ref, send_ref)
+        pack_some(plan, True, range(plan.chips), coef_ref, send_ref)
 
 
 def transform(plan, snapshots, weights, reference_field):
     rows_here = snapshots.shape[1]
     tile = min(256, rows_here)
-    half_freqs = NF // 2
+    small = [
+        pltpu.with_memory_space_constraint(x, pltpu.HBM)
+        for x in (dft_table(), weights[None], reference_field[None])
+    ]
     return pl.pallas_call(
         functools.partial(transform_kernel, plan),
         grid=(rows_here // tile,),
         in_specs=[
-            pl.BlockSpec((snapshots.shape[0], tile), lambda i: (0, i)),
+            pl.BlockSpec((2 * NF, NFFT), lambda i: (0, 0)),
             pl.BlockSpec((1, tile), lambda i: (0, i)),
             pl.BlockSpec((1, tile), lambda i: (0, i)),
-            pl.BlockSpec((2 * NF, NFFT), lambda i: (0, 0)),
+            pl.BlockSpec((snapshots.shape[0], tile), lambda i: (0, i)),
         ],
         out_specs=[pl.BlockSpec(memory_space=pltpu.VMEM)] * 2,
         out_shape=[
             jax.ShapeDtypeStruct((NF, 2 * NB, rows_here), jnp.bfloat16),
-            jax.ShapeDtypeStruct((half_freqs, NB // 2, LANES), jnp.float32),
+            packed_shape(plan, plan.chips),
         ],
         scratch_shapes=[
             pltpu.VMEM((tile // LANES, NF * PITCH, LANES), jnp.float32),
         ],
         compiler_params=pltpu.CompilerParams(vmem_limit_bytes=TRANSFORM_MIB * MIB),
         name="transform",
-    )(snapshots, *(pltpu.with_memory_space_constraint(x, pltpu.HBM) for x in (weights[None], reference_field[None])), dft_table())
-
-
-def own_gram_kernel(plan, coef_ref, keep_ref):
-    pack_half(plan, False, coef_ref, keep_ref)
-
-
-def own_gram(plan, coeffs):
-    freqs, rows, columns = coeffs.shape
+    )(*small, snapshots)
+
+
+def packed_shape(plan, chips):
+    return jax.ShapeDtypeStruct((chips * plan.per, NB // 2, LANES), jnp.float32)
+
+
+def grams(plan, coeffs, other_core, offsets, name):
+    _, rows, columns = coeffs.shape
+    freqs = plan.per * len(offsets)
     return pl.pallas_call(
-        functools.partial(own_gram_kernel, plan),
+        functools.partial(pack_some, plan, other_core, offsets),
         in_specs=[pl.BlockSpec(memory_space=pltpu.VMEM)],
         out_specs=pl.BlockSpec(memory_space=pltpu.VMEM),
-        out_shape=jax.ShapeDtypeStruct((NF // 2, NB // 2, LANES), jnp.float32),
+        out_shape=packed_shape(plan, len(offsets)),
         cost_estimate=pl.CostEstimate(
-            flops=freqs * rows * rows * columns, bytes_accessed=freqs * rows * columns, transcendentals=0
+            flops=2 * freqs * rows * rows * columns,
+            bytes_accessed=2 * freqs * rows * columns,
+            transcendentals=0,
         ),
         compiler_params=pltpu.CompilerParams(vmem_limit_bytes=SOLVE_MIB * MIB),
-        name="own_gram",
+        name=name,
     )(coeffs)
 
 
@@ -455,17 +464,25 @@
     start = start_rows(plan, start_basis)
 
     arrived = swap(send, "core", 2, 1)
-    held = own_gram(plan, coeffs) + arrived
+    mine, near = arrived[: plan.near * plan.per], range(plan.near)
+    own = grams(plan, coeffs, False, range(plan.near, plan.chips), "own_gram")
+    held = own + arrived[plan.near * plan.per :]
+    late, held = lax.optimization_barrier((coeffs, held))
     if plan.split_grp:
-        held = held.reshape((plan.grp, plan.deep * plan.per) + held.shape[1:])
+        held = held.reshape((plan.grp - 1, plan.deep * plan.per) + held.shape[1:])
         arrived = [
-            swap(held[d].astype(jnp.bfloat16), "grp", plan.grp, d).astype(jnp.float32) for d in range(1, plan.grp)
+            swap(held[d - 1].astype(jnp.bfloat16), "grp", plan.grp, d).astype(jnp.float32)
+            for d in range(1, plan.grp)
         ]
+    else:
+        held = held.reshape((plan.deep - 1, plan.per) + held.shape[1:])
+        arrived = [swap(held[d - 1], "z", plan.deep, d) for d in range(1, plan.deep)]
+    held = functools.reduce(jnp.add, arrived, grams(plan, late, False, near, "near_gram") + mine)
+    if plan.split_grp:
+        held = held.reshape((plan.deep, plan.per) + held.shape[1:])
+        arrived = [swap(held[d], "z", plan.deep, d) for d in range(1, plan.deep)]
         held = functools.reduce(jnp.add, arrived, held[0])
-    held = held.reshape((plan.deep, plan.per) + held.shape[1:])
-    arrived = [swap(held[d], "z", plan.deep, d) for d in range(1, plan.deep)]
-    held = functools.reduce(jnp.add, arrived, held[0])
-    if not plan.split_grp:
+    else:
         held = lax.psum(held, "grp")
 
     payload = solve(plan, total_rows, held, start)

time: 58.3 us -> 55.7 us (0.955)
  blocking collectives: 11.8 us -> 10.7 us
  local copies, waits for them, and re-layouts: 0.88 us -> 0.05 us
  waiting for transfers between devices: 9.79 us -> 9.06 us
    all_to_all x1, blocking collectives: 11.8 us -> 10.7 us  [shards(): payload = lax.all_to_all(payload, plan.chip_axes, 0, 0, tiled=True)]
    unnamed x6 -> x4, local copies, waits for them, and re-layouts: 0.84 us -> 0.01 us
    ppermute x8, waiting for transfers between devices: 9.79 us -> 9.06 us  [swap(): return lax.ppermute(x, axis, [(i, i ^ offset) for i in range(size)])]
    pallas_call x1 -> x2, Pallas kernels: 2.41 us -> 2.64 us  [grams(): pl.pallas_call(functools.partial(pack_some, plan, other_core, offsets), i...]
  transfers between devices with their start and end apart: 8 -> 8, of which waited for: 5 -> 5; matrix products, arithmetic and copies ran while one was open for 0% -> 0% of each run, Pallas kernels for 8% -> 9%
where the time goes in v8:
time: 55.7 us; the launch traced here: 55.5 us
  Pallas kernels  26 us (47%)
  blocking collectives  10.7 us (19%)
  waiting for transfers between devices  9.06 us (16%)
  starting transfers between devices  8.9 us (16%)
  between operations  0.73 us (1%)
    pallas_call x1, Pallas kernels, transform(): pl.pallas_call(functools.partial(transform_kernel, plan), grid=(rows_here...  12.6 us
    all_to_all x1, blocking collectives, shards(): payload = lax.all_to_all(payload, plan.chip_axes, 0, 0, tiled=True)  10.7 us
    ppermute x8, waiting for transfers between devices, swap(): return lax.ppermute(x, axis, [(i, i ^ offset) for i in range(size)])  9.06 us
    ppermute x8, starting transfers between devices, swap(): return lax.ppermute(x, axis, [(i, i ^ offset) for i in range(size)])  8.9 us
    pallas_call x1, Pallas kernels, solve(): pl.pallas_call(functools.partial(solve_kernel, plan, total_rows), in_spec...  5.69 us
    pallas_call x2, Pallas kernels, modes(): pl.pallas_call(functools.partial(modes_kernel, plan, bool(earlier)), in_s...  4.74 us
    pallas_call x2, Pallas kernels, grams(): pl.pallas_call(functools.partial(pack_some, plan, other_core, offsets), i...  2.64 us
  transfers between devices with their start and end apart: 8, of which 5 were waited for; matrix products, arithmetic and copies ran while one was open for 0% of the time, Pallas kernels for 9%

profile of v8, /device:TPU:0, one launch (start us, length us, event | category | flops | bytes accessed | tf_op | source)
XLA Modules:
  0.0 55.5 jit_solution(2815616250028948039)
XLA Ops:
  0.6 12.6 %transform.1 = (bf16[64,128,1024]{2,1,0:T(8,128)(2,1)S(1)}, f32[32,32,128]{2,1,0:T(8,128)S(1)}) custom-call(bf16[128,256]{1,0:T(8,128)(2,1)} %constant.3.table_ref, f32[1,1024]{1,0:T(1,128)} %bitcast.5, f32[1,1024]{1,0:T(1,128)} %bitcast.8, bf16[8192,1024]{1,0:T(8,128)(2,1)} %snap_ref.1), custom_call_target="tpu_custom_call" | custom-call | tf_op jit(solution)/shard_map/transform/pallas_call | solution.py:145
  13.2 0.5 collective-permute-start
  13.7 0.0 copy-start
  13.7 0.0 copy-start.1
  13.7 1.9 %own_gram.1 = f32[24,32,128]{2,1,0:T(8,128)S(1)} custom-call(bf16[64,128,1024]{2,1,0:T(8,128)(2,1)S(1)} %get-tuple-element.15.coef_ref), custom_call_target="tpu_custom_call" | custom-call | flops 805306368 | bytes 6291456 | tf_op jit(solution)/shard_map/own_gram/pallas_call | solution.py:174
  15.6 0.0 collective-permute-done
  15.6 0.1 slice_add_fusion
  15.7 2.6 %collective-permute-start.1 = (bf16[8,32,128]{2,1,0:T(8,128)(2,1)S(1)}, bf16[8,32,128]{2,1,0:T(8,128)(2,1)S(1)}, u32[]{:S(2)}, u32[]{:S(2)}) collective-permute-start(bf16[8,32,128]{2,1,0:T(8,128)(2,1)S(1)} %get-tuple-element.22), channel_id=1, source_target_pairs={{0,8},{8,0},{16,24},{24,16},{1,9},{9,1},{17,25},{25,17},{2,10},{10... | collective-permute-start | bytes 196616 | tf_op jit(solution)/shard_map/ppermute | solution.py:457
  18.3 1.5 %collective-permute-start.2 = (bf16[8,32,128]{2,1,0:T(8,128)(2,1)S(1)}, bf16[8,32,128]{2,1,0:T(8,128)(2,1)S(1)}, u32[]{:S(2)}, u32[]{:S(2)}) collective-permute-start(bf16[8,32,128]{2,1,0:T(8,128)(2,1)S(1)} %get-tuple-element.23), channel_id=1, source_target_pairs={{0,16},{8,24},{16,0},{24,8},{1,17},{9,25},{17,1},{25,9},{2,18},{10... | collective-permute-start | bytes 196616 | tf_op jit(solution)/shard_map/ppermute | solution.py:457
  19.8 0.0 collective-permute-start.3
  19.8 0.8 %near_gram.1 = f32[8,32,128]{2,1,0:T(8,128)S(1)} custom-call(bf16[64,128,1024]{2,1,0:T(8,128)(2,1)S(1)} %get-tuple-element.15.coef_ref), custom_call_target="tpu_custom_call" | custom-call | flops 268435456 | bytes 2097152 | tf_op jit(solution)/shard_map/near_gram/pallas_call | solution.py:174
  20.6 0.4 collective-permute-done.1
  21.0 1.5 %collective-permute-done.2 = bf16[8,32,128]{2,1,0:T(8,128)(2,1)S(1)} collective-permute-done((bf16[8,32,128]{2,1,0:T(8,128)(2,1)S(1)}, bf16[8,32,128]{2,1,0:T(8,128)(2,1)S(1)}, u32[]{:S(2)}, u32[]{:S(2)}) %collective-permute-start.2) | collective-permute-done | bytes 65568 | tf_op jit(solution)/shard_map/ppermute | solution.py:457
  22.6 2.4 %collective-permute-done.3 = bf16[8,32,128]{2,1,0:T(8,128)(2,1)S(1)} collective-permute-done((bf16[8,32,128]{2,1,0:T(8,128)(2,1)S(1)}, bf16[8,32,128]{2,1,0:T(8,128)(2,1)S(1)}, u32[]{:S(2)}, u32[]{:S(2)}) %collective-permute-start.3) | collective-permute-done | bytes 65568 | tf_op jit(solution)/shard_map/ppermute | solution.py:457
  25.0 1.6 %collective-permute-start.4 = (f32[2,32,128]{2,1,0:T(8,128)S(1)}, f32[2,32,128]{2,1,0:T(8,128)S(1)}, u32[]{:S(2)}, u32[]{:S(2)}) collective-permute-start(f32[2,32,128]{2,1,0:T(8,128)S(1)} %get-tuple-element.25), channel_id=1, source_target_pairs={{0,2},{2,0},{4,6},{6,4},{1,3},{3,1},{5,7},{7,5},{8,10},{10,8},{12,... | collective-permute-start | bytes 98312 | tf_op jit(solution)/shard_map/ppermute | solution.py:457
  26.7 2.5 %collective-permute-start.6 = (f32[2,32,128]{2,1,0:T(8,128)S(1)}, f32[2,32,128]{2,1,0:T(8,128)S(1)}, u32[]{:S(2)}, u32[]{:S(2)}) collective-permute-start(f32[2,32,128]{2,1,0:T(8,128)S(1)} %get-tuple-element.26), channel_id=1, source_target_pairs={{0,6},{2,4},{4,2},{6,0},{1,7},{3,5},{5,3},{7,1},{8,14},{10,12},{12... | collective-permute-start | bytes 98312 | tf_op jit(solution)/shard_map/ppermute | solution.py:457
  29.2 0.1 collective-permute-start.5
  29.3 0.0 copy-done
  29.3 0.3 start_rows.1.start_ref
  29.6 0.0 collective-permute-done.4
  29.6 2.8 %collective-permute-done.6 = f32[2,32,128]{2,1,0:T(8,128)S(1)} collective-permute-done((f32[2,32,128]{2,1,0:T(8,128)S(1)}, f32[2,32,128]{2,1,0:T(8,128)S(1)}, u32[]{:S(2)}, u32[]{:S(2)}) %collective-permute-start.6) | collective-permute-done | bytes 32800 | tf_op jit(solution)/shard_map/ppermute | solution.py:457
  32.4 1.9 %collective-permute-done.5 = f32[2,32,128]{2,1,0:T(8,128)S(1)} collective-permute-done((f32[2,32,128]{2,1,0:T(8,128)S(1)}, f32[2,32,128]{2,1,0:T(8,128)S(1)}, u32[]{:S(2)}, u32[]{:S(2)}) %collective-permute-start.5) | collective-permute-done | bytes 32800 | tf_op jit(solution)/shard_map/ppermute | solution.py:457
  34.3 5.7 %solve.1 = f32[24,128]{1,0:T(8,128)S(1)} custom-call(f32[2,32,128]{2,1,0:T(8,128)S(1)} %fusion.4.packed_ref, f32[2,8,128]{2,1,0:T(8,128)S(1)} %start_rows.1.start_ref), custom_call_target="tpu_custom_call" | custom-call | tf_op jit(solution)/shard_map/solve/pallas_call | solution.py:384
  40.1 10.7 %all_to_all.5.pay_ref = f32[16,24,128]{2,1,0:T(8,128)S(1)} all-to-all(f32[16,24,128]{2,1,0:T(8,128)S(1)} %broadcast_in_dim.13), channel_id=1, replica_groups=mesh['grp'=4,'z'=4,'core'=2] {'grp','z'}, dimensions={0} | all-to-all | bytes 393216 | tf_op jit(solution)/shard_map/all_to_all | solution.py:490
  50.7 0.0 collective-permute-start.7
  50.7 0.0 copy-done.1
  50.7 2.1 %own_modes.1 = (f32[64,16,1024]{2,1,0:T(8,128)}, f32[8,64]{1,0:T(8,128)S(1)}) custom-call(bf16[64,128,1024]{2,1,0:T(8,128)(2,1)S(1)} %get-tuple-element.15.coef_ref, f32[16,24,128]{2,1,0:T(8,128)S(1)} %all_to_all.5.pay_ref, f32[1,1024]{1,0:T(1,128)S(1)} %bitcast.6), custom_call_target="tpu_custom_call" | custom-call | flops 134217728 | bytes 4194304 | tf_op jit(solution)/shard_map/own_modes/pallas_call | solution.py:435
  52.8 0.0 collective-permute-done.7.pay_ref
  52.8 2.7 %other_modes.1 = (f32[64,16,1024]{2,1,0:T(8,128)}, f32[8,64]{1,0:T(8,128)}) custom-call(bf16[64,128,1024]{2,1,0:T(8,128)(2,1)S(1)} %get-tuple-element.15.coef_ref, f32[16,24,128]{2,1,0:T(8,128)S(1)} %collective-permute-done.7.pay_ref, f32[1,1024]{1,0:T(1,128)S(1)} %bitcast.7, ...), custom_call_target="tpu_custom_call", output_to_operand_aliasing={{0}: (3, {})} | custom-call | flops 134217728 | bytes 4194304 | tf_op jit(solution)/shard_map/other_modes/pallas_call | solution.py:435
  (5 shorter events, 0.1 us)
Async XLA Ops:
  13.2 2.4 %collective-permute-start = (f32[32,32,128]{2,1,0:T(8,128)S(1)}, f32[32,32,128]{2,1,0:T(8,128)S(1)}, u32[]{:S(2)}, u32[]{:S(2)}) collective-permute-start(f32[32,32,128]{2,1,0:T(8,128)S(1)} %get-tuple-element.14), channel_id=1, source_target_pairs={{0,1},{1,0},{2,3},{3,2},{4,5},{5,4},{6,7},{7,6},{8,9},{9,8},{10,11... | collective-permute-start | bytes 1572872 | tf_op jit(solution)/shard_map/ppermute | solution.py:457
  13.7 15.6 %copy-start = (f32[64,2,63,8]{0,3,2,1:T(8,128)S(1)}, f32[64,2,63,8]{0,3,2,1:T(8,128)}, u32[]{:S(2)}) copy-start(f32[64,2,63,8]{0,3,2,1:T(8,128)} %param.8) | copy-start | bytes 774148
  13.7 37.0 %copy-start.1 = (f32[1024]{0:T(1024)S(1)}, f32[1024]{0:T(1024)}, u32[]{:S(2)}) copy-start(f32[1024]{0:T(1024)} %param.6) | copy-start | bytes 12292
  15.7 5.3 %collective-permute-start.1 = (bf16[8,32,128]{2,1,0:T(8,128)(2,1)S(1)}, bf16[8,32,128]{2,1,0:T(8,128)(2,1)S(1)}, u32[]{:S(2)}, u32[]{:S(2)}) collective-permute-start(bf16[8,32,128]{2,1,0:T(8,128)(2,1)S(1)} %get-tuple-element.22), channel_id=1, source_target_pairs={{0,8},{8,0},{16,24},{24,16},{1,9},{9,1},{17,25},{25,17},{2,10},{10... | collective-permute-start | bytes 196616 | tf_op jit(solution)/shard_map/ppermute | solution.py:457
  18.3 4.3 %collective-permute-start.2 = (bf16[8,32,128]{2,1,0:T(8,128)(2,1)S(1)}, bf16[8,32,128]{2,1,0:T(8,128)(2,1)S(1)}, u32[]{:S(2)}, u32[]{:S(2)}) collective-permute-start(bf16[8,32,128]{2,1,0:T(8,128)(2,1)S(1)} %get-tuple-element.23), channel_id=1, source_target_pairs={{0,16},{8,24},{16,0},{24,8},{1,17},{9,25},{17,1},{25,9},{2,18},{10... | collective-permute-start | bytes 196616 | tf_op jit(solution)/shard_map/ppermute | solution.py:457
  19.8 5.2 %collective-permute-start.3 = (bf16[8,32,128]{2,1,0:T(8,128)(2,1)S(1)}, bf16[8,32,128]{2,1,0:T(8,128)(2,1)S(1)}, u32[]{:S(2)}, u32[]{:S(2)}) collective-permute-start(bf16[8,32,128]{2,1,0:T(8,128)(2,1)S(1)} %get-tuple-element.24), channel_id=1, source_target_pairs={{0,24},{8,16},{16,8},{24,0},{1,25},{9,17},{17,9},{25,1},{2,26},{10... | collective-permute-start | bytes 196616 | tf_op jit(solution)/shard_map/ppermute | solution.py:457
  25.0 4.6 %collective-permute-start.4 = (f32[2,32,128]{2,1,0:T(8,128)S(1)}, f32[2,32,128]{2,1,0:T(8,128)S(1)}, u32[]{:S(2)}, u32[]{:S(2)}) collective-permute-start(f32[2,32,128]{2,1,0:T(8,128)S(1)} %get-tuple-element.25), channel_id=1, source_target_pairs={{0,2},{2,0},{4,6},{6,4},{1,3},{3,1},{5,7},{7,5},{8,10},{10,8},{12,... | collective-permute-start | bytes 98312 | tf_op jit(solution)/shard_map/ppermute | solution.py:457
  26.7 5.7 %collective-permute-start.6 = (f32[2,32,128]{2,1,0:T(8,128)S(1)}, f32[2,32,128]{2,1,0:T(8,128)S(1)}, u32[]{:S(2)}, u32[]{:S(2)}) collective-permute-start(f32[2,32,128]{2,1,0:T(8,128)S(1)} %get-tuple-element.26), channel_id=1, source_target_pairs={{0,6},{2,4},{4,2},{6,0},{1,7},{3,5},{5,3},{7,1},{8,14},{10,12},{12... | collective-permute-start | bytes 98312 | tf_op jit(solution)/shard_map/ppermute | solution.py:457
  29.2 5.2 %collective-permute-start.5 = (f32[2,32,128]{2,1,0:T(8,128)S(1)}, f32[2,32,128]{2,1,0:T(8,128)S(1)}, u32[]{:S(2)}, u32[]{:S(2)}) collective-permute-start(f32[2,32,128]{2,1,0:T(8,128)S(1)} %get-tuple-element.27), channel_id=1, source_target_pairs={{0,4},{2,6},{4,0},{6,2},{1,5},{3,7},{5,1},{7,3},{8,12},{10,14},{12... | collective-permute-start | bytes 98312 | tf_op jit(solution)/shard_map/ppermute | solution.py:457
  50.7 2.1 %collective-permute-start.7 = (f32[16,24,128]{2,1,0:T(8,128)S(1)}, f32[16,24,128]{2,1,0:T(8,128)S(1)}, u32[]{:S(2)}, u32[]{:S(2)}) collective-permute-start(f32[16,24,128]{2,1,0:T(8,128)S(1)} %all_to_all.5.pay_ref), channel_id=1, source_target_pairs={{0,1},{1,0},{2,3},{3,2},{4,5},{5,4},{6,7},{7,6},{8,9},{9,8},{10,11... | collective-permute-start | bytes 589832 | tf_op jit(solution)/shard_map/ppermute | solution.py:457

commit v9 on v8

--- a/solution.py
+++ b/solution.py
@@ -262,13 +262,14 @@
         v = jnp.where(row == j, pivot * lax.rsqrt(size), v)
         if j < NM - 1:
             inverse = 1.0 / size
-            scale = (size + EPS) * inverse * inverse
-            scaled_real, scaled_imag = real[j] * scale, imag[j] * scale
+            scale = (1.0 + EPS * inverse) * inverse
             for l in range(j + 1, NM):
                 other_real, other_imag = spread(real[j], l), spread(imag[j], l)
-                real[l] = real[l] - (scaled_real * other_real + scaled_imag * other_imag)
+                both = real[j] * other_real + imag[j] * other_imag
+                real[l] = real[l] - scale * both
                 if l < NM - 1:
-                    imag[l] = imag[l] - (scaled_imag * other_real - scaled_real * other_imag)
+                    cross = imag[j] * other_real - real[j] * other_imag
+                    imag[l] = imag[l] - scale * cross
             a = jnp.where(row > j, real[j] * inverse, 0.0)
             c = jnp.where(row > j, imag[j] * inverse, 0.0)
             y, turned = (
@@ -353,7 +354,7 @@
         return tuple(orthonormalize_checked(y, turned) for y, turned in images)
 
     basis, worst = lax.fori_loop(
-        0, ITERS, quick_sweep, (start, jnp.ones((NM, LANES), jnp.float32))
+        0, ITERS, quick_sweep, (start, jnp.ones((NM, LANES), jnp.float32)), unroll=4
     )
     for i, v in enumerate(basis):
         basis_ref[i] = v

time: 55.7 us -> 55.1 us (0.989)
  Pallas kernels: 26 us -> 25.3 us
    pallas_call x1, Pallas kernels: 5.69 us -> 5.01 us  [solve(): pl.pallas_call(functools.partial(solve_kernel, plan, total_rows), in_spec...]
where the time goes in v9:
time: 55.1 us; the launch traced here: 54.8 us
  Pallas kernels  25.3 us (46%)
  blocking collectives  10.7 us (19%)
  waiting for transfers between devices  9.06 us (16%)
  starting transfers between devices  8.9 us (16%)
  between operations  0.73 us (1%)
    pallas_call x1, Pallas kernels, transform(): pl.pallas_call(functools.partial(transform_kernel, plan), grid=(rows_here...  12.6 us
    all_to_all x1, blocking collectives, shards(): payload = lax.all_to_all(payload, plan.chip_axes, 0, 0, tiled=True)  10.7 us
    ppermute x8, waiting for transfers between devices, swap(): return lax.ppermute(x, axis, [(i, i ^ offset) for i in range(size)])  9.06 us
    ppermute x8, starting transfers between devices, swap(): return lax.ppermute(x, axis, [(i, i ^ offset) for i in range(size)])  8.9 us
    pallas_call x1, Pallas kernels, solve(): pl.pallas_call(functools.partial(solve_kernel, plan, total_rows), in_spec...  5.01 us
    pallas_call x2, Pallas kernels, modes(): pl.pallas_call(functools.partial(modes_kernel, plan, bool(earlier)), in_s...  4.74 us
    pallas_call x2, Pallas kernels, grams(): pl.pallas_call(functools.partial(pack_some, plan, other_core, offsets), i...  2.64 us
  transfers between devices with their start and end apart: 8, of which 5 were waited for; matrix products, arithmetic and copies ran while one was open for 0% of the time, Pallas kernels for 9%

profile of v9, /device:TPU:0, one launch (start us, length us, event | category | flops | bytes accessed | tf_op | source)
XLA Modules:
  0.0 54.8 jit_solution(17724235832802523548)
XLA Ops:
  0.6 12.6 %transform.1 = (bf16[64,128,1024]{2,1,0:T(8,128)(2,1)S(1)}, f32[32,32,128]{2,1,0:T(8,128)S(1)}) custom-call(bf16[128,256]{1,0:T(8,128)(2,1)} %constant.3.table_ref, f32[1,1024]{1,0:T(1,128)} %bitcast.5, f32[1,1024]{1,0:T(1,128)} %bitcast.8, bf16[8192,1024]{1,0:T(8,128)(2,1)} %snap_ref.1), custom_call_target="tpu_custom_call" | custom-call | tf_op jit(solution)/shard_map/transform/pallas_call | solution.py:145
  13.2 0.5 collective-permute-start
  13.7 0.0 copy-start
  13.7 0.0 copy-start.1
  13.7 1.9 %own_gram.1 = f32[24,32,128]{2,1,0:T(8,128)S(1)} custom-call(bf16[64,128,1024]{2,1,0:T(8,128)(2,1)S(1)} %get-tuple-element.15.coef_ref), custom_call_target="tpu_custom_call" | custom-call | flops 805306368 | bytes 6291456 | tf_op jit(solution)/shard_map/own_gram/pallas_call | solution.py:174
  15.6 0.0 collective-permute-done
  15.6 0.1 slice_add_fusion
  15.7 2.6 %collective-permute-start.1 = (bf16[8,32,128]{2,1,0:T(8,128)(2,1)S(1)}, bf16[8,32,128]{2,1,0:T(8,128)(2,1)S(1)}, u32[]{:S(2)}, u32[]{:S(2)}) collective-permute-start(bf16[8,32,128]{2,1,0:T(8,128)(2,1)S(1)} %get-tuple-element.22), channel_id=1, source_target_pairs={{0,8},{8,0},{16,24},{24,16},{1,9},{9,1},{17,25},{25,17},{2,10},{10... | collective-permute-start | bytes 196616 | tf_op jit(solution)/shard_map/ppermute | solution.py:458
  18.3 1.5 %collective-permute-start.2 = (bf16[8,32,128]{2,1,0:T(8,128)(2,1)S(1)}, bf16[8,32,128]{2,1,0:T(8,128)(2,1)S(1)}, u32[]{:S(2)}, u32[]{:S(2)}) collective-permute-start(bf16[8,32,128]{2,1,0:T(8,128)(2,1)S(1)} %get-tuple-element.23), channel_id=1, source_target_pairs={{0,16},{8,24},{16,0},{24,8},{1,17},{9,25},{17,1},{25,9},{2,18},{10... | collective-permute-start | bytes 196616 | tf_op jit(solution)/shard_map/ppermute | solution.py:458
  19.8 0.0 collective-permute-start.3
  19.8 0.8 %near_gram.1 = f32[8,32,128]{2,1,0:T(8,128)S(1)} custom-call(bf16[64,128,1024]{2,1,0:T(8,128)(2,1)S(1)} %get-tuple-element.15.coef_ref), custom_call_target="tpu_custom_call" | custom-call | flops 268435456 | bytes 2097152 | tf_op jit(solution)/shard_map/near_gram/pallas_call | solution.py:174
  20.6 0.4 collective-permute-done.1
  21.0 1.5 %collective-permute-done.2 = bf16[8,32,128]{2,1,0:T(8,128)(2,1)S(1)} collective-permute-done((bf16[8,32,128]{2,1,0:T(8,128)(2,1)S(1)}, bf16[8,32,128]{2,1,0:T(8,128)(2,1)S(1)}, u32[]{:S(2)}, u32[]{:S(2)}) %collective-permute-start.2) | collective-permute-done | bytes 65568 | tf_op jit(solution)/shard_map/ppermute | solution.py:458
  22.6 2.4 %collective-permute-done.3 = bf16[8,32,128]{2,1,0:T(8,128)(2,1)S(1)} collective-permute-done((bf16[8,32,128]{2,1,0:T(8,128)(2,1)S(1)}, bf16[8,32,128]{2,1,0:T(8,128)(2,1)S(1)}, u32[]{:S(2)}, u32[]{:S(2)}) %collective-permute-start.3) | collective-permute-done | bytes 65568 | tf_op jit(solution)/shard_map/ppermute | solution.py:458
  25.0 1.6 %collective-permute-start.4 = (f32[2,32,128]{2,1,0:T(8,128)S(1)}, f32[2,32,128]{2,1,0:T(8,128)S(1)}, u32[]{:S(2)}, u32[]{:S(2)}) collective-permute-start(f32[2,32,128]{2,1,0:T(8,128)S(1)} %get-tuple-element.25), channel_id=1, source_target_pairs={{0,2},{2,0},{4,6},{6,4},{1,3},{3,1},{5,7},{7,5},{8,10},{10,8},{12,... | collective-permute-start | bytes 98312 | tf_op jit(solution)/shard_map/ppermute | solution.py:458
  26.7 2.5 %collective-permute-start.6 = (f32[2,32,128]{2,1,0:T(8,128)S(1)}, f32[2,32,128]{2,1,0:T(8,128)S(1)}, u32[]{:S(2)}, u32[]{:S(2)}) collective-permute-start(f32[2,32,128]{2,1,0:T(8,128)S(1)} %get-tuple-element.26), channel_id=1, source_target_pairs={{0,6},{2,4},{4,2},{6,0},{1,7},{3,5},{5,3},{7,1},{8,14},{10,12},{12... | collective-permute-start | bytes 98312 | tf_op jit(solution)/shard_map/ppermute | solution.py:458
  29.2 0.1 collective-permute-start.5
  29.3 0.0 copy-done
  29.3 0.3 start_rows.1.start_ref
  29.6 0.0 collective-permute-done.4
  29.6 2.8 %collective-permute-done.6 = f32[2,32,128]{2,1,0:T(8,128)S(1)} collective-permute-done((f32[2,32,128]{2,1,0:T(8,128)S(1)}, f32[2,32,128]{2,1,0:T(8,128)S(1)}, u32[]{:S(2)}, u32[]{:S(2)}) %collective-permute-start.6) | collective-permute-done | bytes 32800 | tf_op jit(solution)/shard_map/ppermute | solution.py:458
  32.4 1.9 %collective-permute-done.5 = f32[2,32,128]{2,1,0:T(8,128)S(1)} collective-permute-done((f32[2,32,128]{2,1,0:T(8,128)S(1)}, f32[2,32,128]{2,1,0:T(8,128)S(1)}, u32[]{:S(2)}, u32[]{:S(2)}) %collective-permute-start.5) | collective-permute-done | bytes 32800 | tf_op jit(solution)/shard_map/ppermute | solution.py:458
  34.3 5.0 %solve.1 = f32[24,128]{1,0:T(8,128)S(1)} custom-call(f32[2,32,128]{2,1,0:T(8,128)S(1)} %fusion.4.packed_ref, f32[2,8,128]{2,1,0:T(8,128)S(1)} %start_rows.1.start_ref), custom_call_target="tpu_custom_call" | custom-call | tf_op jit(solution)/shard_map/solve/pallas_call | solution.py:385
  39.4 10.7 %all_to_all.5.pay_ref = f32[16,24,128]{2,1,0:T(8,128)S(1)} all-to-all(f32[16,24,128]{2,1,0:T(8,128)S(1)} %broadcast_in_dim.13), channel_id=1, replica_groups=mesh['grp'=4,'z'=4,'core'=2] {'grp','z'}, dimensions={0} | all-to-all | bytes 393216 | tf_op jit(solution)/shard_map/all_to_all | solution.py:491
  50.1 0.0 collective-permute-start.7
  50.1 0.0 copy-done.1
  50.1 2.1 %own_modes.1 = (f32[64,16,1024]{2,1,0:T(8,128)}, f32[8,64]{1,0:T(8,128)S(1)}) custom-call(bf16[64,128,1024]{2,1,0:T(8,128)(2,1)S(1)} %get-tuple-element.15.coef_ref, f32[16,24,128]{2,1,0:T(8,128)S(1)} %all_to_all.5.pay_ref, f32[1,1024]{1,0:T(1,128)S(1)} %bitcast.6), custom_call_target="tpu_custom_call" | custom-call | flops 134217728 | bytes 4194304 | tf_op jit(solution)/shard_map/own_modes/pallas_call | solution.py:436
  52.1 0.0 collective-permute-done.7.pay_ref
  52.2 2.7 %other_modes.1 = (f32[64,16,1024]{2,1,0:T(8,128)}, f32[8,64]{1,0:T(8,128)}) custom-call(bf16[64,128,1024]{2,1,0:T(8,128)(2,1)S(1)} %get-tuple-element.15.coef_ref, f32[16,24,128]{2,1,0:T(8,128)S(1)} %collective-permute-done.7.pay_ref, f32[1,1024]{1,0:T(1,128)S(1)} %bitcast.7, ...), custom_call_target="tpu_custom_call", output_to_operand_aliasing={{0}: (3, {})} | custom-call | flops 134217728 | bytes 4194304 | tf_op jit(solution)/shard_map/other_modes/pallas_call | solution.py:436
  (5 shorter events, 0.1 us)
Async XLA Ops:
  13.2 2.4 %collective-permute-start = (f32[32,32,128]{2,1,0:T(8,128)S(1)}, f32[32,32,128]{2,1,0:T(8,128)S(1)}, u32[]{:S(2)}, u32[]{:S(2)}) collective-permute-start(f32[32,32,128]{2,1,0:T(8,128)S(1)} %get-tuple-element.14), channel_id=1, source_target_pairs={{0,1},{1,0},{2,3},{3,2},{4,5},{5,4},{6,7},{7,6},{8,9},{9,8},{10,11... | collective-permute-start | bytes 1572872 | tf_op jit(solution)/shard_map/ppermute | solution.py:458
  13.7 15.6 %copy-start = (f32[64,2,63,8]{0,3,2,1:T(8,128)S(1)}, f32[64,2,63,8]{0,3,2,1:T(8,128)}, u32[]{:S(2)}) copy-start(f32[64,2,63,8]{0,3,2,1:T(8,128)} %param.8) | copy-start | bytes 774148
  13.7 36.3 %copy-start.1 = (f32[1024]{0:T(1024)S(1)}, f32[1024]{0:T(1024)}, u32[]{:S(2)}) copy-start(f32[1024]{0:T(1024)} %param.6) | copy-start | bytes 12292
  15.7 5.3 %collective-permute-start.1 = (bf16[8,32,128]{2,1,0:T(8,128)(2,1)S(1)}, bf16[8,32,128]{2,1,0:T(8,128)(2,1)S(1)}, u32[]{:S(2)}, u32[]{:S(2)}) collective-permute-start(bf16[8,32,128]{2,1,0:T(8,128)(2,1)S(1)} %get-tuple-element.22), channel_id=1, source_target_pairs={{0,8},{8,0},{16,24},{24,16},{1,9},{9,1},{17,25},{25,17},{2,10},{10... | collective-permute-start | bytes 196616 | tf_op jit(solution)/shard_map/ppermute | solution.py:458
  18.3 4.3 %collective-permute-start.2 = (bf16[8,32,128]{2,1,0:T(8,128)(2,1)S(1)}, bf16[8,32,128]{2,1,0:T(8,128)(2,1)S(1)}, u32[]{:S(2)}, u32[]{:S(2)}) collective-permute-start(bf16[8,32,128]{2,1,0:T(8,128)(2,1)S(1)} %get-tuple-element.23), channel_id=1, source_target_pairs={{0,16},{8,24},{16,0},{24,8},{1,17},{9,25},{17,1},{25,9},{2,18},{10... | collective-permute-start | bytes 196616 | tf_op jit(solution)/shard_map/ppermute | solution.py:458
  19.8 5.2 %collective-permute-start.3 = (bf16[8,32,128]{2,1,0:T(8,128)(2,1)S(1)}, bf16[8,32,128]{2,1,0:T(8,128)(2,1)S(1)}, u32[]{:S(2)}, u32[]{:S(2)}) collective-permute-start(bf16[8,32,128]{2,1,0:T(8,128)(2,1)S(1)} %get-tuple-element.24), channel_id=1, source_target_pairs={{0,24},{8,16},{16,8},{24,0},{1,25},{9,17},{17,9},{25,1},{2,26},{10... | collective-permute-start | bytes 196616 | tf_op jit(solution)/shard_map/ppermute | solution.py:458
  25.0 4.6 %collective-permute-start.4 = (f32[2,32,128]{2,1,0:T(8,128)S(1)}, f32[2,32,128]{2,1,0:T(8,128)S(1)}, u32[]{:S(2)}, u32[]{:S(2)}) collective-permute-start(f32[2,32,128]{2,1,0:T(8,128)S(1)} %get-tuple-element.25), channel_id=1, source_target_pairs={{0,2},{2,0},{4,6},{6,4},{1,3},{3,1},{5,7},{7,5},{8,10},{10,8},{12,... | collective-permute-start | bytes 98312 | tf_op jit(solution)/shard_map/ppermute | solution.py:458
  26.7 5.7 %collective-permute-start.6 = (f32[2,32,128]{2,1,0:T(8,128)S(1)}, f32[2,32,128]{2,1,0:T(8,128)S(1)}, u32[]{:S(2)}, u32[]{:S(2)}) collective-permute-start(f32[2,32,128]{2,1,0:T(8,128)S(1)} %get-tuple-element.26), channel_id=1, source_target_pairs={{0,6},{2,4},{4,2},{6,0},{1,7},{3,5},{5,3},{7,1},{8,14},{10,12},{12... | collective-permute-start | bytes 98312 | tf_op jit(solution)/shard_map/ppermute | solution.py:458
  29.2 5.2 %collective-permute-start.5 = (f32[2,32,128]{2,1,0:T(8,128)S(1)}, f32[2,32,128]{2,1,0:T(8,128)S(1)}, u32[]{:S(2)}, u32[]{:S(2)}) collective-permute-start(f32[2,32,128]{2,1,0:T(8,128)S(1)} %get-tuple-element.27), channel_id=1, source_target_pairs={{0,4},{2,6},{4,0},{6,2},{1,5},{3,7},{5,1},{7,3},{8,12},{10,14},{12... | collective-permute-start | bytes 98312 | tf_op jit(solution)/shard_map/ppermute | solution.py:458
  50.1 2.1 %collective-permute-start.7 = (f32[16,24,128]{2,1,0:T(8,128)S(1)}, f32[16,24,128]{2,1,0:T(8,128)S(1)}, u32[]{:S(2)}, u32[]{:S(2)}) collective-permute-start(f32[16,24,128]{2,1,0:T(8,128)S(1)} %all_to_all.5.pay_ref), channel_id=1, source_target_pairs={{0,1},{1,0},{2,3},{3,2},{4,5},{5,4},{6,7},{7,6},{8,9},{9,8},{10,11... | collective-permute-start | bytes 589832 | tf_op jit(solution)/shard_map/ppermute | solution.py:458

commit v10 on v9

--- a/solution.py
+++ b/solution.py
@@ -471,10 +471,7 @@
     late, held = lax.optimization_barrier((coeffs, held))
     if plan.split_grp:
         held = held.reshape((plan.grp - 1, plan.deep * plan.per) + held.shape[1:])
-        arrived = [
-            swap(held[d - 1].astype(jnp.bfloat16), "grp", plan.grp, d).astype(jnp.float32)
-            for d in range(1, plan.grp)
-        ]
+        arrived = [swap(held[d - 1], "grp", plan.grp, d) for d in range(1, plan.grp)]
     else:
         held = held.reshape((plan.deep - 1, plan.per) + held.shape[1:])
         arrived = [swap(held[d - 1], "z", plan.deep, d) for d in range(1, plan.deep)]

time: 55.1 us -> 58.8 us (1.067)
  waiting for transfers between devices: 9.06 us -> 12 us
  blocking collectives: 10.7 us -> 11.4 us
    ppermute x8, waiting for transfers between devices: 9.06 us -> 12 us  [swap(): return lax.ppermute(x, axis, [(i, i ^ offset) for i in range(size)])]
    all_to_all x1, blocking collectives: 10.7 us -> 11.4 us  [shards(): payload = lax.all_to_all(payload, plan.chip_axes, 0, 0, tiled=True)]
where the time goes in v10:
time: 58.8 us; the launch traced here: 58.5 us
  Pallas kernels  25.3 us (43%)
  waiting for transfers between devices  12 us (20%)
  blocking collectives  11.4 us (19%)
  starting transfers between devices  8.9 us (15%)
  between operations  0.72 us (1%)
    pallas_call x1, Pallas kernels, transform(): pl.pallas_call(functools.partial(transform_kernel, plan), grid=(rows_here...  12.6 us
    ppermute x8, waiting for transfers between devices, swap(): return lax.ppermute(x, axis, [(i, i ^ offset) for i in range(size)])  12 us
    all_to_all x1, blocking collectives, shards(): payload = lax.all_to_all(payload, plan.chip_axes, 0, 0, tiled=True)  11.4 us
    ppermute x8, starting transfers between devices, swap(): return lax.ppermute(x, axis, [(i, i ^ offset) for i in range(size)])  8.9 us
    pallas_call x1, Pallas kernels, solve(): pl.pallas_call(functools.partial(solve_kernel, plan, total_rows), in_spec...  5.01 us
    pallas_call x2, Pallas kernels, modes(): pl.pallas_call(functools.partial(modes_kernel, plan, bool(earlier)), in_s...  4.74 us
    pallas_call x2, Pallas kernels, grams(): pl.pallas_call(functools.partial(pack_some, plan, other_core, offsets), i...  2.64 us
  transfers between devices with their start and end apart: 8, of which 5 were waited for; matrix products, arithmetic and copies ran while one was open for 0% of the time, Pallas kernels for 9%

profile of v10, /device:TPU:0, one launch (start us, length us, event | category | flops | bytes accessed | tf_op | source)
XLA Modules:
  0.0 58.5 jit_solution(11205433131596189990)
XLA Ops:
  0.6 12.6 %transform.1 = (bf16[64,128,1024]{2,1,0:T(8,128)(2,1)S(1)}, f32[32,32,128]{2,1,0:T(8,128)S(1)}) custom-call(bf16[128,256]{1,0:T(8,128)(2,1)} %constant.3.table_ref, f32[1,1024]{1,0:T(1,128)} %bitcast.5, f32[1,1024]{1,0:T(1,128)} %bitcast.8, bf16[8192,1024]{1,0:T(8,128)(2,1)} %snap_ref.1), custom_call_target="tpu_custom_call" | custom-call | tf_op jit(solution)/shard_map/transform/pallas_call | solution.py:145
  13.2 0.5 collective-permute-start
  13.7 0.0 copy-start
  13.7 0.0 copy-start.1
  13.7 1.9 %own_gram.1 = f32[24,32,128]{2,1,0:T(8,128)S(1)} custom-call(bf16[64,128,1024]{2,1,0:T(8,128)(2,1)S(1)} %get-tuple-element.15.coef_ref), custom_call_target="tpu_custom_call" | custom-call | flops 805306368 | bytes 6291456 | tf_op jit(solution)/shard_map/own_gram/pallas_call | solution.py:174
  15.6 0.0 collective-permute-done
  15.6 0.1 slice_add_fusion
  15.7 2.6 %collective-permute-start.1 = (f32[8,32,128]{2,1,0:T(8,128)S(1)}, f32[8,32,128]{2,1,0:T(8,128)S(1)}, u32[]{:S(2)}, u32[]{:S(2)}) collective-permute-start(f32[8,32,128]{2,1,0:T(8,128)S(1)} %get-tuple-element.22), channel_id=1, source_target_pairs={{0,8},{8,0},{16,24},{24,16},{1,9},{9,1},{17,25},{25,17},{2,10},{10... | collective-permute-start | bytes 393224 | tf_op jit(solution)/shard_map/ppermute | solution.py:458
  18.3 1.5 %collective-permute-start.3 = (f32[8,32,128]{2,1,0:T(8,128)S(1)}, f32[8,32,128]{2,1,0:T(8,128)S(1)}, u32[]{:S(2)}, u32[]{:S(2)}) collective-permute-start(f32[8,32,128]{2,1,0:T(8,128)S(1)} %get-tuple-element.23), channel_id=1, source_target_pairs={{0,24},{8,16},{16,8},{24,0},{1,25},{9,17},{17,9},{25,1},{2,26},{10... | collective-permute-start | bytes 393224 | tf_op jit(solution)/shard_map/ppermute | solution.py:458
  19.8 0.0 collective-permute-start.2
  19.8 0.8 %near_gram.1 = f32[8,32,128]{2,1,0:T(8,128)S(1)} custom-call(bf16[64,128,1024]{2,1,0:T(8,128)(2,1)S(1)} %get-tuple-element.15.coef_ref), custom_call_target="tpu_custom_call" | custom-call | flops 268435456 | bytes 2097152 | tf_op jit(solution)/shard_map/near_gram/pallas_call | solution.py:174
  20.6 2.0 %collective-permute-done.1 = f32[8,32,128]{2,1,0:T(8,128)S(1)} collective-permute-done((f32[8,32,128]{2,1,0:T(8,128)S(1)}, f32[8,32,128]{2,1,0:T(8,128)S(1)}, u32[]{:S(2)}, u32[]{:S(2)}) %collective-permute-start.1) | collective-permute-done | bytes 131104 | tf_op jit(solution)/shard_map/ppermute | solution.py:458
  22.6 3.9 %collective-permute-done.3 = f32[8,32,128]{2,1,0:T(8,128)S(1)} collective-permute-done((f32[8,32,128]{2,1,0:T(8,128)S(1)}, f32[8,32,128]{2,1,0:T(8,128)S(1)}, u32[]{:S(2)}, u32[]{:S(2)}) %collective-permute-start.3) | collective-permute-done | bytes 131104 | tf_op jit(solution)/shard_map/ppermute | solution.py:458
  26.5 1.4 %collective-permute-done.2 = f32[8,32,128]{2,1,0:T(8,128)S(1)} collective-permute-done((f32[8,32,128]{2,1,0:T(8,128)S(1)}, f32[8,32,128]{2,1,0:T(8,128)S(1)}, u32[]{:S(2)}, u32[]{:S(2)}) %collective-permute-start.2) | collective-permute-done | bytes 131104 | tf_op jit(solution)/shard_map/ppermute | solution.py:458
  28.0 1.6 %collective-permute-start.4 = (f32[2,32,128]{2,1,0:T(8,128)S(1)}, f32[2,32,128]{2,1,0:T(8,128)S(1)}, u32[]{:S(2)}, u32[]{:S(2)}) collective-permute-start(f32[2,32,128]{2,1,0:T(8,128)S(1)} %get-tuple-element.25), channel_id=1, source_target_pairs={{0,2},{2,0},{4,6},{6,4},{1,3},{3,1},{5,7},{7,5},{8,10},{10,8},{12,... | collective-permute-start | bytes 98312 | tf_op jit(solution)/shard_map/ppermute | solution.py:458
  29.6 2.5 %collective-permute-start.6 = (f32[2,32,128]{2,1,0:T(8,128)S(1)}, f32[2,32,128]{2,1,0:T(8,128)S(1)}, u32[]{:S(2)}, u32[]{:S(2)}) collective-permute-start(f32[2,32,128]{2,1,0:T(8,128)S(1)} %get-tuple-element.26), channel_id=1, source_target_pairs={{0,6},{2,4},{4,2},{6,0},{1,7},{3,5},{5,3},{7,1},{8,14},{10,12},{12... | collective-permute-start | bytes 98312 | tf_op jit(solution)/shard_map/ppermute | solution.py:458
  32.1 0.1 collective-permute-start.5
  32.2 0.0 copy-done
  32.2 0.3 start_rows.1.start_ref
  32.6 0.0 collective-permute-done.4
  32.6 2.8 %collective-permute-done.6 = f32[2,32,128]{2,1,0:T(8,128)S(1)} collective-permute-done((f32[2,32,128]{2,1,0:T(8,128)S(1)}, f32[2,32,128]{2,1,0:T(8,128)S(1)}, u32[]{:S(2)}, u32[]{:S(2)}) %collective-permute-start.6) | collective-permute-done | bytes 32800 | tf_op jit(solution)/shard_map/ppermute | solution.py:458
  35.3 1.9 %collective-permute-done.5 = f32[2,32,128]{2,1,0:T(8,128)S(1)} collective-permute-done((f32[2,32,128]{2,1,0:T(8,128)S(1)}, f32[2,32,128]{2,1,0:T(8,128)S(1)}, u32[]{:S(2)}, u32[]{:S(2)}) %collective-permute-start.5) | collective-permute-done | bytes 32800 | tf_op jit(solution)/shard_map/ppermute | solution.py:458
  37.3 5.0 %solve.1 = f32[24,128]{1,0:T(8,128)S(1)} custom-call(f32[2,32,128]{2,1,0:T(8,128)S(1)} %fusion.4.packed_ref, f32[2,8,128]{2,1,0:T(8,128)S(1)} %start_rows.1.start_ref), custom_call_target="tpu_custom_call" | custom-call | tf_op jit(solution)/shard_map/solve/pallas_call | solution.py:385
  42.3 11.4 %all_to_all.5.pay_ref = f32[16,24,128]{2,1,0:T(8,128)S(1)} all-to-all(f32[16,24,128]{2,1,0:T(8,128)S(1)} %broadcast_in_dim.13), channel_id=1, replica_groups=mesh['grp'=4,'z'=4,'core'=2] {'grp','z'}, dimensions={0} | all-to-all | bytes 393216 | tf_op jit(solution)/shard_map/all_to_all | solution.py:488
  53.8 0.0 collective-permute-start.7
  53.8 0.0 copy-done.1
  53.8 2.1 %own_modes.1 = (f32[64,16,1024]{2,1,0:T(8,128)}, f32[8,64]{1,0:T(8,128)S(1)}) custom-call(bf16[64,128,1024]{2,1,0:T(8,128)(2,1)S(1)} %get-tuple-element.15.coef_ref, f32[16,24,128]{2,1,0:T(8,128)S(1)} %all_to_all.5.pay_ref, f32[1,1024]{1,0:T(1,128)S(1)} %bitcast.6), custom_call_target="tpu_custom_call" | custom-call | flops 134217728 | bytes 4194304 | tf_op jit(solution)/shard_map/own_modes/pallas_call | solution.py:436
  55.8 0.0 collective-permute-done.7.pay_ref
  55.9 2.7 %other_modes.1 = (f32[64,16,1024]{2,1,0:T(8,128)}, f32[8,64]{1,0:T(8,128)}) custom-call(bf16[64,128,1024]{2,1,0:T(8,128)(2,1)S(1)} %get-tuple-element.15.coef_ref, f32[16,24,128]{2,1,0:T(8,128)S(1)} %collective-permute-done.7.pay_ref, f32[1,1024]{1,0:T(1,128)S(1)} %bitcast.7, ...), custom_call_target="tpu_custom_call", output_to_operand_aliasing={{0}: (3, {})} | custom-call | flops 134217728 | bytes 4194304 | tf_op jit(solution)/shard_map/other_modes/pallas_call | solution.py:436
  (5 shorter events, 0.1 us)
Async XLA Ops:
  13.2 2.4 %collective-permute-start = (f32[32,32,128]{2,1,0:T(8,128)S(1)}, f32[32,32,128]{2,1,0:T(8,128)S(1)}, u32[]{:S(2)}, u32[]{:S(2)}) collective-permute-start(f32[32,32,128]{2,1,0:T(8,128)S(1)} %get-tuple-element.14), channel_id=1, source_target_pairs={{0,1},{1,0},{2,3},{3,2},{4,5},{5,4},{6,7},{7,6},{8,9},{9,8},{10,11... | collective-permute-start | bytes 1572872 | tf_op jit(solution)/shard_map/ppermute | solution.py:458
  13.7 18.5 %copy-start = (f32[64,2,63,8]{0,3,2,1:T(8,128)S(1)}, f32[64,2,63,8]{0,3,2,1:T(8,128)}, u32[]{:S(2)}) copy-start(f32[64,2,63,8]{0,3,2,1:T(8,128)} %param.8) | copy-start | bytes 774148
  13.7 40.0 %copy-start.1 = (f32[1024]{0:T(1024)S(1)}, f32[1024]{0:T(1024)}, u32[]{:S(2)}) copy-start(f32[1024]{0:T(1024)} %param.6) | copy-start | bytes 12292
  15.7 6.9 %collective-permute-start.1 = (f32[8,32,128]{2,1,0:T(8,128)S(1)}, f32[8,32,128]{2,1,0:T(8,128)S(1)}, u32[]{:S(2)}, u32[]{:S(2)}) collective-permute-start(f32[8,32,128]{2,1,0:T(8,128)S(1)} %get-tuple-element.22), channel_id=1, source_target_pairs={{0,8},{8,0},{16,24},{24,16},{1,9},{9,1},{17,25},{25,17},{2,10},{10... | collective-permute-start | bytes 393224 | tf_op jit(solution)/shard_map/ppermute | solution.py:458
  18.3 8.2 %collective-permute-start.3 = (f32[8,32,128]{2,1,0:T(8,128)S(1)}, f32[8,32,128]{2,1,0:T(8,128)S(1)}, u32[]{:S(2)}, u32[]{:S(2)}) collective-permute-start(f32[8,32,128]{2,1,0:T(8,128)S(1)} %get-tuple-element.23), channel_id=1, source_target_pairs={{0,24},{8,16},{16,8},{24,0},{1,25},{9,17},{17,9},{25,1},{2,26},{10... | collective-permute-start | bytes 393224 | tf_op jit(solution)/shard_map/ppermute | solution.py:458
  19.8 8.1 %collective-permute-start.2 = (f32[8,32,128]{2,1,0:T(8,128)S(1)}, f32[8,32,128]{2,1,0:T(8,128)S(1)}, u32[]{:S(2)}, u32[]{:S(2)}) collective-permute-start(f32[8,32,128]{2,1,0:T(8,128)S(1)} %get-tuple-element.24), channel_id=1, source_target_pairs={{0,16},{8,24},{16,0},{24,8},{1,17},{9,25},{17,1},{25,9},{2,18},{10... | collective-permute-start | bytes 393224 | tf_op jit(solution)/shard_map/ppermute | solution.py:458
  28.0 4.6 %collective-permute-start.4 = (f32[2,32,128]{2,1,0:T(8,128)S(1)}, f32[2,32,128]{2,1,0:T(8,128)S(1)}, u32[]{:S(2)}, u32[]{:S(2)}) collective-permute-start(f32[2,32,128]{2,1,0:T(8,128)S(1)} %get-tuple-element.25), channel_id=1, source_target_pairs={{0,2},{2,0},{4,6},{6,4},{1,3},{3,1},{5,7},{7,5},{8,10},{10,8},{12,... | collective-permute-start | bytes 98312 | tf_op jit(solution)/shard_map/ppermute | solution.py:458
  29.6 5.7 %collective-permute-start.6 = (f32[2,32,128]{2,1,0:T(8,128)S(1)}, f32[2,32,128]{2,1,0:T(8,128)S(1)}, u32[]{:S(2)}, u32[]{:S(2)}) collective-permute-start(f32[2,32,128]{2,1,0:T(8,128)S(1)} %get-tuple-element.26), channel_id=1, source_target_pairs={{0,6},{2,4},{4,2},{6,0},{1,7},{3,5},{5,3},{7,1},{8,14},{10,12},{12... | collective-permute-start | bytes 98312 | tf_op jit(solution)/shard_map/ppermute | solution.py:458
  32.1 5.2 %collective-permute-start.5 = (f32[2,32,128]{2,1,0:T(8,128)S(1)}, f32[2,32,128]{2,1,0:T(8,128)S(1)}, u32[]{:S(2)}, u32[]{:S(2)}) collective-permute-start(f32[2,32,128]{2,1,0:T(8,128)S(1)} %get-tuple-element.27), channel_id=1, source_target_pairs={{0,4},{2,6},{4,0},{6,2},{1,5},{3,7},{5,1},{7,3},{8,12},{10,14},{12... | collective-permute-start | bytes 98312 | tf_op jit(solution)/shard_map/ppermute | solution.py:458
  53.8 2.1 %collective-permute-start.7 = (f32[16,24,128]{2,1,0:T(8,128)S(1)}, f32[16,24,128]{2,1,0:T(8,128)S(1)}, u32[]{:S(2)}, u32[]{:S(2)}) collective-permute-start(f32[16,24,128]{2,1,0:T(8,128)S(1)} %all_to_all.5.pay_ref), channel_id=1, source_target_pairs={{0,1},{1,0},{2,3},{3,2},{4,5},{5,4},{6,7},{7,6},{8,9},{9,8},{10,11... | collective-permute-start | bytes 589832 | tf_op jit(solution)/shard_map/ppermute | solution.py:458

commit v11 on v10

--- a/solution.py
+++ b/solution.py
@@ -18,6 +18,7 @@
 NM = 8
 ITERS = 12
 EPS = 1e-06
+PART = 32
 LEAST_LEFT = 1e-03
 LANES = 128
 PITCH = 2 * NB + 1
@@ -364,13 +365,14 @@
         for i, v in enumerate(lax.fori_loop(0, ITERS, checked_sweep, start)):
             basis_ref[i] = v
 
+    rows = []
     extras = jnp.zeros((NM, LANES), jnp.float32)
     scale = 1.0 / math.sqrt(total_rows)
     for i in range(plan.per):
         v = basis_ref[i]
         energy = lane_sum(v * image_of(i, v)[0])
         coef = v.astype(jnp.bfloat16).astype(jnp.float32)
-        out_ref[i * NM : (i + 1) * NM] = coef
+        rows.append(coef)
         gain = 1.0 / jnp.sqrt(energy + EPS)
         tilt_real = gain * (lane_sum(coef * probes[i][0]) * scale)
         tilt_imag = gain * (lane_sum(coef * probes[i][1]) * scale)
@@ -378,7 +380,10 @@
         extras = jnp.where(lane8 == 3 * i, gain * tilt_real / size, extras)
         extras = jnp.where(lane8 == 3 * i + 1, -gain * tilt_imag / size, extras)
         extras = jnp.where(lane8 == 3 * i + 2, energy, extras)
-    out_ref[plan.per * NM :] = extras
+    high, middle, low = (part.astype(jnp.float32) for part in split_three(extras))
+    apart = high + pltpu.roll(middle, PART, 1) + pltpu.roll(low, 2 * PART, 1)
+    rows += [apart, jnp.zeros_like(apart)]
+    out_ref[...] = jnp.concatenate(rows, axis=0).astype(jnp.bfloat16)
 
 
 def solve(plan, total_rows, packed, start):
@@ -386,7 +391,7 @@
         functools.partial(solve_kernel, plan, total_rows),
         in_specs=[pl.BlockSpec(memory_space=pltpu.VMEM)] * 2,
         out_specs=pl.BlockSpec(memory_space=pltpu.VMEM),
-        out_shape=jax.ShapeDtypeStruct(((plan.per + 1) * NM, LANES), jnp.float32),
+        out_shape=jax.ShapeDtypeStruct(((plan.per + 2) * NM, LANES), jnp.bfloat16),
         scratch_shapes=[pltpu.VMEM((plan.per, NM, LANES), jnp.float32)],
         compiler_params=pltpu.CompilerParams(vmem_limit_bytes=SOLVE_MIB * MIB),
         name="solve",
@@ -402,8 +407,13 @@
     copies = []
     for n, (chip, f) in enumerate(plan.half(other_core)):
         j = n % plan.per
-        c = pay_ref[chip, j * NM : (j + 1) * NM]
-        extras = pay_ref[chip, plan.per * NM :]
+        if j == 0:
+            whole_pay = pay_ref[chip].astype(jnp.float32)
+            apart = whole_pay[plan.per * NM : (plan.per + 1) * NM]
+            extras = apart + (
+                pltpu.roll(apart, LANES - PART, 1) + pltpu.roll(apart, LANES - 2 * PART, 1)
+            )
+        c = whole_pay[j * NM : (j + 1) * NM]
         factor_real = extras[:, 3 * j : 3 * j + 1]
         factor_imag = extras[:, 3 * j + 1 : 3 * j + 2]
         matrix = jnp.concatenate([jnp.where(left, c, -c), pltpu.roll(c, NB, 1)], axis=0)

time: 58.8 us -> 58.6 us (level)
  no operation moved by 1% of the time
where the time goes in v11:
time: 58.6 us; the launch traced here: 58.3 us
  Pallas kernels  25.5 us (44%)
  waiting for transfers between devices  12 us (20%)
  blocking collectives  11 us (19%)
  starting transfers between devices  8.9 us (15%)
  between operations  0.72 us (1%)
    pallas_call x1, Pallas kernels, transform(): pl.pallas_call(functools.partial(transform_kernel, plan), grid=(rows_here...  12.6 us
    ppermute x8, waiting for transfers between devices, swap(): return lax.ppermute(x, axis, [(i, i ^ offset) for i in range(size)])  12 us
    all_to_all x1, blocking collectives, shards(): payload = lax.all_to_all(payload, plan.chip_axes, 0, 0, tiled=True)  11 us
    ppermute x8, starting transfers between devices, swap(): return lax.ppermute(x, axis, [(i, i ^ offset) for i in range(size)])  8.9 us
    pallas_call x1, Pallas kernels, solve(): pl.pallas_call(functools.partial(solve_kernel, plan, total_rows), in_spec...  5.09 us
    pallas_call x2, Pallas kernels, modes(): pl.pallas_call(functools.partial(modes_kernel, plan, bool(earlier)), in_s...  4.91 us
    pallas_call x2, Pallas kernels, grams(): pl.pallas_call(functools.partial(pack_some, plan, other_core, offsets), i...  2.64 us
  transfers between devices with their start and end apart: 8, of which 5 were waited for; matrix products, arithmetic and copies ran while one was open for 0% of the time, Pallas kernels for 9%

profile of v11, /device:TPU:0, one launch (start us, length us, event | category | flops | bytes accessed | tf_op | source)
XLA Modules:
  0.0 58.3 jit_solution(2043288747514455200)
XLA Ops:
  0.6 12.6 %transform.1 = (bf16[64,128,1024]{2,1,0:T(8,128)(2,1)S(1)}, f32[32,32,128]{2,1,0:T(8,128)S(1)}) custom-call(bf16[128,256]{1,0:T(8,128)(2,1)} %constant.3.table_ref, f32[1,1024]{1,0:T(1,128)} %bitcast.5, f32[1,1024]{1,0:T(1,128)} %bitcast.8, bf16[8192,1024]{1,0:T(8,128)(2,1)} %snap_ref.1), custom_call_target="tpu_custom_call" | custom-call | tf_op jit(solution)/shard_map/transform/pallas_call | solution.py:146
  13.2 0.5 collective-permute-start
  13.7 0.0 copy-start
  13.7 0.0 copy-start.1
  13.7 1.9 %own_gram.1 = f32[24,32,128]{2,1,0:T(8,128)S(1)} custom-call(bf16[64,128,1024]{2,1,0:T(8,128)(2,1)S(1)} %get-tuple-element.15.coef_ref), custom_call_target="tpu_custom_call" | custom-call | flops 805306368 | bytes 6291456 | tf_op jit(solution)/shard_map/own_gram/pallas_call | solution.py:175
  15.6 0.0 collective-permute-done
  15.6 0.1 slice_add_fusion
  15.7 2.6 %collective-permute-start.1 = (f32[8,32,128]{2,1,0:T(8,128)S(1)}, f32[8,32,128]{2,1,0:T(8,128)S(1)}, u32[]{:S(2)}, u32[]{:S(2)}) collective-permute-start(f32[8,32,128]{2,1,0:T(8,128)S(1)} %get-tuple-element.22), channel_id=1, source_target_pairs={{0,8},{8,0},{16,24},{24,16},{1,9},{9,1},{17,25},{25,17},{2,10},{10... | collective-permute-start | bytes 393224 | tf_op jit(solution)/shard_map/ppermute | solution.py:468
  18.3 1.5 %collective-permute-start.3 = (f32[8,32,128]{2,1,0:T(8,128)S(1)}, f32[8,32,128]{2,1,0:T(8,128)S(1)}, u32[]{:S(2)}, u32[]{:S(2)}) collective-permute-start(f32[8,32,128]{2,1,0:T(8,128)S(1)} %get-tuple-element.23), channel_id=1, source_target_pairs={{0,24},{8,16},{16,8},{24,0},{1,25},{9,17},{17,9},{25,1},{2,26},{10... | collective-permute-start | bytes 393224 | tf_op jit(solution)/shard_map/ppermute | solution.py:468
  19.8 0.0 collective-permute-start.2
  19.8 0.8 %near_gram.1 = f32[8,32,128]{2,1,0:T(8,128)S(1)} custom-call(bf16[64,128,1024]{2,1,0:T(8,128)(2,1)S(1)} %get-tuple-element.15.coef_ref), custom_call_target="tpu_custom_call" | custom-call | flops 268435456 | bytes 2097152 | tf_op jit(solution)/shard_map/near_gram/pallas_call | solution.py:175
  20.6 2.0 %collective-permute-done.1 = f32[8,32,128]{2,1,0:T(8,128)S(1)} collective-permute-done((f32[8,32,128]{2,1,0:T(8,128)S(1)}, f32[8,32,128]{2,1,0:T(8,128)S(1)}, u32[]{:S(2)}, u32[]{:S(2)}) %collective-permute-start.1) | collective-permute-done | bytes 131104 | tf_op jit(solution)/shard_map/ppermute | solution.py:468
  22.6 3.9 %collective-permute-done.3 = f32[8,32,128]{2,1,0:T(8,128)S(1)} collective-permute-done((f32[8,32,128]{2,1,0:T(8,128)S(1)}, f32[8,32,128]{2,1,0:T(8,128)S(1)}, u32[]{:S(2)}, u32[]{:S(2)}) %collective-permute-start.3) | collective-permute-done | bytes 131104 | tf_op jit(solution)/shard_map/ppermute | solution.py:468
  26.5 1.4 %collective-permute-done.2 = f32[8,32,128]{2,1,0:T(8,128)S(1)} collective-permute-done((f32[8,32,128]{2,1,0:T(8,128)S(1)}, f32[8,32,128]{2,1,0:T(8,128)S(1)}, u32[]{:S(2)}, u32[]{:S(2)}) %collective-permute-start.2) | collective-permute-done | bytes 131104 | tf_op jit(solution)/shard_map/ppermute | solution.py:468
  28.0 1.6 %collective-permute-start.4 = (f32[2,32,128]{2,1,0:T(8,128)S(1)}, f32[2,32,128]{2,1,0:T(8,128)S(1)}, u32[]{:S(2)}, u32[]{:S(2)}) collective-permute-start(f32[2,32,128]{2,1,0:T(8,128)S(1)} %get-tuple-element.25), channel_id=1, source_target_pairs={{0,2},{2,0},{4,6},{6,4},{1,3},{3,1},{5,7},{7,5},{8,10},{10,8},{12,... | collective-permute-start | bytes 98312 | tf_op jit(solution)/shard_map/ppermute | solution.py:468
  29.6 2.5 %collective-permute-start.6 = (f32[2,32,128]{2,1,0:T(8,128)S(1)}, f32[2,32,128]{2,1,0:T(8,128)S(1)}, u32[]{:S(2)}, u32[]{:S(2)}) collective-permute-start(f32[2,32,128]{2,1,0:T(8,128)S(1)} %get-tuple-element.26), channel_id=1, source_target_pairs={{0,6},{2,4},{4,2},{6,0},{1,7},{3,5},{5,3},{7,1},{8,14},{10,12},{12... | collective-permute-start | bytes 98312 | tf_op jit(solution)/shard_map/ppermute | solution.py:468
  32.1 0.1 collective-permute-start.5
  32.2 0.0 copy-done
  32.2 0.3 start_rows.1.start_ref
  32.6 0.0 collective-permute-done.4
  32.6 2.8 %collective-permute-done.6 = f32[2,32,128]{2,1,0:T(8,128)S(1)} collective-permute-done((f32[2,32,128]{2,1,0:T(8,128)S(1)}, f32[2,32,128]{2,1,0:T(8,128)S(1)}, u32[]{:S(2)}, u32[]{:S(2)}) %collective-permute-start.6) | collective-permute-done | bytes 32800 | tf_op jit(solution)/shard_map/ppermute | solution.py:468
  35.3 1.9 %collective-permute-done.5 = f32[2,32,128]{2,1,0:T(8,128)S(1)} collective-permute-done((f32[2,32,128]{2,1,0:T(8,128)S(1)}, f32[2,32,128]{2,1,0:T(8,128)S(1)}, u32[]{:S(2)}, u32[]{:S(2)}) %collective-permute-start.5) | collective-permute-done | bytes 32800 | tf_op jit(solution)/shard_map/ppermute | solution.py:468
  37.3 5.1 %solve.1 = bf16[32,128]{1,0:T(8,128)(2,1)S(1)} custom-call(f32[2,32,128]{2,1,0:T(8,128)S(1)} %fusion.4.packed_ref, f32[2,8,128]{2,1,0:T(8,128)S(1)} %start_rows.1.start_ref), custom_call_target="tpu_custom_call" | custom-call | tf_op jit(solution)/shard_map/solve/pallas_call | solution.py:390
  42.4 11.0 %all_to_all.5.pay_ref = bf16[16,32,128]{2,1,0:T(8,128)(2,1)S(1)} all-to-all(bf16[16,32,128]{2,1,0:T(8,128)(2,1)S(1)} %broadcast_in_dim.13), channel_id=1, replica_groups=mesh['grp'=4,'z'=4,'core'=2] {'grp','z'}, dimensions={0} | all-to-all | bytes 262144 | tf_op jit(solution)/shard_map/all_to_all | solution.py:498
  53.4 0.0 collective-permute-start.7
  53.4 0.0 copy-done.1
  53.4 2.1 %own_modes.1 = (f32[64,16,1024]{2,1,0:T(8,128)}, f32[8,64]{1,0:T(8,128)S(1)}) custom-call(bf16[64,128,1024]{2,1,0:T(8,128)(2,1)S(1)} %get-tuple-element.15.coef_ref, bf16[16,32,128]{2,1,0:T(8,128)(2,1)S(1)} %all_to_all.5.pay_ref, f32[1,1024]{1,0:T(1,128)S(1)} %bitcast.6), custom_call_target="tpu_custom_call" | custom-call | flops 134217728 | bytes 4194304 | tf_op jit(solution)/shard_map/own_modes/pallas_call | solution.py:446
  55.5 0.0 collective-permute-done.7.pay_ref
  55.5 2.8 %other_modes.1 = (f32[64,16,1024]{2,1,0:T(8,128)}, f32[8,64]{1,0:T(8,128)}) custom-call(bf16[64,128,1024]{2,1,0:T(8,128)(2,1)S(1)} %get-tuple-element.15.coef_ref, bf16[16,32,128]{2,1,0:T(8,128)(2,1)S(1)} %collective-permute-done.7.pay_ref, f32[1,1024]{1,0:T(1,128)S(1)} %bitcast.7, ...), custom_call_target="tpu_custom_call", output_to_operand_aliasing={{0}: (3, {})} | custom-call | flops 134217728 | bytes 4194304 | tf_op jit(solution)/shard_map/other_modes/pallas_call | solution.py:446
  (5 shorter events, 0.1 us)
Async XLA Ops:
  13.2 2.4 %collective-permute-start = (f32[32,32,128]{2,1,0:T(8,128)S(1)}, f32[32,32,128]{2,1,0:T(8,128)S(1)}, u32[]{:S(2)}, u32[]{:S(2)}) collective-permute-start(f32[32,32,128]{2,1,0:T(8,128)S(1)} %get-tuple-element.14), channel_id=1, source_target_pairs={{0,1},{1,0},{2,3},{3,2},{4,5},{5,4},{6,7},{7,6},{8,9},{9,8},{10,11... | collective-permute-start | bytes 1572872 | tf_op jit(solution)/shard_map/ppermute | solution.py:468
  13.7 18.5 %copy-start = (f32[64,2,63,8]{0,3,2,1:T(8,128)S(1)}, f32[64,2,63,8]{0,3,2,1:T(8,128)}, u32[]{:S(2)}) copy-start(f32[64,2,63,8]{0,3,2,1:T(8,128)} %param.8) | copy-start | bytes 774148
  13.7 39.7 %copy-start.1 = (f32[1024]{0:T(1024)S(1)}, f32[1024]{0:T(1024)}, u32[]{:S(2)}) copy-start(f32[1024]{0:T(1024)} %param.6) | copy-start | bytes 12292
  15.7 6.9 %collective-permute-start.1 = (f32[8,32,128]{2,1,0:T(8,128)S(1)}, f32[8,32,128]{2,1,0:T(8,128)S(1)}, u32[]{:S(2)}, u32[]{:S(2)}) collective-permute-start(f32[8,32,128]{2,1,0:T(8,128)S(1)} %get-tuple-element.22), channel_id=1, source_target_pairs={{0,8},{8,0},{16,24},{24,16},{1,9},{9,1},{17,25},{25,17},{2,10},{10... | collective-permute-start | bytes 393224 | tf_op jit(solution)/shard_map/ppermute | solution.py:468
  18.3 8.2 %collective-permute-start.3 = (f32[8,32,128]{2,1,0:T(8,128)S(1)}, f32[8,32,128]{2,1,0:T(8,128)S(1)}, u32[]{:S(2)}, u32[]{:S(2)}) collective-permute-start(f32[8,32,128]{2,1,0:T(8,128)S(1)} %get-tuple-element.23), channel_id=1, source_target_pairs={{0,24},{8,16},{16,8},{24,0},{1,25},{9,17},{17,9},{25,1},{2,26},{10... | collective-permute-start | bytes 393224 | tf_op jit(solution)/shard_map/ppermute | solution.py:468
  19.8 8.1 %collective-permute-start.2 = (f32[8,32,128]{2,1,0:T(8,128)S(1)}, f32[8,32,128]{2,1,0:T(8,128)S(1)}, u32[]{:S(2)}, u32[]{:S(2)}) collective-permute-start(f32[8,32,128]{2,1,0:T(8,128)S(1)} %get-tuple-element.24), channel_id=1, source_target_pairs={{0,16},{8,24},{16,0},{24,8},{1,17},{9,25},{17,1},{25,9},{2,18},{10... | collective-permute-start | bytes 393224 | tf_op jit(solution)/shard_map/ppermute | solution.py:468
  28.0 4.6 %collective-permute-start.4 = (f32[2,32,128]{2,1,0:T(8,128)S(1)}, f32[2,32,128]{2,1,0:T(8,128)S(1)}, u32[]{:S(2)}, u32[]{:S(2)}) collective-permute-start(f32[2,32,128]{2,1,0:T(8,128)S(1)} %get-tuple-element.25), channel_id=1, source_target_pairs={{0,2},{2,0},{4,6},{6,4},{1,3},{3,1},{5,7},{7,5},{8,10},{10,8},{12,... | collective-permute-start | bytes 98312 | tf_op jit(solution)/shard_map/ppermute | solution.py:468
  29.6 5.7 %collective-permute-start.6 = (f32[2,32,128]{2,1,0:T(8,128)S(1)}, f32[2,32,128]{2,1,0:T(8,128)S(1)}, u32[]{:S(2)}, u32[]{:S(2)}) collective-permute-start(f32[2,32,128]{2,1,0:T(8,128)S(1)} %get-tuple-element.26), channel_id=1, source_target_pairs={{0,6},{2,4},{4,2},{6,0},{1,7},{3,5},{5,3},{7,1},{8,14},{10,12},{12... | collective-permute-start | bytes 98312 | tf_op jit(solution)/shard_map/ppermute | solution.py:468
  32.1 5.2 %collective-permute-start.5 = (f32[2,32,128]{2,1,0:T(8,128)S(1)}, f32[2,32,128]{2,1,0:T(8,128)S(1)}, u32[]{:S(2)}, u32[]{:S(2)}) collective-permute-start(f32[2,32,128]{2,1,0:T(8,128)S(1)} %get-tuple-element.27), channel_id=1, source_target_pairs={{0,4},{2,6},{4,0},{6,2},{1,5},{3,7},{5,1},{7,3},{8,12},{10,14},{12... | collective-permute-start | bytes 98312 | tf_op jit(solution)/shard_map/ppermute | solution.py:468
  53.4 2.1 %collective-permute-start.7 = (bf16[16,32,128]{2,1,0:T(8,128)(2,1)S(1)}, bf16[16,32,128]{2,1,0:T(8,128)(2,1)S(1)}, u32[]{:S(2)}, u32[]{:S(2)}) collective-permute-start(bf16[16,32,128]{2,1,0:T(8,128)(2,1)S(1)} %all_to_all.5.pay_ref), channel_id=1, source_target_pairs={{0,1},{1,0},{2,3},{3,2},{4,5},{5,4},{6,7},{7,6},{8,9},{9,8},{10,11... | collective-permute-start | bytes 393224 | tf_op jit(solution)/shard_map/ppermute | solution.py:468
